TPU v7x, 32 devices: a whole 2x2x4 slice. The times are simulated.
32 devices in a mesh: item: 4 (over y, x), frame: 8 (over z, core).
Axes of the slice: x: 2, y: 2, z: 4, core: 2. Of those that a mesh axis runs over, the one named last changes fastest.
Arguments:
- tokens: bfloat16 [4, 16, 448, 1152], P('item', 'frame'), may hold values from -6 to 6
- cotangent: bfloat16 [4, 16, 448, 1152], P('item', 'frame'), may hold values from -6 to 6
- patch_counts: int32 [12], replicated, may hold values from 64 to 256, as said below
- assignment: int32 [12], replicated, may hold values from 0 to 3, as said below
- timesteps: int32 [12], replicated, may hold values from 0 to 999
- class_ids: int32 [12], replicated, may hold values from 0 to 100
- w_qkv: bfloat16 [1152, 3456], P('frame'), may hold values from -0.1875 to 0.1875
- w_out: bfloat16 [1152, 1152], P('frame'), may hold values from -0.75 to 0.75
- w_fc1: bfloat16 [1152, 4608], P('frame'), may hold values from -0.1875 to 0.1875
- b_fc1: bfloat16 [4608], P('frame'), may hold values from -3 to 3
- w_fc2: bfloat16 [4608, 1152], P('frame'), may hold values from -0.09375 to 0.09375
- w_ada: bfloat16 [1152, 6912], P(None, 'frame'), may hold values from -0.1875 to 0.1875
- b_ada: bfloat16 [6912], P('frame'), may hold values from -3 to 3
- class_table: float32 [101, 1152], replicated, may hold values from -6 to 6
Outputs:
- block_out: bfloat16 [4, 16, 448, 1152], P('item', 'frame')
- grad_tokens: bfloat16 [4, 16, 448, 1152], P('item', 'frame')
- grad_w_qkv: float32 [1152, 3456], P('frame')
- grad_w_out: float32 [1152, 1152], P('frame')
- grad_w_fc1: float32 [1152, 4608], P('frame')
- grad_b_fc1: float32 [4608], P('frame')
- grad_w_fc2: float32 [4608, 1152], P('frame')
- grad_w_ada: float32 [1152, 6912], P(None, 'frame')
- grad_b_ada: float32 [6912], P('frame')
- grad_class_table: float32 [101, 1152], replicated
Inputs may be any that keep to these rules, and one draw needn't show every extreme that they name: `patch_counts`: each clip holds 256 or 64 patches a frame. The clips of one group hold at most 448 patches a frame together, at most one of them with 256, and some group holds exactly 448. `assignment`: every group holds one to four clips.
All inputs are finite; a program needn't handle non-finite values.
Results may differ from a plain program's by a relative error of at most 0.02.
Values may be sent and summed in bfloat16 or wider, within the bound.
No kernel may reach another device: no remote copies, remote signals or barrier semaphores. Data moves between devices by JAX's collectives and lax.ppermute only.
A program may use at most 256 MiB of HBM per device.

v0:
```python
import math

import jax
import jax.numpy as jnp
from jax import lax
from jax.sharding import PartitionSpec as P

D = 1152
HEADS = 16
CLASSES = 101


HIGHEST = lax.Precision.HIGHEST
ROW_DIMS = (((0,), (0,)), ((), ()))
COL_DIMS = (((1,), (1,)), ((), ()))


def layer_norm(values):
    center = values - jnp.mean(values, axis=-1, keepdims=True)
    return center * lax.rsqrt(jnp.mean(center * center, axis=-1, keepdims=True) + 1e-06)


def time_features(timesteps):
    half_width = D // 2
    frequency = jnp.exp(-math.log(10000.0) * jnp.arange(half_width, dtype=jnp.float32) / half_width)
    angles = timesteps.astype(jnp.float32)[:, None] * frequency[None, :]
    return jnp.concatenate([jnp.cos(angles), jnp.sin(angles)], axis=1)


def row_items(patch_counts, assignment, group_idx, total):
    numbers = jnp.arange(patch_counts.shape[0], dtype=jnp.int32)
    same_group = assignment[None, :] == assignment[:, None]
    earlier = numbers[None, :] < numbers[:, None]
    offsets = jnp.sum(jnp.where(same_group & earlier, patch_counts[None, :], 0), axis=1)
    row_ids = jnp.arange(total, dtype=jnp.int32)[:, None]
    inside = (
        (assignment[None, :] == group_idx)
        & (row_ids >= offsets[None, :])
        & (row_ids < offsets[None, :] + patch_counts[None, :])
    )
    return inside.astype(jnp.float32)


def gelu_tanh(pre_vals):
    return jax.nn.gelu(pre_vals, approximate=True)


def body(
    tokens,
    cotangent,
    patch_counts,
    assignment,
    timesteps,
    class_ids,
    w_qkv,
    w_out,
    w_fc1,
    b_fc1,
    w_fc2,
    w_ada,
    b_ada,
    class_table,
):
    frame_count = lax.axis_size("frame")
    group_idx = lax.axis_index("item")
    frame_pos = lax.axis_index("frame")
    capacity = tokens.shape[2]
    model_width = tokens.shape[3]
    positions = capacity // frame_count
    head_dim = model_width // HEADS
    attn_scale = 1.0 / math.sqrt(head_dim)
    layout = row_items(patch_counts, assignment, group_idx, capacity)
    my_rows = lax.dynamic_slice_in_dim(layout, frame_pos * positions, positions, 0)
    valid_rows = jnp.sum(my_rows, axis=1)
    class_hot = (class_ids[:, None] == jnp.arange(CLASSES, dtype=jnp.int32)[None, :]).astype(
        jnp.float32
    )
    condition = time_features(timesteps) + jnp.dot(class_hot, class_table, precision=HIGHEST)
    activated = jax.nn.silu(condition)
    ada_part = jnp.dot(activated, w_ada.astype(jnp.float32), precision=HIGHEST) + b_ada.astype(
        jnp.float32
    )
    ada_cols = ada_part.T.astype(jnp.bfloat16)

    def fetch_weights():
        return (
            lax.all_gather(w_qkv, "frame", axis=0, tiled=True),
            lax.all_gather(w_out, "frame", axis=0, tiled=True),
            lax.all_gather(w_fc1, "frame", axis=0, tiled=True),
            lax.all_gather(w_fc2, "frame", axis=0, tiled=True),
            lax.all_gather(b_fc1, "frame", axis=0, tiled=True),
            lax.all_gather(ada_cols, "frame", axis=0, tiled=True),
        )

    def run_forward(arrived, weights):
        full_qkv, full_out, full_fc1, full_fc2, full_bias, full_ada = weights
        row_mod = lax.dot_general(
            my_rows.astype(jnp.bfloat16), full_ada, COL_DIMS, preferred_element_type=jnp.float32
        )
        shift_attn, scale_attn, gate_attn, shift_mlp, scale_mlp, gate_mlp = jnp.split(
            row_mod, 6, axis=1
        )
        inputs = arrived[0].astype(jnp.float32)
        frames = inputs.shape[0]
        row_total = frames * positions
        first_in = (layer_norm(inputs) * (1.0 + scale_attn) + shift_attn).astype(jnp.bfloat16)
        projected = jnp.dot(
            first_in.reshape(row_total, model_width), full_qkv, preferred_element_type=jnp.float32
        )
        projected = projected.astype(jnp.bfloat16).reshape(frames, positions, 3, HEADS, head_dim)
        queries = projected[:, :, 0]
        key_rows = projected[:, :, 1]
        value_rows = projected[:, :, 2]
        scores = (
            jnp.einsum("iphd,jphd->phij", queries, key_rows, preferred_element_type=jnp.float32)
            * attn_scale
        )
        attn_prob = jax.nn.softmax(scores, axis=-1)
        prob_low = attn_prob.astype(jnp.bfloat16)
        mixed_heads = jnp.einsum(
            "phij,jphd->iphd", prob_low, value_rows, preferred_element_type=jnp.float32
        )
        mixed_heads = mixed_heads.astype(jnp.bfloat16).reshape(row_total, model_width)
        attn_out = jnp.dot(mixed_heads, full_out, preferred_element_type=jnp.float32).reshape(
            frames, positions, model_width
        )
        middle = inputs + gate_attn * attn_out
        second_in = (
            (layer_norm(middle) * (1.0 + scale_mlp) + shift_mlp)
            .astype(jnp.bfloat16)
            .reshape(row_total, model_width)
        )
        pre_act = jnp.dot(
            second_in, full_fc1, preferred_element_type=jnp.float32
        ) + full_bias.astype(jnp.float32)
        post_act = gelu_tanh(pre_act).astype(jnp.bfloat16)
        mlp_out = jnp.dot(post_act, full_fc2, preferred_element_type=jnp.float32).reshape(
            frames, positions, model_width
        )
        result = valid_rows[None, :, None] * (middle + gate_mlp * mlp_out)
        saved_fwd = (
            inputs,
            row_mod,
            first_in,
            queries,
            key_rows,
            value_rows,
            attn_prob,
            prob_low,
            mixed_heads,
            attn_out,
            middle,
            second_in,
            pre_act,
            post_act,
            mlp_out,
        )
        return (result, saved_fwd)

    weights = fetch_weights()
    arrived = lax.all_to_all(tokens, "frame", split_axis=2, concat_axis=1, tiled=True)
    result, saved_fwd = run_forward(arrived, weights)
    block_out = lax.all_to_all(
        result.astype(jnp.bfloat16)[None], "frame", split_axis=1, concat_axis=2, tiled=True
    )
    weights_again = fetch_weights()
    arrived_again, cot_arrived = (
        lax.all_to_all(tokens, "frame", split_axis=2, concat_axis=1, tiled=True),
        lax.all_to_all(cotangent, "frame", split_axis=2, concat_axis=1, tiled=True),
    )
    _, saved_again = run_forward(arrived_again, weights_again)
    full_qkv, full_out, full_fc1, full_fc2, full_bias, full_ada = weights_again
    (
        inputs,
        row_mod,
        first_in,
        queries,
        key_rows,
        value_rows,
        attn_prob,
        prob_low,
        mixed_heads,
        attn_out,
        middle,
        second_in,
        pre_act,
        post_act,
        mlp_out,
    ) = saved_again
    shift_attn, scale_attn, gate_attn, shift_mlp, scale_mlp, gate_mlp = jnp.split(
        row_mod, 6, axis=1
    )
    frames = inputs.shape[0]
    row_total = frames * positions
    grad_rows = cot_arrived[0].astype(jnp.float32) * valid_rows[None, :, None]
    grad_gate_mlp = jnp.sum(grad_rows * mlp_out, axis=0)
    grad_mlp = (grad_rows * gate_mlp).astype(jnp.bfloat16).reshape(row_total, model_width)
    grad_post = lax.dot_general(grad_mlp, full_fc2, COL_DIMS, preferred_element_type=jnp.float32)
    part_fc2 = lax.dot_general(post_act, grad_mlp, ROW_DIMS, preferred_element_type=jnp.float32)
    _, gelu_back = jax.vjp(gelu_tanh, pre_act)
    grad_pre = gelu_back(grad_post)[0].astype(jnp.bfloat16)
    part_bias = jnp.sum(grad_pre.astype(jnp.float32), axis=0)
    part_fc1 = lax.dot_general(second_in, grad_pre, ROW_DIMS, preferred_element_type=jnp.float32)
    grad_second = lax.dot_general(grad_pre, full_fc1, COL_DIMS, preferred_element_type=jnp.float32)
    grad_second = grad_second.reshape(frames, positions, model_width)
    normed_mid, middle_back = jax.vjp(layer_norm, middle)
    grad_shift_mlp = jnp.sum(grad_second, axis=0)
    grad_scale_mlp = jnp.sum(grad_second * normed_mid, axis=0)
    grad_middle = grad_rows + middle_back(grad_second * (1.0 + scale_mlp))[0]
    grad_gate_attn = jnp.sum(grad_middle * attn_out, axis=0)
    grad_attn = (grad_middle * gate_attn).astype(jnp.bfloat16).reshape(row_total, model_width)
    part_out = lax.dot_general(mixed_heads, grad_attn, ROW_DIMS, preferred_element_type=jnp.float32)
    grad_mixed = lax.dot_general(grad_attn, full_out, COL_DIMS, preferred_element_type=jnp.float32)
    grad_mixed = grad_mixed.astype(jnp.bfloat16).reshape(frames, positions, HEADS, head_dim)
    grad_prob = jnp.einsum(
        "iphd,jphd->phij", grad_mixed, value_rows, preferred_element_type=jnp.float32
    )
    grad_value = jnp.einsum(
        "phij,iphd->jphd", prob_low, grad_mixed, preferred_element_type=jnp.float32
    )
    grad_scores = attn_prob * (grad_prob - jnp.sum(attn_prob * grad_prob, axis=-1, keepdims=True))
    grad_scores = grad_scores.astype(jnp.bfloat16)
    grad_query = (
        jnp.einsum("phij,jphd->iphd", grad_scores, key_rows, preferred_element_type=jnp.float32)
        * attn_scale
    )
    grad_key = (
        jnp.einsum("phij,iphd->jphd", grad_scores, queries, preferred_element_type=jnp.float32)
        * attn_scale
    )
    grad_proj = (
        jnp.stack([grad_query, grad_key, grad_value], axis=2)
        .astype(jnp.bfloat16)
        .reshape(row_total, 3 * model_width)
    )
    part_qkv = lax.dot_general(
        first_in.reshape(row_total, model_width),
        grad_proj,
        ROW_DIMS,
        preferred_element_type=jnp.float32,
    )
    grad_first = lax.dot_general(grad_proj, full_qkv, COL_DIMS, preferred_element_type=jnp.float32)
    grad_first = grad_first.reshape(frames, positions, model_width)
    normed_in, inputs_back = jax.vjp(layer_norm, inputs)
    grad_shift_attn = jnp.sum(grad_first, axis=0)
    grad_scale_attn = jnp.sum(grad_first * normed_in, axis=0)
    grad_inputs = grad_middle + inputs_back(grad_first * (1.0 + scale_attn))[0]
    grad_mod = jnp.concatenate(
        [
            grad_shift_attn,
            grad_scale_attn,
            grad_gate_attn,
            grad_shift_mlp,
            grad_scale_mlp,
            grad_gate_mlp,
        ],
        axis=1,
    )
    part_mod = lax.dot_general(grad_mod, my_rows, ROW_DIMS, precision=HIGHEST)
    grad_inputs, partials = (
        grad_inputs,
        (part_qkv, part_out, part_fc1, part_fc2, part_bias, part_mod),
    )
    grad_tokens = lax.all_to_all(
        grad_inputs.astype(jnp.bfloat16)[None], "frame", split_axis=1, concat_axis=2, tiled=True
    )
    shares = (
        lax.psum_scatter(
            partials[0].astype(jnp.bfloat16), "frame", scatter_dimension=0, tiled=True
        ).astype(jnp.float32),
        lax.psum_scatter(
            partials[1].astype(jnp.bfloat16), "frame", scatter_dimension=0, tiled=True
        ).astype(jnp.float32),
        lax.psum_scatter(
            partials[2].astype(jnp.bfloat16), "frame", scatter_dimension=0, tiled=True
        ).astype(jnp.float32),
        lax.psum_scatter(
            partials[3].astype(jnp.bfloat16), "frame", scatter_dimension=0, tiled=True
        ).astype(jnp.float32),
        lax.psum_scatter(
            partials[4].astype(jnp.bfloat16), "frame", scatter_dimension=0, tiled=True
        ).astype(jnp.float32),
        lax.psum_scatter(
            partials[5].astype(jnp.bfloat16), "frame", scatter_dimension=0, tiled=True
        ).astype(jnp.float32),
    )
    totals = (
        lax.psum(shares[0].astype(jnp.bfloat16), "item").astype(jnp.float32),
        lax.psum(shares[1].astype(jnp.bfloat16), "item").astype(jnp.float32),
        lax.psum(shares[2].astype(jnp.bfloat16), "item").astype(jnp.float32),
        lax.psum(shares[3].astype(jnp.bfloat16), "item").astype(jnp.float32),
        lax.psum(shares[4].astype(jnp.bfloat16), "item").astype(jnp.float32),
        lax.psum(shares[5].astype(jnp.bfloat16), "item").astype(jnp.float32),
    )
    sum_qkv, sum_out, sum_fc1, sum_fc2, sum_bias, grad_modulation = totals
    grad_w_ada = lax.dot_general(
        activated, grad_modulation, (((0,), (1,)), ((), ())), precision=HIGHEST
    )
    grad_b_ada = jnp.sum(grad_modulation, axis=1)
    act_part = lax.dot_general(
        w_ada.astype(jnp.float32), grad_modulation, (((1,), (0,)), ((), ())), precision=HIGHEST
    )
    grad_activated = lax.psum(act_part.astype(jnp.bfloat16), "frame").astype(jnp.float32)
    _, silu_back = jax.vjp(jax.nn.silu, condition)
    grad_condition = silu_back(grad_activated.T)[0]
    grad_table = lax.dot_general(class_hot, grad_condition, ROW_DIMS, precision=HIGHEST)
    return (
        block_out,
        grad_tokens,
        sum_qkv,
        sum_out,
        sum_fc1,
        sum_bias,
        sum_fc2,
        grad_w_ada,
        grad_b_ada,
        grad_table,
    )


def solution(mesh):
    return jax.shard_map(
        body,
        mesh=mesh,
        in_specs=(
            P("item", "frame", None, None),
            P("item", "frame", None, None),
            P(),
            P(),
            P(),
            P(),
            P("frame", None),
            P("frame", None),
            P("frame", None),
            P("frame"),
            P("frame", None),
            P(None, "frame"),
            P("frame"),
            P(),
        ),
        out_specs=(
            P("item", "frame", None, None),
            P("item", "frame", None, None),
            P("frame", None),
            P("frame", None),
            P("frame", None),
            P("frame"),
            P("frame", None),
            P(None, "frame"),
            P("frame"),
            P(),
        ),
        check_vma=False,
    )
```

profile of v0, /device:TPU:0, one launch (start us, length us, event | category | flops | bytes accessed | tf_op | source)
XLA Modules:
  0.0 1145.9 jit_solution(8078238238587266525)
XLA Ops:
  26.8 96.7 %all-to-all-done = bf16[1,2,448,1152]{3,1,0,2:T(2,128)(2,1)} async-done(((bf16[1,2,448,1152]{3,1,0,2:T(2,128)(2,1)}), bf16[1,2,448,1152]{3,1,0,2:T(2,128)(2,1)}, u32[]{:S(2)}, u32[]{:S(2)}) %all-to-all-start) | async-done | bytes 2064416 | tf_op jit(solution)/shard_map/all_to_all | solution.py:161
  130.0 83.5 %all-reduce = bf16[4608]{0:T(1024)(128)(2,1)S(1)} all-reduce(bf16[4608]{0:T(1024)(128)(2,1)S(1)} %dynamic-update-slice), channel_id=1, replica_groups=mesh['item'=4,'frame'=8] {'frame'}, use_global_device_ids=true, to_apply=%add | all-reduce | flops 4608 | bytes 18432
  216.4 15.5 %all-gather = bf16[8,864,12]{1,2,0:T(8,128)(2,1)S(1)} all-gather(bf16[1,864,12]{1,2,0:T(8,128)(2,1)S(1)} %fusion.40), channel_id=1, replica_groups=mesh['item'=4,'frame'=8] {'frame'}, dimensions={0}, use_global_device_ids=true | all-gather | bytes 186624 | tf_op jit(solution)/shard_map/all_gather | solution.py:92
  257.2 14.2 %convolution_convert_fusion.5 = bf16[896,3456]{1,0:T(8,128)(2,1)} fusion(bf16[896,1152]{1,0:T(8,128)(2,1)} %fusion.18, bf16[1152,3456]{1,0:T(8,128)(2,1)} %all-gather.6.cloned.1.call-done), kind=kOutput, calls=%fused_computation.24 | convolution fusion | flops 7137607680 | bytes 16220160 | tf_op jit(solution)/shard_map/dot_general | solution.py:107
  271.4 21.0 %reshape.259 = bf16[16,56,3,16,72]{4,3,2,1,0:T(8,128)(2,1)} reshape(bf16[896,3456]{1,0:T(8,128)(2,1)} %convolution_convert_fusion.5) | data formatting | bytes 12386304 | tf_op jit(solution)/shard_map/reshape | solution.py:110
  305.5 28.5 %fusion.74 = (f32[56,16,16]{2,1,0:T(8,128)S(1)}, f32[56,16,16,16]{2,3,1,0:T(8,128)S(1)}) fusion(f32[56,16,16,16]{2,3,1,0:T(8,128)S(1)} %fusion.25), kind=kOutput, calls=%fused_computation.143 | output fusion | flops 917519 | bytes 1892352 | tf_op jit(solution)/shard_map/sub | solution.py:118
  375.7 21.4 %multiply_convert_fusion = (bf16[896,4608]{1,0:T(8,128)(2,1)}, f32[896,4608]{1,0:T(8,128)}) fusion(f32[4608]{0:T(1024)S(1)} %convert_element_type.231, bf16[896,1152]{1,0:T(8,128)(2,1)} %bitcast.171, bf16[1152,4608]{1,0:T(8,128)(2,1)} %all-gather.10.cloned.1.call-done), kind=kOutput, calls=%fused_computation.13 | convolution fusion | flops 9553969152 | bytes 37472256 | tf_op jit(solution)/shard_map/dot_general | solution.py:133
  402.2 27.2 %fusion.69 = (bf16[4608]{0:T(1024)(128)(2,1)}, bf16[896,4608]{1,0:T(8,128)(2,1)}) fusion(f32[896,4608]{1,0:T(8,128)} %get-tuple-element.51, f32[4608]{0:T(1024)S(1)} %convert_element_type.231, bf16[896,1152]{1,0:T(8,128)(2,1)} %fusion.14, bf16[4608,1152]{1,0:T(8,128)(2,1)} %all-gather.12.cloned.1.call-done), kind=kOutput, calls=%fused_computation.139 | convolution fusion | flops 9603510272 | bytes 37481472 | tf_op jit(solution)/shard_map/dot_general | solution.py:198
  429.4 14.3 %fusion.76 = f32[896,1152]{1,0:T(8,128)S(1)} fusion(bf16[896,4608]{1,0:T(8,128)(2,1)} %get-tuple-element.25, bf16[1152,4608]{1,0:T(8,128)(2,1)} %all-gather.10.cloned.1.call-done), kind=kOutput, calls=%fused_computation.145 | convolution fusion | flops 9512681472 | bytes 23003136 | tf_op jit(solution)/shard_map/dot_general | solution.py:204
  447.5 16.0 %fusion.75 = f32[896,1152]{1,0:T(8,128)} fusion(bf16[896,4608]{1,0:T(8,128)(2,1)S(1)} %bitcast.183, bf16[4608,1152]{1,0:T(8,128)(2,1)} %all-gather.12.cloned.1.call-done), kind=kOutput, calls=%fused_computation.144 | convolution fusion | flops 9512681472 | bytes 23003136 | tf_op jit(solution)/shard_map/dot_general | solution.py:137
  495.0 12.4 %multiply_reduce_fusion = (f32[56,16,16]{2,1,0:T(8,128)S(1)}, f32[56,16,16,16]{2,3,1,0:T(8,128)}) fusion(f32[56,16,16,16]{2,3,1,0:T(8,128)} %copy-done.12, f32[56,16,16]{2,1,0:T(8,128)S(1)} %copy-done.26, bf16[16,56,1,16,72]{4,3,2,1,0:T(8,128)(2,1)} %get-tuple-element.28, bf16[16,56,16,72]{3,2,1,0:T(8,128)(2,1)S(1)} %copy-done.18), kind=kOutput, calls=%fused_computation.22 | convolution fusion | flops 33703936 | bytes 6078464 | tf_op jit(solution)/shard_map/iphd,jphd->phij/dot_general | solution.py:215
  530.9 17.5 %convert_element_type.250 = bf16[896,3456]{1,0:T(8,128)(2,1)} reshape(bf16[16,56,3,16,72]{4,3,2,1,0:T(8,128)(2,1)} %copy.86) | data formatting | bytes 12386304 | tf_op jit(solution)/shard_map/convert_element_type | solution.py:233
  548.3 17.5 %convert_element_type.246 = bf16[16,56,3456]{2,1,0:T(8,128)(2,1)} reshape(bf16[16,56,3,16,72]{4,3,2,1,0:T(8,128)(2,1)} %copy.86) | data formatting | bytes 12386304 | tf_op jit(solution)/shard_map/convert_element_type | solution.py:233
  572.9 14.9 %multiply_reduce_fusion.6 = (f32[16,56]{1,0:T(8,128)S(1)}, f32[16,56,1152]{2,1,0:T(8,128)S(1)}) fusion(f32[16,56,1152]{2,1,0:T(8,128)} %bitcast.165, f32[16,56]{1,0:T(8,128)S(1)} %bitcast.178, f32[56,1152]{1,0:T(8,128)S(1)} %copy-done.17, bf16[16,56,3456]{2,1,0:T(8,128)(2,1)} %convert_element_type.246, bf16[1152,3456]{1,0:T(8,128)(2,1)} %all-gather.6.cloned.1.call-done), kind=kOutput, calls=%fused_computation.48 | convolution fusion | flops 7138638848 | bytes 22678528 | tf_op jit(solution)/shard_map/dot_general | solution.py:242
  591.7 13.5 %convolution_convert_fusion.2 = bf16[1152,3456]{1,0:T(8,128)(2,1)} fusion(bf16[896,1152]{1,0:T(8,128)(2,1)S(1)} %bitcast.173, bf16[896,3456]{1,0:T(8,128)(2,1)} %convert_element_type.250), kind=kOutput, calls=%fused_computation.14 | convolution fusion | flops 7138492416 | bytes 16220160 | tf_op jit(solution)/shard_map/dot_general | solution.py:236
  605.2 17.9 %convolution_convert_fusion = bf16[4608,1152]{1,0:T(8,128)(2,1)} fusion(bf16[896,4608]{1,0:T(8,128)(2,1)} %get-tuple-element.50, bf16[896,1152]{1,0:T(8,128)(2,1)} %fusion.14), kind=kOutput, calls=%fused_computation.4 | convolution fusion | flops 9517989888 | bytes 20938752 | tf_op jit(solution)/shard_map/dot_general | solution.py:199
  623.1 16.8 %convolution_convert_fusion.1 = bf16[1152,4608]{1,0:T(8,128)(2,1)} fusion(bf16[896,1152]{1,0:T(8,128)(2,1)} %bitcast.172, bf16[896,4608]{1,0:T(8,128)(2,1)} %get-tuple-element.25), kind=kOutput, calls=%fused_computation.5 | convolution fusion | flops 9517989888 | bytes 20938752 | tf_op jit(solution)/shard_map/dot_general | solution.py:203
  649.7 78.8 %reduce-scatter.8.cloned.1.call-done = bf16[144,3456]{1,0:T(8,128)(2,1)} async-done(((bf16[1152,3456]{1,0:T(8,128)(2,1)}), bf16[144,3456]{1,0:T(8,128)(2,1)}) %reduce-scatter.8.cloned.1.call-update) | async-done | bytes 995344 | tf_op jit(solution)/shard_map/reduce_scatter | solution.py:268
  728.4 122.6 %reduce-scatter.14.cloned.1.call-done = bf16[576,1152]{1,0:T(8,128)(2,1)} async-done(((bf16[4608,1152]{1,0:T(8,128)(2,1)}), bf16[576,1152]{1,0:T(8,128)(2,1)}) %reduce-scatter.14.cloned.1.call-update) | async-done | bytes 1327120 | tf_op jit(solution)/shard_map/reduce_scatter | solution.py:277
  851.0 111.3 %reduce-scatter.12.cloned.1.call-done = bf16[144,4608]{1,0:T(8,128)(2,1)} async-done(((bf16[1152,4608]{1,0:T(8,128)(2,1)}), bf16[144,4608]{1,0:T(8,128)(2,1)}) %reduce-scatter.12.cloned.1.call-update) | async-done | bytes 1327120 | tf_op jit(solution)/shard_map/reduce_scatter | solution.py:274
  973.9 39.7 %reduce-scatter.16.cloned.1.call-done = bf16[864,12]{1,0:T(8,128)(2,1)} async-done(((bf16[6912,12]{1,0:T(8,128)(2,1)}), bf16[864,12]{1,0:T(8,128)(2,1)}) %reduce-scatter.16.cloned.1.call-update) | async-done | bytes 20752
  1014.7 16.2 %psum.54 = bf16[864,12]{0,1:T(8,128)(2,1)S(1)} all-reduce(bf16[864,12]{0,1:T(8,128)(2,1)S(1)} %copy.94), channel_id=1, replica_groups=mesh['item'=4,'frame'=8] {'item'}, use_global_device_ids=true, to_apply=%region_31.32 | all-reduce | flops 10368 | bytes 41472 | tf_op jit(solution)/shard_map/psum | solution.py:293
  1031.3 33.6 %all-reduce.2 = (bf16[4608]{0:T(1024)(128)(2,1)S(1)}, bf16[12,1152]{1,0:T(8,128)(2,1)S(1)}) all-reduce(bf16[4608]{0:T(1024)(128)(2,1)S(1)} %copy-done.42, bf16[12,1152]{1,0:T(8,128)(2,1)S(1)} %convolution_convert_fusion.7), channel_id=5, replica_groups=mesh['item'=4,'frame'=8] {'frame'}, use_global_device_ids=true, to_apply=%region_20.21.clone | all-reduce | flops 18432 | bytes 73728
  1085.4 45.3 %all-reduce.6.cloned.1.call-done = (bf16[144,3456]{1,0:T(8,128)(2,1)}, bf16[144,1152]{1,0:T(8,128)(2,1)}, bf16[144,4608]{1,0:T(8,128)(2,1)}, bf16[576,1152]{1,0:T(8,128)(2,1)}) async-done(((bf16[144,3456]{1,0:T(8,128)(2,1)}, bf16[144,1152]{1,0:T(8,128)(2,1)}, bf16[144,4608]{1,0:T(8,128)(2,1)}, bf16[576,1152]{1,0:T(8,128)(2,1)}), (bf16[144,3456]{1,0:T(8,128)(2,1)}, bf16[144,1152]{1,0:T(8,128)(2,1)}, ...) | async-done | bytes 3981328 | tf_op jit(solution)/shard_map/psum | solution.py:288
  (232 shorter events, 233.2 us)
Async XLA Ops:
  7.2 207.5 %copy-start = (bf16[1152,864]{0,1:T(8,128)(2,1)S(1)}, bf16[1152,864]{0,1:T(8,128)(2,1)}, u32[]{:S(2)}) copy-start(bf16[1152,864]{0,1:T(8,128)(2,1)} %param.25) | copy-start | bytes 5971972
  7.2 250.0 %all-gather.6.cloned.1.call-start = ((), (), s32[]{:S(2)}) async-start(), calls=%async_computation.9 | async-start | bytes 8957952 | tf_op jit(solution)/shard_map/all_gather | solution.py:87
  7.9 349.3 %all-gather.8.cloned.1.call-start = ((), (), s32[]{:S(2)}) async-start(), calls=%async_computation.10 | async-start | bytes 2985984 | tf_op jit(solution)/shard_map/all_gather | solution.py:88
  8.7 367.0 %all-gather.10.cloned.1.call-start = ((), (), s32[]{:S(2)}) async-start(), calls=%async_computation.11 | async-start | bytes 11943936 | tf_op jit(solution)/shard_map/all_gather | solution.py:89
  9.4 392.8 %all-gather.12.cloned.1.call-start = ((), (), s32[]{:S(2)}) async-start(), calls=%async_computation.12 | async-start | bytes 11943936 | tf_op jit(solution)/shard_map/all_gather | solution.py:90
  15.0 108.5 %all-to-all-start = ((bf16[1,2,448,1152]{3,1,0,2:T(2,128)(2,1)}), bf16[1,2,448,1152]{3,1,0,2:T(2,128)(2,1)}, u32[]{:S(2)}, u32[]{:S(2)}) async-start(bf16[1,2,448,1152]{3,1,0,2:T(2,128)(2,1)} %copy.71), calls=%async_computation | async-start | bytes 4128768 | tf_op jit(solution)/shard_map/all_to_all | solution.py:161
  21.3 106.6 %copy-start.48 = (s32[12]{0:T(128)S(1)}, s32[12]{0:T(128)}, u32[]{:S(2)}) copy-start(s32[12]{0:T(128)} %param.17) | copy-start | bytes 148
  21.3 106.6 %copy-start.51 = (s32[12]{0:T(128)S(1)}, s32[12]{0:T(128)}, u32[]{:S(2)}) copy-start(s32[12]{0:T(128)} %param.16) | copy-start | bytes 148
  21.3 106.8 %copy-start.53 = (s32[12]{0:T(128)S(1)}, s32[12]{0:T(128)}, u32[]{:S(2)}) copy-start(s32[12]{0:T(128)} %param.18) | copy-start | bytes 148
  21.3 106.8 %copy-start.45 = (bf16[864]{0:T(1024)(128)(2,1)S(1)}, bf16[864]{0:T(1024)(128)(2,1)}, u32[]{:S(2)}) copy-start(bf16[864]{0:T(1024)(128)(2,1)} %param.26) | copy-start | bytes 5188
  21.4 107.1 %copy-start.46 = (u32[32]{0:T(128)S(1)}, u32[32]{0:T(128)}, u32[]{:S(2)}) copy-start(u32[32]{0:T(128)} %constant.64) | copy-start | bytes 388
  21.4 108.4 %copy-start.47 = (bf16[576]{0:T(1024)(128)(2,1)S(1)}, bf16[576]{0:T(1024)(128)(2,1)}, u32[]{:S(2)}) copy-start(bf16[576]{0:T(1024)(128)(2,1)} %param.23) | copy-start | bytes 3460
  21.4 192.4 %copy-start.35 = (f32[101,1152]{1,0:T(8,128)S(1)}, f32[101,1152]{1,0:T(8,128)}, u32[]{:S(2)}) copy-start(f32[101,1152]{1,0:T(8,128)} %param.27) | copy-start | bytes 1396228
  21.4 192.4 %copy-start.49 = (s32[12]{0:T(128)S(1)}, s32[12]{0:T(128)}, u32[]{:S(2)}) copy-start(s32[12]{0:T(128)} %param.19) | copy-start | bytes 148
  123.5 119.1 %all-to-all-start.2 = ((bf16[1,2,448,1152]{3,1,0,2:T(2,128)(2,1)}), bf16[1,2,448,1152]{3,1,0,2:T(2,128)(2,1)}, u32[]{:S(2)}, u32[]{:S(2)}) async-start(bf16[1,2,448,1152]{3,1,0,2:T(2,128)(2,1)} %copy.81), calls=%async_computation.2 | async-start | bytes 4128768 | tf_op jit(solution)/shard_map/all_to_all | solution.py:169
  127.8 521.8 %reduce-scatter.10.cloned.1.call-start = ((), (), s32[]{:S(2)}) async-start(), calls=%async_computation.14 | async-start | bytes 2985984 | tf_op jit(solution)/shard_map/reduce_scatter | solution.py:271
  572.8 155.7 %reduce-scatter.8.cloned.1.call-start = ((), (), s32[]{:S(2)}) async-start(), calls=%async_computation.13 | async-start | bytes 8957952 | tf_op jit(solution)/shard_map/reduce_scatter | solution.py:268
  605.1 245.9 %reduce-scatter.14.cloned.1.call-start = ((), (), s32[]{:S(2)}) async-start(), calls=%async_computation.16 | async-start | bytes 11943936 | tf_op jit(solution)/shard_map/reduce_scatter | solution.py:277
  623.1 339.3 %reduce-scatter.12.cloned.1.call-start = ((), (), s32[]{:S(2)}) async-start(), calls=%async_computation.15 | async-start | bytes 11943936 | tf_op jit(solution)/shard_map/reduce_scatter | solution.py:274
  639.9 328.8 %all-to-all-start.1 = ((bf16[1,16,56,1152]{3,2,0,1:T(8,128)(2,1)}), bf16[1,16,56,1152]{3,2,0,1:T(8,128)(2,1)}, u32[]{:S(2)}, u32[]{:S(2)}) async-start(bf16[1,16,56,1152]{3,2,0,1:T(8,128)(2,1)} %get-tuple-element.31), calls=%async_computation.1 | async-start | bytes 4128768 | tf_op jit(solution)/shard_map/all_to_all | solution.py:163
  644.5 369.2 %reduce-scatter.16.cloned.1.call-start = ((), (), s32[]{:S(2)}) async-start(), calls=%async_computation.17 | async-start | bytes 1990656
  647.2 315.2 %copy-start.39 = (f32[16,56]{1,0:T(8,128)S(1)}, f32[16,56]{1,0:T(8,128)}, u32[]{:S(2)}) copy-start(f32[16,56]{1,0:T(8,128)} %copy-done.38) | copy-start | bytes 10756
  648.9 481.8 %all-reduce.6.cloned.1.call-start = ((), (), s32[]{:S(2)}) async-start(), calls=%async_computation.18 | async-start | bytes 7962624 | tf_op jit(solution)/shard_map/psum | solution.py:288
  968.8 113.6 %all-to-all-start.3 = ((bf16[1,16,56,1152]{3,2,0,1:T(8,128)(2,1)}), bf16[1,16,56,1152]{3,2,0,1:T(8,128)(2,1)}, u32[]{:S(2)}, u32[]{:S(2)}) async-start(bf16[1,16,56,1152]{3,2,0,1:T(8,128)(2,1)} %fusion.36), calls=%async_computation.3 | async-start | bytes 4128768 | tf_op jit(solution)/shard_map/all_to_all | solution.py:264
  (46 other events, 709.3 us)
Sparse Core Ops, SparseCore 0:
  9.7 128.2 all-gather.5
  139.6 60.0 all-gather.7
  201.3 100.4 all-gather.9
  303.3 98.8 all-gather.11
  572.9 36.0 reduce-scatter.9
  611.1 117.2 reduce-scatter.7
  730.9 120.1 reduce-scatter.13
  853.3 108.9 reduce-scatter.11
  965.3 48.2 reduce-scatter.15
  1017.8 112.8 all-reduce.5
where the time goes:
time: 1150 us
  waiting for transfers between devices  502 us (44%)
  matrix products  225 us (20%)
  blocking collectives  157 us (14%)
  local copies, waits for them, and re-layouts  133 us (12%)
  other arithmetic  92.5 us (8%)
  starting transfers between devices  20.3 us (2%)
  between operations  16.6 us (1%)
    reduce_scatter x1, waiting for transfers between devices, body(): lax.psum_scatter(partials[3].astype(jnp.bfloat16), 'frame', scatter_dimen...  123 us
    unnamed x2, blocking collectives  117 us
    reduce_scatter x1, waiting for transfers between devices, body(): lax.psum_scatter(partials[2].astype(jnp.bfloat16), 'frame', scatter_dimen...  111 us
    all_to_all x1, waiting for transfers between devices, body(): lax.all_to_all(tokens, 'frame', split_axis=2, concat_axis=1, tiled=True)  96.7 us
    reduce_scatter x1, waiting for transfers between devices, body(): lax.psum_scatter(partials[0].astype(jnp.bfloat16), 'frame', scatter_dimen...  78.8 us
    psum x1, waiting for transfers between devices, body(): lax.psum(shares[0].astype(jnp.bfloat16), 'item').astype(jnp.float32)  45.3 us
    convert_element_type x3, local copies, waits for them, and re-layouts, body(): grad_proj = jnp.stack([grad_query, grad_key, grad_value], axis=2).astype(...  42.9 us
    unnamed x11, waiting for transfers between devices  42.4 us
  transfers between devices with their start and end apart: 14, of which 7 were waited for; matrix products, arithmetic and copies ran while one was open for 23% of the time, Pallas kernels for 0%

commit v1 on v0

v1 whole, which is shorter than its diff:
```python
import math

import jax
import jax.numpy as jnp
from jax import lax
from jax.experimental import pallas as pl
from jax.experimental.pallas import tpu as pltpu
from jax.sharding import PartitionSpec as P

D = 1152
HEADS = 16
CLASSES = 101


HIGHEST = lax.Precision.HIGHEST
ROW_DIMS = (((0,), (0,)), ((), ()))
COL_DIMS = (((1,), (1,)), ((), ()))


def layer_norm(values):
    center = values - jnp.mean(values, axis=-1, keepdims=True)
    return center * lax.rsqrt(jnp.mean(center * center, axis=-1, keepdims=True) + 1e-06)


def time_features(timesteps):
    half_width = D // 2
    frequency = jnp.exp(-math.log(10000.0) * jnp.arange(half_width, dtype=jnp.float32) / half_width)
    angles = timesteps.astype(jnp.float32)[:, None] * frequency[None, :]
    return jnp.concatenate([jnp.cos(angles), jnp.sin(angles)], axis=1)


def row_items(patch_counts, assignment, group_idx, total):
    numbers = jnp.arange(patch_counts.shape[0], dtype=jnp.int32)
    same_group = assignment[None, :] == assignment[:, None]
    earlier = numbers[None, :] < numbers[:, None]
    offsets = jnp.sum(jnp.where(same_group & earlier, patch_counts[None, :], 0), axis=1)
    row_ids = jnp.arange(total, dtype=jnp.int32)[:, None]
    inside = (
        (assignment[None, :] == group_idx)
        & (row_ids >= offsets[None, :])
        & (row_ids < offsets[None, :] + patch_counts[None, :])
    )
    return inside.astype(jnp.float32)


def gelu_tanh(pre_vals):
    return jax.nn.gelu(pre_vals, approximate=True)

LANES = 128


def head_windows(heads, head_dim):
    windows = []
    for head in range(heads):
        low, high = head * head_dim, (head + 1) * head_dim
        windows.append((low // LANES * LANES, -(-high // LANES) * LANES, low, high))
    return windows


def lane_mask(window):
    start, end, low, high = window
    lanes = start + lax.broadcasted_iota(jnp.int32, (1, end - start), 1)
    return ((lanes >= low) & (lanes < high)).astype(jnp.float32).astype(jnp.bfloat16)


def add_window(totals, window, value):
    start, end, _, _ = window
    for lane in range(start, end, LANES):
        piece = value[:, lane - start : lane - start + LANES]
        totals[lane] = piece if lane not in totals else totals[lane] + piece


def joined(totals):
    return jnp.concatenate([totals[lane] for lane in sorted(totals)], axis=1)


def same_position(rows, frames):
    left = lax.broadcasted_iota(jnp.int32, (rows, rows), 0) // frames
    right = lax.broadcasted_iota(jnp.int32, (rows, rows), 1) // frames
    return left == right


def head_probs(queries, keys, inside, scale):
    scores = lax.dot_general(queries, keys, COL_DIMS, preferred_element_type=jnp.float32) * scale
    scores = jnp.where(inside, scores, -1e30)
    weights = jnp.exp(scores - jnp.max(scores, axis=1, keepdims=True))
    return weights / jnp.sum(weights, axis=1, keepdims=True)


def attend_kernel(frames, scale, proj_ref, mixed_ref):
    rows, width = mixed_ref.shape
    inside = same_position(rows, frames)
    totals = {}
    for window in head_windows(HEADS, width // HEADS):
        cols = slice(window[0], window[1])
        mask = lane_mask(window)
        prob = head_probs(proj_ref[0, :, cols] * mask, proj_ref[1, :, cols], inside, scale)
        add_window(
            totals,
            window,
            jnp.dot(
                prob.astype(jnp.bfloat16),
                proj_ref[2, :, cols] * mask,
                preferred_element_type=jnp.float32,
            ),
        )
    mixed_ref[...] = joined(totals).astype(jnp.bfloat16)


def attend_back_kernel(frames, scale, proj_ref, grad_ref, out_ref):
    rows, width = grad_ref.shape
    inside = same_position(rows, frames)
    to_query, to_key, to_value = {}, {}, {}
    for window in head_windows(HEADS, width // HEADS):
        cols = slice(window[0], window[1])
        mask = lane_mask(window)
        queries = proj_ref[0, :, cols] * mask
        keys = proj_ref[1, :, cols]
        grads = grad_ref[:, cols] * mask
        prob = head_probs(queries, keys, inside, scale)
        grad_prob = lax.dot_general(
            grads, proj_ref[2, :, cols], COL_DIMS, preferred_element_type=jnp.float32
        )
        weighted = prob * grad_prob
        grad_scores = weighted - prob * jnp.sum(weighted, axis=1, keepdims=True)
        grad_scores = grad_scores.astype(jnp.bfloat16)
        add_window(
            to_value,
            window,
            lax.dot_general(
                prob.astype(jnp.bfloat16), grads, ROW_DIMS, preferred_element_type=jnp.float32
            ),
        )
        add_window(
            to_query,
            window,
            jnp.dot(grad_scores, keys * mask, preferred_element_type=jnp.float32),
        )
        add_window(
            to_key,
            window,
            lax.dot_general(grad_scores, queries, ROW_DIMS, preferred_element_type=jnp.float32),
        )
    out_ref[0] = (joined(to_query) * scale).astype(jnp.bfloat16)
    out_ref[1] = (joined(to_key) * scale).astype(jnp.bfloat16)
    out_ref[2] = joined(to_value).astype(jnp.bfloat16)


def tile_rows(positions, frames):
    for count in (8, 4, 2):
        if positions % count == 0:
            return count * frames
    return frames


def attend(projected, positions, frames, scale):
    _, rows, width = projected.shape
    tile = tile_rows(positions, frames)
    return pl.pallas_call(
        lambda *refs: attend_kernel(frames, scale, *refs),
        out_shape=jax.ShapeDtypeStruct((rows, width), jnp.bfloat16),
        grid=(rows // tile,),
        in_specs=[pl.BlockSpec((3, tile, width), lambda step: (0, step, 0))],
        out_specs=pl.BlockSpec((tile, width), lambda step: (step, 0)),
        cost_estimate=pl.CostEstimate(
            flops=22 * 10**9, bytes_accessed=8 * rows * width, transcendentals=0
        ),
        compiler_params=pltpu.CompilerParams(vmem_limit_bytes=40 << 20),
        name="attend",
    )(projected)


def attend_back(projected, grad_mixed, positions, frames, scale):
    _, rows, width = projected.shape
    tile = tile_rows(positions, frames)
    return pl.pallas_call(
        lambda *refs: attend_back_kernel(frames, scale, *refs),
        out_shape=jax.ShapeDtypeStruct((3, rows, width), jnp.bfloat16),
        grid=(rows // tile,),
        in_specs=[
            pl.BlockSpec((3, tile, width), lambda step: (0, step, 0)),
            pl.BlockSpec((tile, width), lambda step: (step, 0)),
        ],
        out_specs=pl.BlockSpec((3, tile, width), lambda step: (0, step, 0)),
        cost_estimate=pl.CostEstimate(
            flops=46 * 10**9, bytes_accessed=14 * rows * width, transcendentals=0
        ),
        compiler_params=pltpu.CompilerParams(vmem_limit_bytes=40 << 20),
        name="attend_back",
    )(projected, grad_mixed)


VMEM_LIMIT = 52 << 20
BF16, F32 = jnp.bfloat16, jnp.float32


def row_tile(rows):
    for tile in (224, 128, 112, 64, 32, 16):
        if rows % tile == 0:
            return tile
    return rows


def dot(left, right, dims=(((1,), (0,)), ((), ()))):
    return lax.dot_general(left, right, dims, preferred_element_type=F32)


def call(kernel, name, grid, ins, outs, scratch=(), flops=0, vmem=VMEM_LIMIT):
    moved = sum(array.size * array.dtype.itemsize for array, _ in ins)
    moved += sum(math.prod(shape) * jnp.dtype(dtype).itemsize for shape, dtype, _ in outs)
    return pl.pallas_call(
        kernel,
        out_shape=[jax.ShapeDtypeStruct(shape, dtype) for shape, dtype, _ in outs],
        grid=grid,
        in_specs=[spec for _, spec in ins],
        out_specs=[spec for _, _, spec in outs],
        scratch_shapes=list(scratch),
        cost_estimate=pl.CostEstimate(flops=flops, bytes_accessed=moved, transcendentals=0),
        compiler_params=pltpu.CompilerParams(vmem_limit_bytes=vmem),
        name=name,
    )(*[array for array, _ in ins])


HBM = pl.BlockSpec(memory_space=pl.ANY)
SCALARS = pl.BlockSpec(memory_space=pltpu.SMEM)


def whole(array):
    return pl.BlockSpec(array.shape, lambda step: (0,) * array.ndim)


def tiled(tile, width):
    return pl.BlockSpec((tile, width), lambda step: (step, 0))


class Pieces:
    def __init__(self, arrays, places, shape, slot_first):
        self.arrays, self.places, self.shape, self.slot_first = arrays, places, shape, slot_first

    def start(self, where_ref, refs, full, sems):
        for ref, place in zip(refs, self.places):
            slot, first, count = place(where_ref[0], where_ref[1])
            span = pl.ds(first, count)
            target = full.at[slot, span] if self.slot_first else full.at[span, slot]
            pltpu.make_async_copy(ref, target, sems.at[slot]).start()

    def wait(self, slot, full, sems):
        part = full.at[slot] if self.slot_first else full.at[:, slot]
        pltpu.make_async_copy(part, part, sems.at[slot]).wait()

    def scratch(self):
        return [pltpu.VMEM(self.shape, BF16), pltpu.SemaphoreType.DMA((5,))]


def norm_parts(values):
    center = values - jnp.mean(values, axis=1, keepdims=True)
    inverse = lax.rsqrt(jnp.mean(center * center, axis=1, keepdims=True) + 1e-06)
    return center * inverse, inverse


def norm_back(normed, inverse, grad):
    mean_grad = jnp.mean(grad, axis=1, keepdims=True)
    mean_both = jnp.mean(grad * normed, axis=1, keepdims=True)
    return (grad - mean_grad - normed * mean_both) * inverse


def row_order(rows, first, count, inner, outer):
    at = first + lax.broadcasted_iota(jnp.int32, (count, rows), 0)
    source = lax.broadcasted_iota(jnp.int32, (count, rows), 1)
    return (source == (at % outer) * inner + at // outer).astype(F32).astype(BF16)


def clip_sums(hot, values):
    high = values.astype(BF16)
    low = (values - high.astype(F32)).astype(BF16)
    return dot(hot, high, ROW_DIMS) + dot(hot, low, ROW_DIMS)


def add_into(ref, index, value):
    @pl.when(pl.program_id(0) == 0)
    def _():
        ref[index] = jnp.zeros_like(ref[index])

    ref[index] += value


def qkv_call(where, arrived, hot, mod, pieces, positions, frames):
    rows, width = arrived.shape
    tile = row_tile(rows)
    steps = rows // tile
    count = len(pieces.arrays)

    def kernel(where_ref, x_ref, hot_ref, mod_ref, *rest):
        piece_refs, rest = rest[:count], rest[count:]
        x_out, first_out, proj_out, full_out, full, sems = rest
        step = pl.program_id(0)

        @pl.when(step == 0)
        def _():
            pieces.start(where_ref, piece_refs, full, sems)

        order = row_order(rows, step * tile, tile, positions, frames)
        inputs = dot(order, x_ref[...])
        x_out[...] = inputs.astype(BF16)
        normed, _ = norm_parts(inputs)
        shift = dot(hot_ref[...], mod_ref[:, :width])
        scale = dot(hot_ref[...], mod_ref[:, width : 2 * width])
        first = (normed * (1.0 + scale) + shift).astype(BF16)
        first_out[...] = first
        back = pltpu.make_async_copy(full, full_out, sems.at[4])

        @pl.when(step == 0)
        def _():
            for slot in range(4):
                pieces.wait(slot, full, sems)
            back.start()

        for slot in range(3):
            proj_out[slot] = dot(first, full[slot]).astype(BF16)

        @pl.when(step == steps - 1)
        def _():
            back.wait()

    return call(
        kernel,
        "project",
        (steps,),
        [
            (where, SCALARS),
            (arrived, whole(arrived)),
            (hot, tiled(tile, hot.shape[1])),
            (mod, whole(mod)),
            *[(array, HBM) for array in pieces.arrays],
        ],
        [
            ((rows, width), BF16, tiled(tile, width)),
            ((rows, width), BF16, tiled(tile, width)),
            ((3, rows, width), BF16, pl.BlockSpec((3, tile, width), lambda step: (0, step, 0))),
            (pieces.shape, BF16, HBM),
        ],
        pieces.scratch(),
        flops=20 * 10**9,
    )


def out_call(mixed, x_rows, hot, mod, full_attn):
    rows, width = mixed.shape
    tile = row_tile(rows)

    def kernel(mixed_ref, x_ref, hot_ref, mod_ref, w_ref, attn_out, middle_out, second_out):
        attn = dot(mixed_ref[...], w_ref[0])
        hot = hot_ref[...]
        middle = x_ref[...].astype(F32) + dot(hot, mod_ref[:, 2 * width : 3 * width]) * attn
        normed, _ = norm_parts(middle)
        shift = dot(hot, mod_ref[:, 3 * width : 4 * width])
        scale = dot(hot, mod_ref[:, 4 * width : 5 * width])
        attn_out[...] = attn.astype(BF16)
        middle_out[...] = middle
        second_out[...] = (normed * (1.0 + scale) + shift).astype(BF16)

    return call(
        kernel,
        "attn_out",
        (rows // tile,),
        [
            (mixed, tiled(tile, width)),
            (x_rows, tiled(tile, width)),
            (hot, tiled(tile, hot.shape[1])),
            (mod, whole(mod)),
            (full_attn, pl.BlockSpec((1, width, width), lambda step: (3, 0, 0))),
        ],
        [
            ((rows, width), BF16, tiled(tile, width)),
            ((rows, width), F32, tiled(tile, width)),
            ((rows, width), BF16, tiled(tile, width)),
        ],
        flops=9 * 10**9,
    )


GELU_A = math.sqrt(2.0 / math.pi)
GELU_B = GELU_A * 0.044715


def fc1_call(where, second_in, bias, pieces):
    rows, width = second_in.shape
    tile = row_tile(rows)
    steps = rows // tile
    count = len(pieces.arrays)
    part = pieces.shape[2]

    def kernel(where_ref, x_ref, bias_ref, *rest):
        piece_refs, rest = rest[:count], rest[count:]
        post_out, slope_out, full_out, full, sems = rest
        step = pl.program_id(0)
        back = pltpu.make_async_copy(full, full_out, sems.at[4])

        @pl.when(step == 0)
        def _():
            pieces.start(where_ref, piece_refs, full, sems)
            for slot in range(4):
                pieces.wait(slot, full, sems)
            back.start()

        for slot in range(4):
            cols = slice(slot * part, (slot + 1) * part)
            pre = dot(x_ref[...], full[slot]) + bias_ref[:, cols].astype(F32)
            square = pre * pre
            curve = jnp.tanh(pre * (GELU_A + GELU_B * square))
            half = 0.5 + 0.5 * curve
            post_out[:, cols] = (pre * half).astype(BF16)
            rise = (0.5 * pre) * (1.0 - curve * curve)
            slope_out[:, cols] = (half + rise * (GELU_A + 3.0 * GELU_B * square)).astype(BF16)

        @pl.when(step == steps - 1)
        def _():
            back.wait()

    return call(
        kernel,
        "fc1",
        (steps,),
        [
            (where, SCALARS),
            (second_in, tiled(tile, width)),
            (bias, whole(bias)),
            *[(array, HBM) for array in pieces.arrays],
        ],
        [
            ((rows, 4 * part), BF16, tiled(tile, 4 * part)),
            ((rows, 4 * part), BF16, tiled(tile, 4 * part)),
            (pieces.shape, BF16, HBM),
        ],
        pieces.scratch(),
        flops=25 * 10**9,
    )


def cot_call(arrived, hot, mod, positions, frames):
    rows, width = arrived.shape
    tile = row_tile(rows)

    def kernel(cot_ref, hot_ref, mod_ref, rows_out, mlp_out):
        order = row_order(rows, pl.program_id(0) * tile, tile, positions, frames)
        hot = hot_ref[...]
        valid = jnp.sum(hot.astype(F32), axis=1, keepdims=True)
        grad = dot(order, cot_ref[...]) * valid
        rows_out[...] = grad.astype(BF16)
        mlp_out[...] = (grad * dot(hot, mod_ref[:, 5 * width :])).astype(BF16)

    return call(
        kernel,
        "cotangent",
        (rows // tile,),
        [
            (arrived, whole(arrived)),
            (hot, tiled(tile, hot.shape[1])),
            (mod, whole(mod)),
        ],
        [
            ((rows, width), BF16, tiled(tile, width)),
            ((rows, width), BF16, tiled(tile, width)),
        ],
        flops=6 * 10**9,
    )


def fc2_call(where, post_act, slope, grad_mlp, grad_rows, middle, hot, mod, pieces, positions, frames):
    rows, hidden = post_act.shape
    width = grad_mlp.shape[1]
    tile = row_tile(rows)
    steps = rows // tile
    count = len(pieces.arrays)
    clips = hot.shape[1]
    turns = pieces.shape[0] // 4
    part = hidden // 4

    def kernel(where_ref, post_ref, slope_ref, gmlp_ref, grows_ref, mid_ref, hot_ref, mod_ref, *rest):
        piece_refs, rest = rest[:count], rest[count:]
        block_out, pre_out, bias_out, gate_out, full, sems, held = rest
        step = pl.program_id(0)

        @pl.when(step == 0)
        def _():
            pieces.start(where_ref, piece_refs, full, sems)
            for slot in range(4):
                pieces.wait(slot, full, sems)

        total = None
        for at in range(4):
            cols = slice(at * part, (at + 1) * part)
            weight = full[at * turns : (at + 1) * turns].reshape(part, width)
            term = dot(post_ref[:, cols], weight)
            total = term if total is None else total + term
            grad_pre = (dot(gmlp_ref[...], weight, COL_DIMS) * slope_ref[:, cols].astype(F32)).astype(BF16)
            pre_out[:, cols] = grad_pre
            add_into(
                bias_out,
                (slice(None), cols),
                jnp.sum(grad_pre.astype(F32), axis=0, keepdims=True),
            )
        hot = hot_ref[...]
        valid = jnp.sum(hot.astype(F32), axis=1, keepdims=True)
        gate = dot(hot, mod_ref[:, 5 * width :])
        result = valid * (mid_ref[...] + gate * total)
        held[pl.ds(pl.multiple_of(step * tile, 16), tile), :] = result.astype(BF16)
        add_into(gate_out, slice(None), clip_sums(hot, grows_ref[...].astype(F32) * total))

        @pl.when(step == steps - 1)
        def _():
            for at in range(steps):
                order = row_order(rows, at * tile, tile, frames, positions)
                block_out[at * tile : (at + 1) * tile, :] = dot(order, held[...]).astype(BF16)

    return call(
        kernel,
        "fc2",
        (steps,),
        [
            (where, SCALARS),
            (post_act, tiled(tile, hidden)),
            (slope, tiled(tile, hidden)),
            (grad_mlp, tiled(tile, width)),
            (grad_rows, tiled(tile, width)),
            (middle, tiled(tile, width)),
            (hot, tiled(tile, clips)),
            (mod, whole(mod)),
            *[(array, HBM) for array in pieces.arrays],
        ],
        [
            ((rows, width), BF16, pl.BlockSpec((rows, width), lambda step: (0, 0))),
            ((rows, hidden), BF16, tiled(tile, hidden)),
            ((1, hidden), F32, pl.BlockSpec((1, hidden), lambda step: (0, 0))),
            ((clips, width), F32, pl.BlockSpec((clips, width), lambda step: (0, 0))),
        ],
        [*pieces.scratch(), pltpu.VMEM((rows, width), BF16)],
        flops=44 * 10**9,
    )


def fc1_back_call(grad_pre, full_fc1, middle, attn_out, grad_rows, hot, mod, full_attn):
    rows, hidden = grad_pre.shape
    width = middle.shape[1]
    tile = row_tile(rows)
    clips = hot.shape[1]
    part = hidden // 4

    def kernel(pre_ref, w_ref, mid_ref, attn_ref, grows_ref, hot_ref, mod_ref, wo_ref, *outs):
        gmid_out, gattn_out, gmix_out, sums_out = outs
        grad = None
        for at in range(4):
            term = dot(pre_ref[:, at * part : (at + 1) * part], w_ref[at], COL_DIMS)
            grad = term if grad is None else grad + term
        hot = hot_ref[...]
        scale = dot(hot, mod_ref[:, 4 * width : 5 * width])
        gate = dot(hot, mod_ref[:, 2 * width : 3 * width])
        normed, inverse = norm_parts(mid_ref[...])
        grad_middle = grows_ref[...].astype(F32) + norm_back(normed, inverse, grad * (1.0 + scale))
        gmid_out[...] = grad_middle
        grad_attn = (grad_middle * gate).astype(BF16)
        gattn_out[...] = grad_attn
        gmix_out[...] = dot(grad_attn, wo_ref[0], COL_DIMS).astype(BF16)
        add_into(sums_out, 0, clip_sums(hot, grad_middle * attn_ref[...].astype(F32)))
        add_into(sums_out, 1, clip_sums(hot, grad))
        add_into(sums_out, 2, clip_sums(hot, grad * normed))

    return call(
        kernel,
        "fc1_back",
        (rows // tile,),
        [
            (grad_pre, tiled(tile, hidden)),
            (full_fc1, whole(full_fc1)),
            (middle, tiled(tile, width)),
            (attn_out, tiled(tile, width)),
            (grad_rows, tiled(tile, width)),
            (hot, tiled(tile, clips)),
            (mod, whole(mod)),
            (full_attn, pl.BlockSpec((1, width, width), lambda step: (3, 0, 0))),
        ],
        [
            ((rows, width), F32, tiled(tile, width)),
            ((rows, width), BF16, tiled(tile, width)),
            ((rows, width), BF16, tiled(tile, width)),
            ((3, clips, width), F32, pl.BlockSpec((3, clips, width), lambda step: (0, 0, 0))),
        ],
        flops=32 * 10**9,
    )


def qkv_back_call(grad_proj, full_attn, x_rows, grad_middle, hot, mod, positions, frames):
    _, rows, width = grad_proj.shape
    tile = row_tile(rows)
    steps = rows // tile
    clips = hot.shape[1]

    def kernel(proj_ref, w_ref, x_ref, gmid_ref, hot_ref, mod_ref, tok_out, sums_out, held):
        step = pl.program_id(0)
        grad = None
        for at in range(3):
            term = dot(proj_ref[at], w_ref[at], COL_DIMS)
            grad = term if grad is None else grad + term
        hot = hot_ref[...]
        scale = dot(hot, mod_ref[:, width : 2 * width])
        normed, inverse = norm_parts(x_ref[...].astype(F32))
        result = gmid_ref[...] + norm_back(normed, inverse, grad * (1.0 + scale))
        held[pl.ds(pl.multiple_of(step * tile, 16), tile), :] = result.astype(BF16)
        add_into(sums_out, 0, clip_sums(hot, grad))
        add_into(sums_out, 1, clip_sums(hot, grad * normed))

        @pl.when(step == steps - 1)
        def _():
            for at in range(steps):
                order = row_order(rows, at * tile, tile, frames, positions)
                tok_out[at * tile : (at + 1) * tile, :] = dot(order, held[...]).astype(BF16)

    return call(
        kernel,
        "project_back",
        (steps,),
        [
            (grad_proj, pl.BlockSpec((3, tile, width), lambda step: (0, step, 0))),
            (full_attn, pl.BlockSpec((3, width, width), lambda step: (0, 0, 0))),
            (x_rows, tiled(tile, width)),
            (grad_middle, tiled(tile, width)),
            (hot, tiled(tile, clips)),
            (mod, whole(mod)),
        ],
        [
            ((rows, width), BF16, pl.BlockSpec((rows, width), lambda step: (0, 0))),
            ((2, clips, width), F32, pl.BlockSpec((2, clips, width), lambda step: (0, 0, 0))),
        ],
        [pltpu.VMEM((rows, width), BF16)],
        flops=23 * 10**9,
    )


def split_store(product, where_ref, keep_out, give_out, rows, slot_first):
    units = product.shape[0] // rows
    for core in range(2):

        @pl.when(where_ref[1] == core)
        def _():
            for unit in range(units):
                piece = product[unit * rows : (unit + 1) * rows]
                side = unit % 2 if slot_first else unit // 4
                out = keep_out if side == core else give_out
                if slot_first:
                    out[0, unit // 2] = piece
                else:
                    out[unit % 4, 0] = piece


def terms_out(chips, rows, width, slot_first):
    if slot_first:
        spec = pl.BlockSpec((1, chips, rows, width), lambda step: (step, 0, 0, 0))
    else:
        spec = pl.BlockSpec((4, 1, rows, width), lambda step: (0, step, 0, 0))
    return [((4, chips, rows, width), BF16, spec)] * 2


def fc2_terms(where, post_act, grad_mlp, chips):
    count, hidden = post_act.shape
    width = grad_mlp.shape[1]
    block, rows = hidden // chips, hidden // chips // 8

    def kernel(where_ref, left_ref, right_ref, keep_out, give_out):
        product = dot(left_ref[...], right_ref[...], ROW_DIMS).astype(BF16)
        split_store(product, where_ref, keep_out, give_out, rows, False)

    return call(
        kernel,
        "fc2_terms",
        (chips,),
        [
            (where, SCALARS),
            (post_act, pl.BlockSpec((count, block), lambda step: (0, step))),
            (grad_mlp, whole(grad_mlp)),
        ],
        terms_out(chips, rows, width, False),
        flops=18 * 10**9,
    )


def fc1_terms(where, second_in, grad_pre, chips):
    count, hidden = grad_pre.shape
    width = second_in.shape[1]
    rows, part = width // chips // 2, hidden // 4

    def kernel(where_ref, left_ref, right_ref, keep_out, give_out):
        product = dot(left_ref[...], right_ref[...], ROW_DIMS).astype(BF16)
        split_store(product, where_ref, keep_out, give_out, rows, True)

    return call(
        kernel,
        "fc1_terms",
        (4,),
        [
            (where, SCALARS),
            (second_in, whole(second_in)),
            (grad_pre, pl.BlockSpec((count, part), lambda step: (0, step))),
        ],
        terms_out(chips, rows, part, True),
        flops=18 * 10**9,
    )


def attn_terms(where, first_in, grad_proj, mixed, grad_attn, chips):
    count, width = first_in.shape
    rows = width // chips // 2

    def kernel(where_ref, first_ref, proj_ref, mixed_ref, attn_ref, keep_out, give_out):
        step = pl.program_id(0)

        @pl.when(step < 3)
        def _():
            product = dot(first_ref[...], proj_ref[0], ROW_DIMS).astype(BF16)
            split_store(product, where_ref, keep_out, give_out, rows, True)

        @pl.when(step == 3)
        def _():
            product = dot(mixed_ref[...], attn_ref[...], ROW_DIMS).astype(BF16)
            split_store(product, where_ref, keep_out, give_out, rows, True)

    return call(
        kernel,
        "attn_terms",
        (4,),
        [
            (where, SCALARS),
            (first_in, whole(first_in)),
            (
                grad_proj,
                pl.BlockSpec((1, count, width), lambda step: (jnp.minimum(step, 2), 0, 0)),
            ),
            (mixed, whole(mixed)),
            (grad_attn, whole(grad_attn)),
        ],
        terms_out(chips, rows, width, True),
        flops=19 * 10**9,
    )


X_SWAP = [(0, 1), (1, 0), (2, 3), (3, 2)]
Y_SWAP = [(0, 2), (2, 0), (1, 3), (3, 1)]


def swap_x(value):
    return lax.ppermute(value, "item", X_SWAP)


def swap_y(value):
    return lax.ppermute(value, "item", Y_SWAP)


def swap_core(value):
    count = lax.axis_size("frame")
    return lax.ppermute(value, "frame", [(at, at ^ 1) for at in range(count)])


def is_square():
    return lax.axis_size("item") == 4 and lax.axis_size("frame") % 2 == 0


def after(value, *others):
    return lax.optimization_barrier((value, *others))[0]


def after2(values, *others):
    return lax.optimization_barrier((*values, *others))[: len(values)]


def pick(stack, index):
    return lax.dynamic_index_in_dim(stack, index, 0, keepdims=False)


def by_column_quarter(stack):
    return jnp.concatenate([stack[part] for part in range(4)], axis=1)


def gather_frame(parts):
    if not is_square():
        return lax.all_gather(parts, "frame", axis=1)
    return lax.all_gather(pick(parts, lax.axis_index("item")), "frame", axis=0)


class Spread:
    def __init__(self, gathered, slot_first):
        self.gathered, self.slot_first = gathered, slot_first
        self.square = is_square()

    def near(self, *wait_for):
        if not self.square:
            return ()
        self.gathered = after(self.gathered, *wait_for)
        half = self.gathered.shape[0] // 2
        core = lax.axis_index("frame") % 2
        own = lax.dynamic_slice_in_dim(self.gathered, core * half, half, 0)
        self.cut = half // 2
        self.from_x, self.from_y = swap_x(own), swap_y(own)
        return self.from_x, self.from_y

    def far(self, *wait_for):
        if not self.square:
            return ()
        from_x, from_y = after2((self.from_x, self.from_y), *wait_for)
        self.far_low, self.far_high = swap_y(from_x[: self.cut]), swap_x(from_y[self.cut :])
        self.core_x, self.core_y = swap_core(from_x), swap_core(from_y)
        return self.far_low, self.far_high

    def pieces(self):
        gathered, slot_first = self.gathered, self.slot_first
        if not self.square:
            _, count, rows, width = gathered.shape
            if slot_first:
                return Pieces(
                    [gathered[part].reshape(count * rows, width) for part in range(4)],
                    [lambda item, core, part=part: (part, 0, count * rows) for part in range(4)],
                    (4, count * rows, width),
                    True,
                )
            return Pieces(
                [gathered[part] for part in range(4)],
                [lambda item, core, part=part: (part, 0, count) for part in range(4)],
                (count, 4, rows, width),
                False,
            )
        count, rows, width = gathered.shape
        half, cut = count // 2, self.cut
        far = [self.far_low, self.far_high]
        arrays = [gathered, self.from_x, self.from_y, *far, self.core_x, self.core_y]
        arrays += [swap_core(value) for value in far]
        unit = rows if slot_first else 1
        if slot_first:
            arrays = [array.reshape(-1, width) for array in arrays]
            shape = (4, count * rows, width)
        else:
            shape = (count, 4, rows, width)
        places = [lambda item, core: (item, 0, count * unit)]
        for flip in (0, 1):
            for slot, start, length in ((1, 0, half), (2, 0, half), (3, 0, cut), (3, cut, half - cut)):
                places.append(
                    lambda item, core, flip=flip, slot=slot, start=start, length=length: (
                        item ^ slot,
                        ((core ^ flip) * half + start) * unit,
                        length * unit,
                    )
                )
        return Pieces(arrays, places, shape, slot_first)


class Collect:
    def __init__(self, keep, give):
        self.keep, self.give = keep, give
        self.item = lax.axis_index("item")

    def pair(self):
        self.got = swap_core(self.give)

    def near(self, *wait_for):
        got = after(self.got, *wait_for)
        cut = self.keep.shape[1] // 2
        item = self.item

        def low(slot):
            return pick(self.keep[:, :cut], slot) + pick(got[:, :cut], slot)

        def high(slot):
            return pick(self.keep[:, cut:], slot) + pick(got[:, cut:], slot)

        x_out = jnp.stack([low(item ^ 1), low(item ^ 3)])
        y_out = jnp.stack([high(item ^ 2), high(item ^ 3)])
        self.low, self.low_on = low(item), low(item ^ 2)
        self.high, self.high_on = high(item), high(item ^ 1)
        self.x_in, self.y_in = swap_x(x_out), swap_y(y_out)
        return self.low, self.low_on, self.high, self.high_on, x_out, y_out

    def far(self, *wait_for):
        x_in, y_in = after2((self.x_in, self.y_in), *wait_for)
        low_on, high_on = self.low_on + x_in[1], self.high_on + y_in[1]
        self.low, self.high = self.low + x_in[0], self.high + y_in[0]
        self.y_far, self.x_far = swap_y(low_on), swap_x(high_on)
        return low_on, high_on

    def line(self, *wait_for):
        y_far, x_far = after2((self.y_far, self.x_far), *wait_for)
        plane = jnp.concatenate([self.low + y_far, self.high + x_far], axis=0)
        count = lax.axis_size("frame")
        groups = [list(range(side, count, 2)) for side in range(2)]
        self.own = lax.psum_scatter(
            plane, "frame", scatter_dimension=0, tiled=False, axis_index_groups=groups
        )
        return (plane,)

    def finish(self):
        own, item = self.own, self.item
        far = lax.ppermute(own, "item", [(at, at ^ 3) for at in range(4)])
        stack = jnp.stack([own, swap_x(own), swap_y(own), far])
        return jnp.stack([pick(stack, item ^ part) for part in range(4)])


def sum_plain(partial):
    share = lax.psum_scatter(partial.astype(BF16), "frame", scatter_dimension=1, tiled=False)
    return lax.psum(share, "item")


def share_small(value):
    count = lax.axis_size("frame")
    return lax.all_to_all(
        jnp.broadcast_to(value[None], (count, *value.shape)), "frame", 0, 0, tiled=False
    )


def sum_items(value):
    if not is_square():
        return lax.psum(value.astype(BF16), "item").astype(F32)
    value = value + swap_x(value.astype(BF16)).astype(F32)
    return value + swap_y(value.astype(BF16)).astype(F32)


def round_up(number, unit):
    return -(-number // unit) * unit


def body(
    tokens,
    cotangent,
    patch_counts,
    assignment,
    timesteps,
    class_ids,
    w_qkv,
    w_out,
    w_fc1,
    b_fc1,
    w_fc2,
    w_ada,
    b_ada,
    class_table,
):
    frame_count = lax.axis_size("frame")
    group_idx = lax.axis_index("item")
    frame_pos = lax.axis_index("frame")
    _, own_frames, capacity, width = tokens.shape
    frames = own_frames * frame_count
    positions = capacity // frame_count
    rows = frames * positions
    clips = patch_counts.shape[0]
    attn_scale = 1.0 / math.sqrt(width // HEADS)
    where = jnp.stack([group_idx, frame_pos % 2, frame_pos]).astype(jnp.int32)

    def to_positions(value):
        chunks = value[0].reshape(own_frames, frame_count, positions, width).transpose(1, 0, 2, 3)
        return lax.all_to_all(chunks, "frame", 0, 0, tiled=True).reshape(rows, width)

    def to_frames(value, *wait_for):
        chunks = value.reshape(frame_count, own_frames, positions, width)
        moved = after(lax.all_to_all(chunks, "frame", 0, 0, tiled=True), *wait_for)
        return moved.transpose(1, 0, 2, 3).reshape(1, own_frames, capacity, width)

    layout = row_items(patch_counts, assignment, group_idx, capacity)
    my_rows = lax.dynamic_slice_in_dim(layout, frame_pos * positions, positions, 0)
    class_hot = (class_ids[:, None] == jnp.arange(CLASSES, dtype=jnp.int32)[None, :]).astype(F32)
    condition = time_features(timesteps) + jnp.dot(class_hot, class_table, precision=HIGHEST)
    activated = jax.nn.silu(condition)
    ada_part = jnp.dot(activated, w_ada.astype(F32), precision=HIGHEST) + b_ada.astype(F32)

    ada_cols, bias_cols = b_ada.shape[0], b_fc1.shape[0]
    small_rows, small_cols = round_up(clips + 1, 16), round_up(max(ada_cols, bias_cols), LANES)
    small = jnp.concatenate(
        [
            jnp.pad(ada_part.astype(BF16), ((0, 0), (0, small_cols - ada_cols))),
            jnp.pad(b_fc1[None], ((0, small_rows - clips - 1), (0, small_cols - bias_cols))),
        ],
        axis=0,
    )
    x_arrived = to_positions(tokens)
    small_all = share_small(after(small, x_arrived))
    clip_slots = round_up(clips, 16)
    mod = small_all[:, :clips, :ada_cols].transpose(1, 0, 2).reshape(clips, -1)
    mod = jnp.pad(mod, ((0, clip_slots - clips), (0, 0)))
    bias = small_all[:, clips, :bias_cols].reshape(1, -1)
    hot = jnp.pad(my_rows.astype(BF16), ((0, 0), (0, clip_slots - clips)))
    hot = jnp.repeat(hot, frames, axis=0)

    shard_rows = w_out.shape[0]
    got_attn = gather_frame(jnp.stack([*jnp.split(w_qkv, 3, axis=1), w_out]))
    spread_attn = Spread(got_attn, True)
    near_attn = spread_attn.near()
    got_fc1 = gather_frame(
        after(jnp.stack(jnp.split(w_fc1, 4, axis=1)), x_arrived, *near_attn)
    )
    far_attn = spread_attn.far()
    fc2_rows = w_fc2.shape[0] // 4
    got_fc2 = gather_frame(after(w_fc2.reshape(4, fc2_rows, width), *far_attn))

    square = is_square()
    chips = frame_count // 2
    spread_fc1 = Spread(got_fc1, True)
    spread_fc2 = Spread(got_fc2, False)
    cot_arrived = to_positions(after(cotangent, x_arrived))
    near_fc1 = spread_fc1.near(*far_attn)
    x_rows, first_in, projected, full_attn = qkv_call(
        where, x_arrived, hot, mod, spread_attn.pieces(), positions, frames
    )
    mixed = attend(after(projected, *near_fc1), positions, frames, attn_scale)
    far_fc1 = spread_fc1.far()
    near_fc2 = spread_fc2.near(*far_fc1)
    attn_out, middle, second_in = out_call(
        after(mixed, *far_fc1), x_rows, hot, mod, full_attn
    )
    far_fc2 = spread_fc2.far()
    grad_rows, grad_mlp = cot_call(after(cot_arrived, second_in), hot, mod, positions, frames)
    post_act, slope, full_fc1 = fc1_call(
        where, after(second_in, grad_mlp), bias, spread_fc1.pieces()
    )

    if square:
        sum_fc2 = Collect(*fc2_terms(where, post_act, after(grad_mlp, *near_fc2), chips))
        sum_fc2.pair()
        seen = (sum_fc2.give,)
    else:
        part_fc2 = lax.dot_general(post_act, grad_mlp, ROW_DIMS, preferred_element_type=F32)
        part_fc2 = part_fc2.reshape(frame_count, 4, fc2_rows, width).transpose(1, 0, 2, 3)
        seen = ()
    block_rows, grad_pre, part_bias, sum_gate_mlp = fc2_call(
        where,
        post_act,
        slope,
        after(grad_mlp, *seen),
        grad_rows,
        middle,
        hot,
        mod,
        spread_fc2.pieces(),
        positions,
        frames,
    )
    if square:
        seen = sum_fc2.near(grad_pre)
        sum_fc1 = Collect(*fc1_terms(where, second_in, after(grad_pre, *seen), chips))
        sum_fc1.pair()
        seen = (sum_fc1.give,)
    else:
        part_fc1 = [dot(second_in, part, ROW_DIMS) for part in jnp.split(grad_pre, 4, axis=1)]
        part_fc1 = jnp.stack(part_fc1).reshape(4, frame_count, shard_rows, -1)
    grad_middle, grad_attn, grad_mixed, sums_mlp = fc1_back_call(
        after(grad_pre, *seen), full_fc1, middle, attn_out, grad_rows, hot, mod, full_attn
    )
    block_out = to_frames(block_rows, grad_mixed)
    seen = ()
    if square:
        seen = (*sum_fc2.far(grad_mixed), *sum_fc1.near(grad_mixed), block_out)
    grad_proj = attend_back(
        projected, after(grad_mixed, *seen), positions, frames, attn_scale
    )
    if square:
        seen = (*sum_fc2.line(grad_proj), *sum_fc1.far(grad_proj))
        sum_attn = Collect(
            *attn_terms(where, first_in, after(grad_proj, *seen), mixed, grad_attn, chips)
        )
        sum_attn.pair()
        seen = (*sum_fc1.line(sum_attn.give), *sum_attn.near())
    else:
        part_attn = [dot(first_in, grad_proj[part], ROW_DIMS) for part in range(3)]
        part_attn = jnp.stack([*part_attn, dot(mixed, grad_attn, ROW_DIMS)])
        part_attn = part_attn.reshape(4, frame_count, shard_rows, width)
    token_rows, sums_attn = qkv_back_call(
        after(grad_proj, *seen), full_attn, x_rows, grad_middle, hot, mod, positions, frames
    )
    if square:
        sum_attn.far(token_rows)
        sum_attn.line()
        sum_fc2, sum_fc1, sum_attn = sum_fc2.finish(), sum_fc1.finish(), sum_attn.finish()
    else:
        sum_fc2, sum_fc1, sum_attn = sum_plain(part_fc2), sum_plain(part_fc1), sum_plain(part_attn)
    part_mod = jnp.concatenate([sums_attn, sums_mlp, sum_gate_mlp[None]], axis=0)[:, :clips]
    part_mod = part_mod.transpose(1, 0, 2).reshape(clips, frame_count, ada_cols)
    part_small = jnp.concatenate(
        [
            jnp.pad(part_mod, ((0, 0), (0, 0), (0, small_cols - ada_cols))),
            jnp.pad(
                part_bias.reshape(1, frame_count, bias_cols),
                ((0, small_rows - clips - 1), (0, 0), (0, small_cols - bias_cols)),
            ),
        ],
        axis=0,
    ).astype(BF16)
    small_terms = lax.all_to_all(part_small.transpose(1, 0, 2), "frame", 0, 0, tiled=False)
    grad_tokens = to_frames(after(token_rows, small_terms))
    small_sum = sum_items(jnp.sum(small_terms.astype(F32), axis=0))
    grad_modulation = small_sum[:clips, :ada_cols]
    sum_bias = small_sum[clips, :bias_cols]
    grad_w_ada = lax.dot_general(activated, grad_modulation, ROW_DIMS, precision=HIGHEST)
    grad_b_ada = jnp.sum(grad_modulation, axis=0)
    act_part = lax.dot_general(grad_modulation, w_ada.astype(F32), COL_DIMS, precision=HIGHEST)
    grad_activated = jnp.sum(share_small(act_part.astype(BF16)).astype(F32), axis=0)
    _, silu_back = jax.vjp(jax.nn.silu, condition)
    grad_condition = silu_back(grad_activated)[0]
    grad_table = lax.dot_general(class_hot, grad_condition, ROW_DIMS, precision=HIGHEST)
    return (
        block_out,
        grad_tokens,
        by_column_quarter(sum_attn)[:, : 3 * width].astype(F32),
        sum_attn[3].astype(F32),
        by_column_quarter(sum_fc1).astype(F32),
        sum_bias,
        sum_fc2.reshape(-1, width).astype(F32),
        grad_w_ada,
        grad_b_ada,
        grad_table,
    )


def solution(mesh):
    return jax.shard_map(
        body,
        mesh=mesh,
        in_specs=(
            P("item", "frame", None, None),
            P("item", "frame", None, None),
            P(),
            P(),
            P(),
            P(),
            P("frame", None),
            P("frame", None),
            P("frame", None),
            P("frame"),
            P("frame", None),
            P(None, "frame"),
            P("frame"),
            P(),
        ),
        out_specs=(
            P("item", "frame", None, None),
            P("item", "frame", None, None),
            P("frame", None),
            P("frame", None),
            P("frame", None),
            P("frame"),
            P("frame", None),
            P(None, "frame"),
            P("frame"),
            P(),
        ),
        check_vma=False,
    )
```

time: 1150 us -> 712 us (0.62)
  waiting for transfers between devices: 502 us -> 191 us
  Pallas kernels: 0 us -> 283 us
  matrix products: 225 us -> 10.4 us
  blocking collectives: 157 us -> 0 us
  local copies, waits for them, and re-layouts: 133 us -> 72.1 us
  starting transfers between devices: 20.3 us -> 78.2 us
  other arithmetic: 92.5 us -> 50.6 us
    reduce_scatter x4 -> x3, waiting for transfers between devices: 313 us -> 24.8 us  [line(): lax.psum_scatter(plane, 'frame', scatter_dimension=0, tiled=False, axis_i...]
    pallas_call x0 -> x12, Pallas kernels: none -> 283 us  [the longest x10 214 us: call(): pl.pallas_call(kernel, out_shape=[jax.ShapeDtypeStruct(shape, dtype) for...]
    dot_general x23 -> x3, matrix products: 223 us -> 7.81 us  [the longest x1 5.25 us: body(): lax.dot_general(activated, grad_modulation, ROW_DIMS, precision=HIGHEST)]
    unnamed x2 -> x0, blocking collectives: 117 us -> none
    ppermute x0 -> x50, waiting for transfers between devices: none -> 80.1 us  [the longest x16 47.8 us: swap_x(): return lax.ppermute(value, 'item', X_SWAP)]
    all_to_all x4 -> x7, waiting for transfers between devices: 96.7 us -> 34.4 us  [the longest x2 14.5 us: to_positions(): lax.all_to_all(chunks, 'frame', 0, 0, tiled=True).reshape(rows, width)]
    convert_element_type x6 -> x0, local copies, waits for them, and re-layouts: 53.9 us -> none  [the longest x3 42.9 us: body(): grad_proj = jnp.stack([grad_query, grad_key, grad_value], axis=2).astype(...]
    all_gather x4 -> x3, waiting for transfers between devices: 5.17 us -> 52 us  [gather_frame(): return lax.all_gather(pick(parts, lax.axis_index('item')), 'frame', axis=0)]
  transfers between devices with their start and end apart: 14 -> 63, of which waited for: 7 -> 27; matrix products, arithmetic and copies ran while one was open for 23% -> 16% of each run, Pallas kernels for 0% -> 38%
where the time goes in v1:
time: 712 us; the launch traced here: 701 us
  Pallas kernels  283 us (40%)
  waiting for transfers between devices  191 us (27%)
  starting transfers between devices  78.2 us (11%)
  local copies, waits for them, and re-layouts  72.1 us (10%)
  other arithmetic  50.6 us (7%)
  between operations  15.1 us (2%)
  matrix products  10.4 us (1%)
    pallas_call x10, Pallas kernels, call(): pl.pallas_call(kernel, out_shape=[jax.ShapeDtypeStruct(shape, dtype) for...  214 us
    all_gather x3, waiting for transfers between devices, gather_frame(): return lax.all_gather(pick(parts, lax.axis_index('item')), 'frame', axis=0)  52 us
    ppermute x16, waiting for transfers between devices, swap_x(): return lax.ppermute(value, 'item', X_SWAP)  47.8 us
    pallas_call x1, Pallas kernels, attend_back(): pl.pallas_call(lambda *refs: attend_back_kernel(frames, scale, *refs), ou...  46.7 us
    ppermute x16, waiting for transfers between devices, swap_y(): return lax.ppermute(value, 'item', Y_SWAP)  28.1 us
    reduce_scatter x3, waiting for transfers between devices, line(): lax.psum_scatter(plane, 'frame', scatter_dimension=0, tiled=False, axis_i...  24.8 us
    slice x6, local copies, waits for them, and re-layouts, high(): return pick(self.keep[:, cut:], slot) + pick(got[:, cut:], slot)  22.9 us
    pallas_call x1, Pallas kernels, attend(): pl.pallas_call(lambda *refs: attend_kernel(frames, scale, *refs), out_sha...  22.1 us
  transfers between devices with their start and end apart: 63, of which 27 were waited for; matrix products, arithmetic and copies ran while one was open for 16% of the time, Pallas kernels for 38%

profile of v1, /device:TPU:0, one launch (start us, length us, event | category | flops | bytes accessed | tf_op | source)
XLA Modules:
  0.0 700.9 jit_solution(5695387531578895947)
XLA Ops:
  12.8 6.3 all-to-all-start
  19.2 49.5 %all-gather.4.cloned.1.call-done = bf16[8,144,1152]{2,1,0:T(8,128)(2,1)} async-done(((bf16[1,144,1152]{2,1,0:T(8,128)(2,1)}), bf16[8,144,1152]{2,1,0:T(8,128)(2,1)}) %all-gather.4.cloned.1.call-update) | async-done | bytes 2654224 | tf_op jit(solution)/shard_map/all_gather | solution.py:785
  74.4 14.5 %all-to-all-done = bf16[8,2,56,1152]{3,2,1,0:T(8,128)(2,1)} async-done(((bf16[8,2,56,1152]{3,2,1,0:T(8,128)(2,1)}), bf16[8,2,56,1152]{3,2,1,0:T(8,128)(2,1)}, u32[]{:S(2)}, u32[]{:S(2)}) %all-to-all-start) | async-done | bytes 2064416 | tf_op jit(solution)/shard_map/all_to_all | solution.py:955
  88.9 13.8 %collective-permute-done = bf16[4,144,1152]{2,1,0:T(8,128)(2,1)} collective-permute-done((bf16[4,144,1152]{2,1,0:T(8,128)(2,1)}, bf16[4,144,1152]{2,1,0:T(8,128)(2,1)}, u32[]{:S(2)}, u32[]{:S(2)}) %collective-permute-start) | collective-permute-done | bytes 1327136 | tf_op jit(solution)/shard_map/ppermute | solution.py:750
  115.6 6.8 all-to-all-start.1
  150.8 20.6 %project.1 = (bf16[896,1152]{1,0:T(8,128)(2,1)}, bf16[896,1152]{1,0:T(8,128)(2,1)}, bf16[3,896,1152]{2,1,0:T(8,128)(2,1)}, bf16[4,1152,1152]{2,1,0:T(8,128)(2,1)}) custom-call(s32[3]{0:T(128)S(1)} %pad_add_fusion.where_ref, bf16[896,1152]{1,0:T(8,128)(2,1)} %bitcast.5.x_ref, bf16[896,16]{1,0:T(8,128)(2,1)S(1)} %bitcast.157, ...), custom_call_target="tpu_custom_call" | custom-call | flops 20000000000 | bytes 33869836 | tf_op jit(solution)/shard_map/project/pallas_call | solution.py:211
  171.4 7.7 %collective-permute-done.8 = bf16[4,144,1152]{2,1,0:T(8,128)(2,1)} collective-permute-done((bf16[4,144,1152]{2,1,0:T(8,128)(2,1)S(1)}, bf16[4,144,1152]{2,1,0:T(8,128)(2,1)}, u32[]{:S(2)}, u32[]{:S(2)}) %collective-permute-start.8) | collective-permute-done | bytes 1327136 | tf_op jit(solution)/shard_map/ppermute | solution.py:750
  189.6 22.1 %attend.1.mixed_ref = bf16[896,1152]{1,0:T(8,128)(2,1)S(1)} custom-call(bf16[3,896,1152]{2,1,0:T(8,128)(2,1)S(1)} %copy-done.3), custom_call_target="tpu_custom_call" | custom-call | flops 22000001024 | bytes 8257536 | tf_op jit(solution)/shard_map/attend/pallas_call | solution.py:159
  217.5 9.0 %attn_out.1 = (bf16[896,1152]{1,0:T(8,128)(2,1)}, f32[896,1152]{1,0:T(8,128)}, bf16[896,1152]{1,0:T(8,128)(2,1)}) custom-call(bf16[896,1152]{1,0:T(8,128)(2,1)} %copy-done.1, bf16[896,1152]{1,0:T(8,128)(2,1)} %get-tuple-element.87.x_ref, bf16[896,16]{1,0:T(8,128)(2,1)S(1)} %bitcast.158, bf16[16,6912]{1,0:T(8,128)(2,1)S(1)} %pad.29.mod_ref, ...), custom_call_target="tpu_custom_call" | custom-call | flops 8999999488 | bytes 23252992 | tf_op jit(solution)/shard_map/attn_out/pallas_call | solution.py:211
  226.5 6.2 cotangent.1
  233.2 25.1 %fc1.1 = (bf16[896,4608]{1,0:T(8,128)(2,1)}, bf16[896,4608]{1,0:T(8,128)(2,1)}, bf16[4,1152,1152]{2,1,0:T(8,128)(2,1)}) custom-call(s32[3]{0:T(128)S(1)} %pad_add_fusion.where_ref, bf16[896,1152]{1,0:T(8,128)(2,1)} %get-tuple-element.93.x_ref.left_ref, bf16[1,4608]{1,0:T(2,128)(2,1)S(1)} %reshape_squeeze.11.bias_ref, bf16[1152,1152]{1,0:T(8,128)(2,1)} %bitcast.175, ...), custom_call_target="tpu_custom_call" | custom-call | flops 24999999488 | bytes 39822348 | tf_op jit(solution)/shard_map/fc1/pallas_call | solution.py:211
  258.3 5.7 collective-permute-done.17.rest_2_
  269.6 17.7 %fc2_terms.1 = (bf16[4,4,144,1152]{3,2,1,0:T(8,128)(2,1)}, bf16[4,4,144,1152]{3,2,1,0:T(8,128)(2,1)}) custom-call(s32[3]{0:T(128)S(1)} %pad_add_fusion.where_ref, bf16[896,4608]{1,0:T(8,128)(2,1)} %get-tuple-element.94.left_ref.post_ref, bf16[896,1152]{1,0:T(8,128)(2,1)} %get-tuple-element.100.right_ref.gmlp_ref), custom_call_target="tpu_custom_call" | custom-call | flops 17999998976 | bytes 20938764 | tf_op jit(solution)/shard_map/fc2_terms/pallas_call | solution.py:211
  297.8 44.1 %fc2.1 = (bf16[896,1152]{1,0:T(8,128)(2,1)}, bf16[896,4608]{1,0:T(8,128)(2,1)}, f32[1,4608]{1,0:T(1,128)S(1)}, f32[16,1152]{1,0:T(8,128)S(1)}) custom-call(s32[3]{0:T(128)S(1)} %pad_add_fusion.where_ref, bf16[896,4608]{1,0:T(8,128)(2,1)} %get-tuple-element.94.left_ref.post_ref, bf16[896,4608]{1,0:T(8,128)(2,1)} %get-tuple-element.95.slope_ref, ...), custom_call_target="tpu_custom_call" | custom-call | flops 44000002048 | bytes 46053388 | tf_op jit(solution)/shard_map/fc2/pallas_call | solution.py:211
  355.8 18.0 %fc1_terms.1 = (bf16[4,4,144,1152]{3,2,1,0:T(8,128)(2,1)}, bf16[4,4,144,1152]{3,2,1,0:T(8,128)(2,1)}) custom-call(s32[3]{0:T(128)S(1)} %pad_add_fusion.where_ref, bf16[896,1152]{1,0:T(8,128)(2,1)} %get-tuple-element.93.x_ref.left_ref, bf16[896,4608]{1,0:T(8,128)(2,1)} %get-tuple-element.111.right_ref.pre_ref), custom_call_target="tpu_custom_call" | custom-call | flops 17999998976 | bytes 20938764 | tf_op jit(solution)/shard_map/fc1_terms/pallas_call | solution.py:211
  377.2 31.7 %fc1_back.1 = (f32[896,1152]{1,0:T(8,128)}, bf16[896,1152]{1,0:T(8,128)(2,1)}, bf16[896,1152]{1,0:T(8,128)(2,1)}, f32[3,16,1152]{2,1,0:T(8,128)S(1)}) custom-call(bf16[896,4608]{1,0:T(8,128)(2,1)} %get-tuple-element.111.right_ref.pre_ref, bf16[4,1152,1152]{2,1,0:T(8,128)(2,1)} %get-tuple-element.112.w_ref, f32[896,1152]{1,0:T(8,128)} %get-tuple-element.102.mid_ref, ...), custom_call_target="tpu_custom_call" | custom-call | flops 32000000000 | bytes 46477312 | tf_op jit(solution)/shard_map/fc1_back/pallas_call | solution.py:211
  429.7 46.7 %attend_back.1.proj_ref = bf16[3,896,1152]{2,1,0:T(8,128)(2,1)S(1)} custom-call(bf16[3,896,1152]{2,1,0:T(8,128)(2,1)S(1)} %bitcast.166, bf16[896,1152]{1,0:T(8,128)(2,1)S(1)} %copy-done.4), custom_call_target="tpu_custom_call" | custom-call | flops 46000001024 | bytes 14450688 | tf_op jit(solution)/shard_map/attend_back/pallas_call | solution.py:176
  486.2 19.1 %attn_terms.1 = (bf16[4,4,144,1152]{3,2,1,0:T(8,128)(2,1)}, bf16[4,4,144,1152]{3,2,1,0:T(8,128)(2,1)}) custom-call(s32[3]{0:T(128)S(1)} %pad_add_fusion.where_ref, bf16[896,1152]{1,0:T(8,128)(2,1)} %get-tuple-element.123.first_ref, bf16[3,896,1152]{2,1,0:T(8,128)(2,1)} %copy-done.2, bf16[896,1152]{1,0:T(8,128)(2,1)} %copy-done.1, ...), custom_call_target="tpu_custom_call" | custom-call | flops 19000000512 | bytes 23003148 | tf_op jit(solution)/shard_map/attn_terms/pallas_call | solution.py:211
  513.2 10.7 %collective-permute-done.31 = bf16[2,144,1152]{2,1,0:T(8,128)(2,1)S(1)} collective-permute-done((bf16[2,144,1152]{2,1,0:T(8,128)(2,1)}, bf16[2,144,1152]{2,1,0:T(8,128)(2,1)S(1)}, u32[]{:S(2)}, u32[]{:S(2)}) %collective-permute-start.31) | collective-permute-done | bytes 663584 | tf_op jit(solution)/shard_map/ppermute | solution.py:750
  538.8 22.6 %project_back.1 = (bf16[896,1152]{1,0:T(8,128)(2,1)}, f32[2,16,1152]{2,1,0:T(8,128)S(1)}) custom-call(bf16[3,896,1152]{2,1,0:T(8,128)(2,1)} %copy-done.2, bf16[4,1152,1152]{2,1,0:T(8,128)(2,1)} %get-tuple-element.88.w_ref.wo_ref, bf16[896,1152]{1,0:T(8,128)(2,1)} %get-tuple-element.87.x_ref, f32[896,1152]{1,0:T(8,128)} %get-tuple-element.133.gmid_ref, ...), custom_call_target="tpu_custom_call" | custom-call | flops 23000000512 | bytes 25464832 | tf_op jit(solution)/shard_map/project_back/pallas_call | solution.py:211
  579.3 6.1 collective-permute-done.48
  632.1 7.3 %collective-permute-done.43 = bf16[144,1152]{1,0:T(8,128)(2,1)S(1)} collective-permute-done((bf16[144,1152]{1,0:T(8,128)(2,1)}, bf16[144,1152]{1,0:T(8,128)(2,1)S(1)}, u32[]{:S(2)}, u32[]{:S(2)}) %collective-permute-start.43) | collective-permute-done | bytes 331808 | tf_op jit(solution)/shard_map/ppermute | solution.py:754
  648.1 24.8 %reduce-scatter.4.cloned.1.call-done = bf16[1,144,1152]{2,1,0:T(8,128)(2,1)} async-done(((bf16[4,144,1152]{2,1,0:T(8,128)(2,1)}), bf16[1,144,1152]{2,1,0:T(8,128)(2,1)}) %reduce-scatter.4.cloned.1.call-update) | async-done | bytes 331792 | tf_op jit(solution)/shard_map/reduce_scatter | solution.py:891
  678.8 7.9 %all-to-all-done.5 = bf16[8,2,56,1152]{3,2,1,0:T(8,128)(2,1)} async-done(((bf16[8,2,56,1152]{3,2,1,0:T(8,128)(2,1)}), bf16[8,2,56,1152]{3,2,1,0:T(8,128)(2,1)}, u32[]{:S(2)}, u32[]{:S(2)}) %all-to-all-start.5) | async-done | bytes 2064416 | tf_op jit(solution)/shard_map/all_to_all | solution.py:959
  (296 shorter events, 241.6 us)
Async XLA Ops:
  7.2 61.5 %all-gather.4.cloned.1.call-start = ((), (), s32[]{:S(2)}) async-start(), calls=%async_computation.10 | async-start | bytes 2985984 | tf_op jit(solution)/shard_map/all_gather | solution.py:785
  12.8 76.1 %all-to-all-start = ((bf16[8,2,56,1152]{3,2,1,0:T(8,128)(2,1)}), bf16[8,2,56,1152]{3,2,1,0:T(8,128)(2,1)}, u32[]{:S(2)}, u32[]{:S(2)}) async-start(bf16[8,2,56,1152]{3,2,1,0:T(8,128)(2,1)} %bitcast.168), calls=%async_computation | async-start | bytes 4128768 | tf_op jit(solution)/shard_map/all_to_all | solution.py:955
  19.1 127.2 %all-gather.6.cloned.1.call-start = ((), (), s32[]{:S(2)}) async-start(), calls=%async_computation.11 | async-start | bytes 2985984 | tf_op jit(solution)/shard_map/all_gather | solution.py:785
  114.3 36.4 %collective-permute-start.4 = (bf16[4,144,1152]{2,1,0:T(8,128)(2,1)}, bf16[4,144,1152]{2,1,0:T(8,128)(2,1)}, u32[]{:S(2)}, u32[]{:S(2)}) collective-permute-start(bf16[4,144,1152]{2,1,0:T(8,128)(2,1)} %collective-permute-done), channel_id=1, source_target_pairs={{0,1},{1,0},{2,3},{3,2},{4,5},{5,4},{6,7},{7,6},{8,9},{9,8},{10,11... | collective-permute-start | bytes 3981320 | tf_op jit(solution)/shard_map/ppermute | solution.py:759
  122.4 90.6 %all-gather.8.cloned.1.call-start = ((), (), s32[]{:S(2)}) async-start(), calls=%async_computation.12 | async-start | bytes 2985984 | tf_op jit(solution)/shard_map/all_gather | solution.py:785
  138.3 88.1 %all-to-all-start.2 = ((bf16[8,2,56,1152]{3,2,1,0:T(8,128)(2,1)}), bf16[8,2,56,1152]{3,2,1,0:T(8,128)(2,1)}, u32[]{:S(2)}, u32[]{:S(2)}) async-start(bf16[8,2,56,1152]{3,2,1,0:T(8,128)(2,1)} %bitcast.167), calls=%async_computation.2 | async-start | bytes 4128768 | tf_op jit(solution)/shard_map/all_to_all | solution.py:955
  182.3 50.9 %collective-permute-start.12 = (bf16[4,144,1152]{2,1,0:T(8,128)(2,1)}, bf16[4,144,1152]{2,1,0:T(8,128)(2,1)}, u32[]{:S(2)}, u32[]{:S(2)}) collective-permute-start(bf16[4,144,1152]{2,1,0:T(8,128)(2,1)} %collective-permute-done.8), channel_id=1, source_target_pairs={{0,1},{1,0},{2,3},{3,2},{4,5},{5,4},{6,7},{7,6},{8,9},{9,8},{10,11... | collective-permute-start | bytes 3981320 | tf_op jit(solution)/shard_map/ppermute | solution.py:759
  184.3 48.9 %collective-permute-start.13 = (bf16[4,144,1152]{2,1,0:T(8,128)(2,1)}, bf16[4,144,1152]{2,1,0:T(8,128)(2,1)}, u32[]{:S(2)}, u32[]{:S(2)}) collective-permute-start(bf16[4,144,1152]{2,1,0:T(8,128)(2,1)} %collective-permute-done.9), channel_id=1, source_target_pairs={{0,1},{1,0},{2,3},{3,2},{4,5},{5,4},{6,7},{7,6},{8,9},{9,8},{10,11... | collective-permute-start | bytes 3981320 | tf_op jit(solution)/shard_map/ppermute | solution.py:759
  215.5 42.8 %collective-permute-start.16 = (bf16[4,144,1152]{2,1,0:T(8,128)(2,1)}, bf16[4,144,1152]{2,1,0:T(8,128)(2,1)}, u32[]{:S(2)}, u32[]{:S(2)}) collective-permute-start(bf16[4,144,1152]{2,1,0:T(8,128)(2,1)} %constant_dynamic-slice_fusion.4), channel_id=1, source_target_pairs={{0,8},{8,0},{16,24},{24,16},{1,9},{9,1},{17,25},{25,17},{2,10},{10... | collective-permute-start | bytes 3981320 | tf_op jit(solution)/shard_map/ppermute | solution.py:750
  287.3 59.0 %collective-permute-start.24 = (bf16[4,4,144,1152]{3,2,1,0:T(8,128)(2,1)}, bf16[4,4,144,1152]{3,2,1,0:T(8,128)(2,1)}, u32[]{:S(2)}, u32[]{:S(2)}) collective-permute-start(bf16[4,4,144,1152]{3,2,1,0:T(8,128)(2,1)} %get-tuple-element.99), channel_id=1, source_target_pairs={{0,1},{1,0},{2,3},{3,2},{4,5},{5,4},{6,7},{7,6},{8,9},{9,8},{10,11... | collective-permute-start | bytes 15925256 | tf_op jit(solution)/shard_map/ppermute | solution.py:759
  341.9 66.9 %all-to-all-start.3 = ((bf16[8,2,56,1152]{3,2,1,0:T(8,128)(2,1)}), bf16[8,2,56,1152]{3,2,1,0:T(8,128)(2,1)}, u32[]{:S(2)}, u32[]{:S(2)}) async-start(bf16[8,2,56,1152]{3,2,1,0:T(8,128)(2,1)} %bitcast.173), calls=%async_computation.3 | async-start | bytes 4128768 | tf_op jit(solution)/shard_map/all_to_all | solution.py:959
  346.3 221.1 %reduce-scatter.8.cloned.1.call-start = ((), (), s32[]{:S(2)}) async-start(), calls=%async_computation.15 | async-start | bytes 1658880 | tf_op jit(solution)/shard_map/reduce_scatter | solution.py:891
  373.9 44.7 %collective-permute-start.27 = (bf16[4,4,144,1152]{3,2,1,0:T(8,128)(2,1)}, bf16[4,4,144,1152]{3,2,1,0:T(8,128)(2,1)}, u32[]{:S(2)}, u32[]{:S(2)}) collective-permute-start(bf16[4,4,144,1152]{3,2,1,0:T(8,128)(2,1)} %get-tuple-element.110), channel_id=1, source_target_pairs={{0,1},{1,0},{2,3},{3,2},{4,5},{5,4},{6,7},{7,6},{8,9},{9,8},{10,11... | collective-permute-start | bytes 15925256 | tf_op jit(solution)/shard_map/ppermute | solution.py:759
  374.2 40.7 %collective-permute-start.26 = (bf16[2,2,144,1152]{3,2,1,0:T(8,128)(2,1)}, bf16[2,2,144,1152]{3,2,1,0:T(8,128)(2,1)}, u32[]{:S(2)}, u32[]{:S(2)}) collective-permute-start(bf16[2,2,144,1152]{3,2,1,0:T(8,128)(2,1)} %pad_maximum_fusion.2), channel_id=1, source_target_pairs={{0,16},{16,0},{8,24},{24,8},{1,17},{17,1},{9,25},{25,9},{2,18},{18... | collective-permute-start | bytes 3981320 | tf_op jit(solution)/shard_map/ppermute | solution.py:754
  375.7 39.2 %collective-permute-start.25 = (bf16[2,2,144,1152]{3,2,1,0:T(8,128)(2,1)}, bf16[2,2,144,1152]{3,2,1,0:T(8,128)(2,1)}, u32[]{:S(2)}, u32[]{:S(2)}) collective-permute-start(bf16[2,2,144,1152]{3,2,1,0:T(8,128)(2,1)} %pad_maximum_fusion.1), channel_id=1, source_target_pairs={{0,8},{8,0},{16,24},{24,16},{1,9},{9,1},{17,25},{25,17},{2,10},{10... | collective-permute-start | bytes 3981320 | tf_op jit(solution)/shard_map/ppermute | solution.py:750
  416.2 62.8 %collective-permute-start.33 = (bf16[2,144,1152]{2,1,0:T(8,128)(2,1)S(1)}, bf16[2,144,1152]{2,1,0:T(8,128)(2,1)S(1)}, u32[]{:S(2)}, u32[]{:S(2)}) collective-permute-start(bf16[2,144,1152]{2,1,0:T(8,128)(2,1)S(1)} %bitcast_add_fusion.10), channel_id=1, source_target_pairs={{0,8},{8,0},{16,24},{24,16},{1,9},{9,1},{17,25},{25,17},{2,10},{10... | collective-permute-start | bytes 1990664 | tf_op jit(solution)/shard_map/ppermute | solution.py:750
  418.0 61.0 %collective-permute-start.32 = (bf16[2,144,1152]{2,1,0:T(8,128)(2,1)S(1)}, bf16[2,144,1152]{2,1,0:T(8,128)(2,1)S(1)}, u32[]{:S(2)}, u32[]{:S(2)}) collective-permute-start(bf16[2,144,1152]{2,1,0:T(8,128)(2,1)S(1)} %bitcast_add_fusion.11), channel_id=1, source_target_pairs={{0,16},{16,0},{8,24},{24,8},{1,17},{17,1},{9,25},{25,9},{2,18},{18... | collective-permute-start | bytes 1990664 | tf_op jit(solution)/shard_map/ppermute | solution.py:754
  424.0 57.8 %collective-permute-start.29 = (bf16[2,2,144,1152]{3,2,1,0:T(8,128)(2,1)}, bf16[2,2,144,1152]{3,2,1,0:T(8,128)(2,1)}, u32[]{:S(2)}, u32[]{:S(2)}) collective-permute-start(bf16[2,2,144,1152]{3,2,1,0:T(8,128)(2,1)} %pad_maximum_fusion.4), channel_id=1, source_target_pairs={{0,16},{16,0},{8,24},{24,8},{1,17},{17,1},{9,25},{25,9},{2,18},{18... | collective-permute-start | bytes 3981320 | tf_op jit(solution)/shard_map/ppermute | solution.py:754
  428.2 53.7 %collective-permute-start.28 = (bf16[2,2,144,1152]{3,2,1,0:T(8,128)(2,1)}, bf16[2,2,144,1152]{3,2,1,0:T(8,128)(2,1)}, u32[]{:S(2)}, u32[]{:S(2)}) collective-permute-start(bf16[2,2,144,1152]{3,2,1,0:T(8,128)(2,1)} %pad_maximum_fusion.3), channel_id=1, source_target_pairs={{0,8},{8,0},{16,24},{24,16},{1,9},{9,1},{17,25},{25,17},{2,10},{10... | collective-permute-start | bytes 3981320 | tf_op jit(solution)/shard_map/ppermute | solution.py:750
  534.0 54.4 %collective-permute-start.36 = (bf16[2,2,144,1152]{3,2,1,0:T(8,128)(2,1)}, bf16[2,2,144,1152]{3,2,1,0:T(8,128)(2,1)}, u32[]{:S(2)}, u32[]{:S(2)}) collective-permute-start(bf16[2,2,144,1152]{3,2,1,0:T(8,128)(2,1)} %pad_maximum_fusion.8), channel_id=1, source_target_pairs={{0,16},{16,0},{8,24},{24,8},{1,17},{17,1},{9,25},{25,9},{2,18},{18... | collective-permute-start | bytes 3981320 | tf_op jit(solution)/shard_map/ppermute | solution.py:754
  537.7 50.7 %collective-permute-start.35 = (bf16[2,2,144,1152]{3,2,1,0:T(8,128)(2,1)}, bf16[2,2,144,1152]{3,2,1,0:T(8,128)(2,1)}, u32[]{:S(2)}, u32[]{:S(2)}) collective-permute-start(bf16[2,2,144,1152]{3,2,1,0:T(8,128)(2,1)} %pad_maximum_fusion.7), channel_id=1, source_target_pairs={{0,8},{8,0},{16,24},{24,16},{1,9},{9,1},{17,25},{25,17},{2,10},{10... | collective-permute-start | bytes 3981320 | tf_op jit(solution)/shard_map/ppermute | solution.py:750
  567.3 53.9 %reduce-scatter.6.cloned.1.call-start = ((), (), s32[]{:S(2)}) async-start(), calls=%async_computation.14 | async-start | bytes 1658880 | tf_op jit(solution)/shard_map/reduce_scatter | solution.py:891
  612.5 74.2 %all-to-all-start.5 = ((bf16[8,2,56,1152]{3,2,1,0:T(8,128)(2,1)}), bf16[8,2,56,1152]{3,2,1,0:T(8,128)(2,1)}, u32[]{:S(2)}, u32[]{:S(2)}) async-start(bf16[8,2,56,1152]{3,2,1,0:T(8,128)(2,1)} %bitcast.172), calls=%async_computation.5 | async-start | bytes 4128768 | tf_op jit(solution)/shard_map/all_to_all | solution.py:959
  616.8 56.0 %reduce-scatter.4.cloned.1.call-start = ((), (), s32[]{:S(2)}) async-start(), calls=%async_computation.13 | async-start | bytes 1658880 | tf_op jit(solution)/shard_map/reduce_scatter | solution.py:891
  (74 other events, 1305.3 us)
Sparse Core Ops, SparseCore 0:
  10.3 58.3 all-gather.3
  104.8 41.4 all-gather.5
  148.5 60.9 all-gather.7
  506.4 31.4 reduce-scatter.7
  571.1 31.9 reduce-scatter.5
  620.2 52.5 reduce-scatter.3

commit v2 on v1

--- a/solution.py
+++ b/solution.py
@@ -74,33 +74,46 @@
     return jnp.concatenate([totals[lane] for lane in sorted(totals)], axis=1)
 
 
-def same_position(rows, frames):
-    left = lax.broadcasted_iota(jnp.int32, (rows, rows), 0) // frames
-    right = lax.broadcasted_iota(jnp.int32, (rows, rows), 1) // frames
-    return left == right
-
-
-def head_probs(queries, keys, inside, scale):
-    scores = lax.dot_general(queries, keys, COL_DIMS, preferred_element_type=jnp.float32) * scale
-    scores = jnp.where(inside, scores, -1e30)
-    weights = jnp.exp(scores - jnp.max(scores, axis=1, keepdims=True))
-    return weights / jnp.sum(weights, axis=1, keepdims=True)
+class Spots:
+    def __init__(self, rows, frames):
+        self.frames = frames
+        spot = lax.broadcasted_iota(jnp.int32, (frames, rows), 1) // frames
+        self.own = [spot == at for at in range(rows // frames)]
+        self.masks = [own.astype(jnp.float32).astype(jnp.bfloat16) for own in self.own]
+
+    def compact(self, full):
+        found = full[: self.frames]
+        for at, own in enumerate(self.own[1:], 1):
+            found = jnp.where(own, full[at * self.frames : (at + 1) * self.frames], found)
+        return found
+
+    def expand(self, compact):
+        return jnp.concatenate([compact * mask for mask in self.masks], axis=0)
+
+    def probs(self, queries, keys, scale):
+        scores = lax.dot_general(keys, queries, COL_DIMS, preferred_element_type=jnp.float32)
+        scores = self.compact(scores) * scale
+        weights = jnp.exp(scores - jnp.max(scores, axis=0, keepdims=True))
+        return weights / jnp.sum(weights, axis=0, keepdims=True)
 
 
 def attend_kernel(frames, scale, proj_ref, mixed_ref):
     rows, width = mixed_ref.shape
-    inside = same_position(rows, frames)
+    spots = Spots(rows, frames)
     totals = {}
     for window in head_windows(HEADS, width // HEADS):
-        cols = slice(window[0], window[1])
+        query, key, value = [
+            slice(part * width + window[0], part * width + window[1]) for part in range(3)
+        ]
         mask = lane_mask(window)
-        prob = head_probs(proj_ref[0, :, cols] * mask, proj_ref[1, :, cols], inside, scale)
+        prob = spots.probs(proj_ref[:, query] * mask, proj_ref[:, key], scale)
         add_window(
             totals,
             window,
-            jnp.dot(
-                prob.astype(jnp.bfloat16),
-                proj_ref[2, :, cols] * mask,
+            lax.dot_general(
+                spots.expand(prob.astype(jnp.bfloat16)),
+                proj_ref[:, value] * mask,
+                ROW_DIMS,
                 preferred_element_type=jnp.float32,
             ),
         )
@@ -109,41 +122,42 @@
 
 def attend_back_kernel(frames, scale, proj_ref, grad_ref, out_ref):
     rows, width = grad_ref.shape
-    inside = same_position(rows, frames)
+    spots = Spots(rows, frames)
     to_query, to_key, to_value = {}, {}, {}
     for window in head_windows(HEADS, width // HEADS):
-        cols = slice(window[0], window[1])
+        query, key, value = [
+            slice(part * width + window[0], part * width + window[1]) for part in range(3)
+        ]
         mask = lane_mask(window)
-        queries = proj_ref[0, :, cols] * mask
-        keys = proj_ref[1, :, cols]
-        grads = grad_ref[:, cols] * mask
-        prob = head_probs(queries, keys, inside, scale)
-        grad_prob = lax.dot_general(
-            grads, proj_ref[2, :, cols], COL_DIMS, preferred_element_type=jnp.float32
+        queries = proj_ref[:, query] * mask
+        keys = proj_ref[:, key]
+        grads = grad_ref[:, window[0] : window[1]] * mask
+        prob = spots.probs(queries, keys, scale)
+        grad_prob = spots.compact(
+            lax.dot_general(
+                proj_ref[:, value], grads, COL_DIMS, preferred_element_type=jnp.float32
+            )
         )
         weighted = prob * grad_prob
-        grad_scores = weighted - prob * jnp.sum(weighted, axis=1, keepdims=True)
-        grad_scores = grad_scores.astype(jnp.bfloat16)
+        grad_scores = weighted - prob * jnp.sum(weighted, axis=0, keepdims=True)
+        grad_scores = spots.expand(grad_scores.astype(jnp.bfloat16))
+        prob_low = spots.expand(prob.astype(jnp.bfloat16))
         add_window(
-            to_value,
-            window,
-            lax.dot_general(
-                prob.astype(jnp.bfloat16), grads, ROW_DIMS, preferred_element_type=jnp.float32
-            ),
+            to_value, window, jnp.dot(prob_low, grads, preferred_element_type=jnp.float32)
+        )
+        add_window(
+            to_key, window, jnp.dot(grad_scores, queries, preferred_element_type=jnp.float32)
         )
         add_window(
             to_query,
             window,
-            jnp.dot(grad_scores, keys * mask, preferred_element_type=jnp.float32),
+            lax.dot_general(
+                grad_scores, keys * mask, ROW_DIMS, preferred_element_type=jnp.float32
+            ),
         )
-        add_window(
-            to_key,
-            window,
-            lax.dot_general(grad_scores, queries, ROW_DIMS, preferred_element_type=jnp.float32),
-        )
-    out_ref[0] = (joined(to_query) * scale).astype(jnp.bfloat16)
-    out_ref[1] = (joined(to_key) * scale).astype(jnp.bfloat16)
-    out_ref[2] = joined(to_value).astype(jnp.bfloat16)
+    out_ref[:, :width] = (joined(to_query) * scale).astype(jnp.bfloat16)
+    out_ref[:, width : 2 * width] = (joined(to_key) * scale).astype(jnp.bfloat16)
+    out_ref[:, 2 * width :] = joined(to_value).astype(jnp.bfloat16)
 
 
 def tile_rows(positions, frames):
@@ -154,43 +168,43 @@
 
 
 def attend(projected, positions, frames, scale):
-    _, rows, width = projected.shape
+    rows, width = projected.shape[0], projected.shape[1] // 3
     tile = tile_rows(positions, frames)
     return pl.pallas_call(
         lambda *refs: attend_kernel(frames, scale, *refs),
         out_shape=jax.ShapeDtypeStruct((rows, width), jnp.bfloat16),
         grid=(rows // tile,),
-        in_specs=[pl.BlockSpec((3, tile, width), lambda step: (0, step, 0))],
+        in_specs=[pl.BlockSpec((tile, 3 * width), lambda step: (step, 0))],
         out_specs=pl.BlockSpec((tile, width), lambda step: (step, 0)),
         cost_estimate=pl.CostEstimate(
-            flops=22 * 10**9, bytes_accessed=8 * rows * width, transcendentals=0
+            flops=13 * 10**9, bytes_accessed=8 * rows * width, transcendentals=0
         ),
-        compiler_params=pltpu.CompilerParams(vmem_limit_bytes=40 << 20),
+        compiler_params=pltpu.CompilerParams(vmem_limit_bytes=VMEM_LIMIT),
         name="attend",
     )(projected)
 
 
 def attend_back(projected, grad_mixed, positions, frames, scale):
-    _, rows, width = projected.shape
+    rows, width = projected.shape[0], projected.shape[1] // 3
     tile = tile_rows(positions, frames)
     return pl.pallas_call(
         lambda *refs: attend_back_kernel(frames, scale, *refs),
-        out_shape=jax.ShapeDtypeStruct((3, rows, width), jnp.bfloat16),
+        out_shape=jax.ShapeDtypeStruct((rows, 3 * width), jnp.bfloat16),
         grid=(rows // tile,),
         in_specs=[
-            pl.BlockSpec((3, tile, width), lambda step: (0, step, 0)),
+            pl.BlockSpec((tile, 3 * width), lambda step: (step, 0)),
             pl.BlockSpec((tile, width), lambda step: (step, 0)),
         ],
-        out_specs=pl.BlockSpec((3, tile, width), lambda step: (0, step, 0)),
+        out_specs=pl.BlockSpec((tile, 3 * width), lambda step: (step, 0)),
         cost_estimate=pl.CostEstimate(
-            flops=46 * 10**9, bytes_accessed=14 * rows * width, transcendentals=0
+            flops=27 * 10**9, bytes_accessed=14 * rows * width, transcendentals=0
         ),
-        compiler_params=pltpu.CompilerParams(vmem_limit_bytes=40 << 20),
+        compiler_params=pltpu.CompilerParams(vmem_limit_bytes=VMEM_LIMIT),
         name="attend_back",
     )(projected, grad_mixed)
 
 
-VMEM_LIMIT = 52 << 20
+VMEM_LIMIT = 58 << 20
 BF16, F32 = jnp.bfloat16, jnp.float32
 
 
@@ -234,22 +248,35 @@
 
 
 class Pieces:
-    def __init__(self, arrays, places, shape, slot_first):
-        self.arrays, self.places, self.shape, self.slot_first = arrays, places, shape, slot_first
+    def __init__(self, arrays, places, shape, by_columns):
+        self.arrays, self.places, self.shape, self.by_columns = arrays, places, shape, by_columns
 
     def start(self, where_ref, refs, full, sems):
         for ref, place in zip(refs, self.places):
             slot, first, count = place(where_ref[0], where_ref[1])
-            span = pl.ds(first, count)
-            target = full.at[slot, span] if self.slot_first else full.at[span, slot]
-            pltpu.make_async_copy(ref, target, sems.at[slot]).start()
-
-    def wait(self, slot, full, sems):
-        part = full.at[slot] if self.slot_first else full.at[:, slot]
-        pltpu.make_async_copy(part, part, sems.at[slot]).wait()
+            if self.by_columns:
+                width = self.shape[2] // 2
+                column = pl.multiple_of(slot % 2 * width, width)
+                target = full.at[slot // 2, pl.ds(first, count), pl.ds(column, width)]
+                pltpu.make_async_copy(ref, target, sems.at[slot // 2]).start()
+                continue
+            half = self.shape[0] // 2
+            for turn in range(count):
+                target = full.at[first + turn, slot]
+                pltpu.make_async_copy(ref.at[turn], target, sems.at[(first + turn) // half]).start()
+
+    def part(self, full, half):
+        if self.by_columns:
+            return full.at[half]
+        turns = self.shape[0] // 2
+        return full.at[half * turns : (half + 1) * turns]
+
+    def wait(self, half, full, sems):
+        part = self.part(full, half)
+        pltpu.make_async_copy(part, part, sems.at[half]).wait()
 
     def scratch(self):
-        return [pltpu.VMEM(self.shape, BF16), pltpu.SemaphoreType.DMA((5,))]
+        return [pltpu.VMEM(self.shape, BF16), pltpu.SemaphoreType.DMA((3,))]
 
 
 def norm_parts(values):
@@ -264,6 +291,14 @@
     return (grad - mean_grad - normed * mean_both) * inverse
 
 
+def gather_order(first, count, frames, positions, own_frames, chunk):
+    at = first + lax.broadcasted_iota(jnp.int32, (count, frames // own_frames * chunk), 0)
+    source = lax.broadcasted_iota(jnp.int32, (count, frames // own_frames * chunk), 1)
+    frame, position = at % frames, at // frames
+    wanted = frame // own_frames * chunk + frame % own_frames * positions + position
+    return (source == wanted).astype(F32).astype(BF16)
+
+
 def row_order(rows, first, count, inner, outer):
     at = first + lax.broadcasted_iota(jnp.int32, (count, rows), 0)
     source = lax.broadcasted_iota(jnp.int32, (count, rows), 1)
@@ -276,6 +311,12 @@
     return dot(hot, high, ROW_DIMS) + dot(hot, low, ROW_DIMS)
 
 
+def first_step(step, action):
+    @pl.when(step == 0)
+    def _():
+        action()
+
+
 def add_into(ref, index, value):
     @pl.when(pl.program_id(0) == 0)
     def _():
@@ -284,8 +325,9 @@
     ref[index] += value
 
 
-def qkv_call(where, arrived, hot, mod, pieces, positions, frames):
-    rows, width = arrived.shape
+def qkv_call(where, arrived, hot, mod, pieces, positions, frames, own_frames):
+    rows, width = positions * frames, arrived.shape[1]
+    chunk = arrived.shape[0] * own_frames // frames
     tile = row_tile(rows)
     steps = rows // tile
     count = len(pieces.arrays)
@@ -299,7 +341,7 @@
         def _():
             pieces.start(where_ref, piece_refs, full, sems)
 
-        order = row_order(rows, step * tile, tile, positions, frames)
+        order = gather_order(step * tile, tile, frames, positions, own_frames, chunk)
         inputs = dot(order, x_ref[...])
         x_out[...] = inputs.astype(BF16)
         normed, _ = norm_parts(inputs)
@@ -307,16 +349,12 @@
         scale = dot(hot_ref[...], mod_ref[:, width : 2 * width])
         first = (normed * (1.0 + scale) + shift).astype(BF16)
         first_out[...] = first
-        back = pltpu.make_async_copy(full, full_out, sems.at[4])
-
-        @pl.when(step == 0)
-        def _():
-            for slot in range(4):
-                pieces.wait(slot, full, sems)
-            back.start()
-
-        for slot in range(3):
-            proj_out[slot] = dot(first, full[slot]).astype(BF16)
+        back = pltpu.make_async_copy(full, full_out, sems.at[2])
+        first_step(step, lambda: pieces.wait(0, full, sems))
+        proj_out[:, : 2 * width] = dot(first, full[0]).astype(BF16)
+        first_step(step, lambda: pieces.wait(1, full, sems))
+        first_step(step, back.start)
+        proj_out[:, 2 * width :] = dot(first, full[1, :, :width]).astype(BF16)
 
         @pl.when(step == steps - 1)
         def _():
@@ -336,7 +374,7 @@
         [
             ((rows, width), BF16, tiled(tile, width)),
             ((rows, width), BF16, tiled(tile, width)),
-            ((3, rows, width), BF16, pl.BlockSpec((3, tile, width), lambda step: (0, step, 0))),
+            ((rows, 3 * width), BF16, tiled(tile, 3 * width)),
             (pieces.shape, BF16, HBM),
         ],
         pieces.scratch(),
@@ -368,7 +406,7 @@
             (x_rows, tiled(tile, width)),
             (hot, tiled(tile, hot.shape[1])),
             (mod, whole(mod)),
-            (full_attn, pl.BlockSpec((1, width, width), lambda step: (3, 0, 0))),
+            (full_attn, pl.BlockSpec((1, width, width), lambda step: (1, 0, 1))),
         ],
         [
             ((rows, width), BF16, tiled(tile, width)),
@@ -394,18 +432,14 @@
         piece_refs, rest = rest[:count], rest[count:]
         post_out, slope_out, full_out, full, sems = rest
         step = pl.program_id(0)
-        back = pltpu.make_async_copy(full, full_out, sems.at[4])
-
-        @pl.when(step == 0)
-        def _():
-            pieces.start(where_ref, piece_refs, full, sems)
-            for slot in range(4):
-                pieces.wait(slot, full, sems)
-            back.start()
-
-        for slot in range(4):
-            cols = slice(slot * part, (slot + 1) * part)
-            pre = dot(x_ref[...], full[slot]) + bias_ref[:, cols].astype(F32)
+        back = pltpu.make_async_copy(full, full_out, sems.at[2])
+        first_step(step, lambda: pieces.start(where_ref, piece_refs, full, sems))
+        for half in range(2):
+            first_step(step, lambda half=half: pieces.wait(half, full, sems))
+            if half:
+                first_step(step, back.start)
+            cols = slice(half * part, (half + 1) * part)
+            pre = dot(x_ref[...], full[half]) + bias_ref[:, cols].astype(F32)
             square = pre * pre
             curve = jnp.tanh(pre * (GELU_A + GELU_B * square))
             half = 0.5 + 0.5 * curve
@@ -428,8 +462,8 @@
             *[(array, HBM) for array in pieces.arrays],
         ],
         [
-            ((rows, 4 * part), BF16, tiled(tile, 4 * part)),
-            ((rows, 4 * part), BF16, tiled(tile, 4 * part)),
+            ((rows, 2 * part), BF16, tiled(tile, 2 * part)),
+            ((rows, 2 * part), BF16, tiled(tile, 2 * part)),
             (pieces.shape, BF16, HBM),
         ],
         pieces.scratch(),
@@ -437,12 +471,13 @@
     )
 
 
-def cot_call(arrived, hot, mod, positions, frames):
+def cot_call(arrived, hot, mod, positions, frames, own_frames):
     rows, width = arrived.shape
     tile = row_tile(rows)
 
     def kernel(cot_ref, hot_ref, mod_ref, rows_out, mlp_out):
-        order = row_order(rows, pl.program_id(0) * tile, tile, positions, frames)
+        first = pl.program_id(0) * tile
+        order = gather_order(first, tile, frames, positions, own_frames, own_frames * positions)
         hot = hot_ref[...]
         valid = jnp.sum(hot.astype(F32), axis=1, keepdims=True)
         grad = dot(order, cot_ref[...]) * valid
@@ -473,24 +508,19 @@
     steps = rows // tile
     count = len(pieces.arrays)
     clips = hot.shape[1]
-    turns = pieces.shape[0] // 4
-    part = hidden // 4
+    part = hidden // 2
 
     def kernel(where_ref, post_ref, slope_ref, gmlp_ref, grows_ref, mid_ref, hot_ref, mod_ref, *rest):
         piece_refs, rest = rest[:count], rest[count:]
         block_out, pre_out, bias_out, gate_out, full, sems, held = rest
         step = pl.program_id(0)
 
-        @pl.when(step == 0)
-        def _():
-            pieces.start(where_ref, piece_refs, full, sems)
-            for slot in range(4):
-                pieces.wait(slot, full, sems)
-
+        first_step(step, lambda: pieces.start(where_ref, piece_refs, full, sems))
         total = None
-        for at in range(4):
-            cols = slice(at * part, (at + 1) * part)
-            weight = full[at * turns : (at + 1) * turns].reshape(part, width)
+        for half in range(2):
+            first_step(step, lambda half=half: pieces.wait(half, full, sems))
+            cols = slice(half * part, (half + 1) * part)
+            weight = pieces.part(full, half)[...].reshape(part, width)
             term = dot(post_ref[:, cols], weight)
             total = term if total is None else total + term
             grad_pre = (dot(gmlp_ref[...], weight, COL_DIMS) * slope_ref[:, cols].astype(F32)).astype(BF16)
@@ -544,13 +574,19 @@
     width = middle.shape[1]
     tile = row_tile(rows)
     clips = hot.shape[1]
-    part = hidden // 4
+    part = hidden // 2
 
     def kernel(pre_ref, w_ref, mid_ref, attn_ref, grows_ref, hot_ref, mod_ref, wo_ref, *outs):
-        gmid_out, gattn_out, gmix_out, sums_out = outs
+        gmid_out, gattn_out, gmix_out, sums_out, held, sems = outs
+        step = pl.program_id(0)
+        loads = [pltpu.make_async_copy(w_ref.at[at], held.at[at], sems.at[at]) for at in range(2)]
         grad = None
-        for at in range(4):
-            term = dot(pre_ref[:, at * part : (at + 1) * part], w_ref[at], COL_DIMS)
+        for at in range(2):
+            if not at:
+                first_step(step, loads[0].start)
+                first_step(step, loads[1].start)
+            first_step(step, loads[at].wait)
+            term = dot(pre_ref[:, at * part : (at + 1) * part], held[at], COL_DIMS)
             grad = term if grad is None else grad + term
         hot = hot_ref[...]
         scale = dot(hot, mod_ref[:, 4 * width : 5 * width])
@@ -571,13 +607,13 @@
         (rows // tile,),
         [
             (grad_pre, tiled(tile, hidden)),
-            (full_fc1, whole(full_fc1)),
+            (full_fc1, HBM),
             (middle, tiled(tile, width)),
             (attn_out, tiled(tile, width)),
             (grad_rows, tiled(tile, width)),
             (hot, tiled(tile, clips)),
             (mod, whole(mod)),
-            (full_attn, pl.BlockSpec((1, width, width), lambda step: (3, 0, 0))),
+            (full_attn, pl.BlockSpec((1, width, width), lambda step: (1, 0, 1))),
         ],
         [
             ((rows, width), F32, tiled(tile, width)),
@@ -585,22 +621,31 @@
             ((rows, width), BF16, tiled(tile, width)),
             ((3, clips, width), F32, pl.BlockSpec((3, clips, width), lambda step: (0, 0, 0))),
         ],
+        [pltpu.VMEM(full_fc1.shape, BF16), pltpu.SemaphoreType.DMA((2,))],
         flops=32 * 10**9,
     )
 
 
 def qkv_back_call(grad_proj, full_attn, x_rows, grad_middle, hot, mod, positions, frames):
-    _, rows, width = grad_proj.shape
+    rows, width = x_rows.shape
     tile = row_tile(rows)
     steps = rows // tile
     clips = hot.shape[1]
 
-    def kernel(proj_ref, w_ref, x_ref, gmid_ref, hot_ref, mod_ref, tok_out, sums_out, held):
+    def kernel(proj_ref, w_ref, x_ref, gmid_ref, hot_ref, mod_ref, tok_out, sums_out, held, w_held, sems):
         step = pl.program_id(0)
-        grad = None
-        for at in range(3):
-            term = dot(proj_ref[at], w_ref[at], COL_DIMS)
-            grad = term if grad is None else grad + term
+        loads = [
+            pltpu.make_async_copy(w_ref.at[0], w_held.at[0], sems.at[0]),
+            pltpu.make_async_copy(
+                w_ref.at[1, :, :width], w_held.at[1, :, :width], sems.at[1]
+            ),
+        ]
+        first_step(step, loads[0].start)
+        first_step(step, loads[1].start)
+        first_step(step, loads[0].wait)
+        grad = dot(proj_ref[:, : 2 * width], w_held[0], COL_DIMS)
+        first_step(step, loads[1].wait)
+        grad += dot(proj_ref[:, 2 * width :], w_held[1, :, :width], COL_DIMS)
         hot = hot_ref[...]
         scale = dot(hot, mod_ref[:, width : 2 * width])
         normed, inverse = norm_parts(x_ref[...].astype(F32))
@@ -620,8 +665,8 @@
         "project_back",
         (steps,),
         [
-            (grad_proj, pl.BlockSpec((3, tile, width), lambda step: (0, step, 0))),
-            (full_attn, pl.BlockSpec((3, width, width), lambda step: (0, 0, 0))),
+            (grad_proj, tiled(tile, 3 * width)),
+            (full_attn, HBM),
             (x_rows, tiled(tile, width)),
             (grad_middle, tiled(tile, width)),
             (hot, tiled(tile, clips)),
@@ -631,12 +676,16 @@
             ((rows, width), BF16, pl.BlockSpec((rows, width), lambda step: (0, 0))),
             ((2, clips, width), F32, pl.BlockSpec((2, clips, width), lambda step: (0, 0, 0))),
         ],
-        [pltpu.VMEM((rows, width), BF16)],
+        [
+            pltpu.VMEM((rows, width), BF16),
+            pltpu.VMEM(full_attn.shape, BF16),
+            pltpu.SemaphoreType.DMA((2,)),
+        ],
         flops=23 * 10**9,
     )
 
 
-def split_store(product, where_ref, keep_out, give_out, rows, slot_first):
+def split_store(product, where_ref, keep_out, give_out, rows, slot_first, slot=0):
     units = product.shape[0] // rows
     for core in range(2):
 
@@ -647,14 +696,14 @@
                 side = unit % 2 if slot_first else unit // 4
                 out = keep_out if side == core else give_out
                 if slot_first:
-                    out[0, unit // 2] = piece
+                    out[slot, unit // 2] = piece
                 else:
                     out[unit % 4, 0] = piece
 
 
-def terms_out(chips, rows, width, slot_first):
+def terms_out(chips, rows, width, slot_first, slots=1):
     if slot_first:
-        spec = pl.BlockSpec((1, chips, rows, width), lambda step: (step, 0, 0, 0))
+        spec = pl.BlockSpec((slots, chips, rows, width), lambda step: (step, 0, 0, 0))
     else:
         spec = pl.BlockSpec((4, 1, rows, width), lambda step: (0, step, 0, 0))
     return [((4, chips, rows, width), BF16, spec)] * 2
@@ -690,18 +739,20 @@
 
     def kernel(where_ref, left_ref, right_ref, keep_out, give_out):
         product = dot(left_ref[...], right_ref[...], ROW_DIMS).astype(BF16)
-        split_store(product, where_ref, keep_out, give_out, rows, True)
+        for slot in range(2):
+            piece = product[:, slot * part : (slot + 1) * part]
+            split_store(piece, where_ref, keep_out, give_out, rows, True, slot)
 
     return call(
         kernel,
         "fc1_terms",
-        (4,),
+        (2,),
         [
             (where, SCALARS),
             (second_in, whole(second_in)),
-            (grad_pre, pl.BlockSpec((count, part), lambda step: (0, step))),
-        ],
-        terms_out(chips, rows, part, True),
+            (grad_pre, pl.BlockSpec((count, 2 * part), lambda step: (0, step))),
+        ],
+        terms_out(chips, rows, part, True, 2),
         flops=18 * 10**9,
     )
 
@@ -715,7 +766,7 @@
 
         @pl.when(step < 3)
         def _():
-            product = dot(first_ref[...], proj_ref[0], ROW_DIMS).astype(BF16)
+            product = dot(first_ref[...], proj_ref[...], ROW_DIMS).astype(BF16)
             split_store(product, where_ref, keep_out, give_out, rows, True)
 
         @pl.when(step == 3)
@@ -732,7 +783,7 @@
             (first_in, whole(first_in)),
             (
                 grad_proj,
-                pl.BlockSpec((1, count, width), lambda step: (jnp.minimum(step, 2), 0, 0)),
+                pl.BlockSpec((count, width), lambda step: (0, jnp.minimum(step, 2))),
             ),
             (mixed, whole(mixed)),
             (grad_attn, whole(grad_attn)),
@@ -740,6 +791,53 @@
         terms_out(chips, rows, width, True),
         flops=19 * 10**9,
     )
+
+
+def plane_terms(where, keep, got):
+    _, chips, rows, width = keep.shape
+    cut = chips // 2
+    flips = (1, 3, 2, 0)
+
+    def place(step, where_ref):
+        flip = 0
+        for at in range(4):
+            flip = jnp.where(step == at, flips[at], flip)
+        return where_ref[0] ^ flip, 0, 0, 0
+
+    def kernel(where_ref, keep_ref, got_ref, x_out, y_out, stay_out):
+        targets = {
+            1: ((x_out, 0), (stay_out, 3)),
+            3: ((x_out, 1), (y_out, 1)),
+            2: ((stay_out, 1), (y_out, 0)),
+            0: ((stay_out, 0), (stay_out, 2)),
+        }
+        for at, flip in enumerate(flips):
+
+            @pl.when(pl.program_id(0) == at)
+            def _(flip=flip):
+                for half, (out, slot) in enumerate(targets[flip]):
+                    span = slice(half * cut, half * cut + cut)
+                    out[slot] = keep_ref[0, span] + got_ref[0, span]
+
+    block = (1, chips, rows, width)
+    shapes = [(2, cut, rows, width), (2, cut, rows, width), (4, cut, rows, width)]
+    return pl.pallas_call(
+        kernel,
+        out_shape=[jax.ShapeDtypeStruct(shape, BF16) for shape in shapes],
+        grid_spec=pltpu.PrefetchScalarGridSpec(
+            num_scalar_prefetch=1,
+            grid=(4,),
+            in_specs=[pl.BlockSpec(block, place), pl.BlockSpec(block, place)],
+            out_specs=[
+                pl.BlockSpec(shape, lambda step, where_ref: (0, 0, 0, 0)) for shape in shapes
+            ],
+        ),
+        cost_estimate=pl.CostEstimate(
+            flops=7 * 10**9, bytes_accessed=6 * keep.size, transcendentals=0
+        ),
+        compiler_params=pltpu.CompilerParams(vmem_limit_bytes=VMEM_LIMIT),
+        name="plane_terms",
+    )(where, keep, got)
 
 
 X_SWAP = [(0, 1), (1, 0), (2, 3), (3, 2)]
@@ -817,7 +915,7 @@
                 return Pieces(
                     [gathered[part].reshape(count * rows, width) for part in range(4)],
                     [lambda item, core, part=part: (part, 0, count * rows) for part in range(4)],
-                    (4, count * rows, width),
+                    (2, count * rows, 2 * width),
                     True,
                 )
             return Pieces(
@@ -834,7 +932,7 @@
         unit = rows if slot_first else 1
         if slot_first:
             arrays = [array.reshape(-1, width) for array in arrays]
-            shape = (4, count * rows, width)
+            shape = (2, count * rows, 2 * width)
         else:
             shape = (count, 4, rows, width)
         places = [lambda item, core: (item, 0, count * unit)]
@@ -851,35 +949,24 @@
 
 
 class Collect:
-    def __init__(self, keep, give):
-        self.keep, self.give = keep, give
+    def __init__(self, where, keep, give):
+        self.where, self.keep, self.give = where, keep, give
         self.item = lax.axis_index("item")
 
-    def pair(self):
+    def pair(self, *wait_for):
+        self.give = after(self.give, *wait_for)
         self.got = swap_core(self.give)
 
     def near(self, *wait_for):
         got = after(self.got, *wait_for)
-        cut = self.keep.shape[1] // 2
-        item = self.item
-
-        def low(slot):
-            return pick(self.keep[:, :cut], slot) + pick(got[:, :cut], slot)
-
-        def high(slot):
-            return pick(self.keep[:, cut:], slot) + pick(got[:, cut:], slot)
-
-        x_out = jnp.stack([low(item ^ 1), low(item ^ 3)])
-        y_out = jnp.stack([high(item ^ 2), high(item ^ 3)])
-        self.low, self.low_on = low(item), low(item ^ 2)
-        self.high, self.high_on = high(item), high(item ^ 1)
+        x_out, y_out, self.stay = plane_terms(self.where, self.keep, got)
         self.x_in, self.y_in = swap_x(x_out), swap_y(y_out)
-        return self.low, self.low_on, self.high, self.high_on, x_out, y_out
+        return (self.stay,)
 
     def far(self, *wait_for):
         x_in, y_in = after2((self.x_in, self.y_in), *wait_for)
-        low_on, high_on = self.low_on + x_in[1], self.high_on + y_in[1]
-        self.low, self.high = self.low + x_in[0], self.high + y_in[0]
+        low_on, high_on = self.stay[1] + x_in[1], self.stay[3] + y_in[1]
+        self.low, self.high = self.stay[0] + x_in[0], self.stay[2] + y_in[0]
         self.y_far, self.x_far = swap_y(low_on), swap_x(high_on)
         return low_on, high_on
 
@@ -893,8 +980,8 @@
         )
         return (plane,)
 
-    def finish(self):
-        own, item = self.own, self.item
+    def finish(self, *wait_for):
+        own, item = after(self.own, *wait_for), self.item
         far = lax.ppermute(own, "item", [(at, at ^ 3) for at in range(4)])
         stack = jnp.stack([own, swap_x(own), swap_y(own), far])
         return jnp.stack([pick(stack, item ^ part) for part in range(4)])
@@ -950,9 +1037,13 @@
     attn_scale = 1.0 / math.sqrt(width // HEADS)
     where = jnp.stack([group_idx, frame_pos % 2, frame_pos]).astype(jnp.int32)
 
-    def to_positions(value):
+    def to_positions(value, *extra):
         chunks = value[0].reshape(own_frames, frame_count, positions, width).transpose(1, 0, 2, 3)
-        return lax.all_to_all(chunks, "frame", 0, 0, tiled=True).reshape(rows, width)
+        chunks = chunks.reshape(frame_count, own_frames * positions, width)
+        for more in extra:
+            more = jnp.broadcast_to(more[None], (frame_count, *more.shape))
+            chunks = jnp.concatenate([chunks, more], axis=1)
+        return lax.all_to_all(chunks, "frame", 0, 0, tiled=True)
 
     def to_frames(value, *wait_for):
         chunks = value.reshape(frame_count, own_frames, positions, width)
@@ -970,13 +1061,14 @@
     small_rows, small_cols = round_up(clips + 1, 16), round_up(max(ada_cols, bias_cols), LANES)
     small = jnp.concatenate(
         [
-            jnp.pad(ada_part.astype(BF16), ((0, 0), (0, small_cols - ada_cols))),
-            jnp.pad(b_fc1[None], ((0, small_rows - clips - 1), (0, small_cols - bias_cols))),
+            jnp.pad(ada_part.astype(BF16), ((0, 0), (0, width - ada_cols))),
+            jnp.pad(b_fc1[None], ((0, small_rows - clips - 1), (0, width - bias_cols))),
         ],
         axis=0,
     )
-    x_arrived = to_positions(tokens)
-    small_all = share_small(after(small, x_arrived))
+    x_arrived = to_positions(tokens, small)
+    small_all = x_arrived[:, own_frames * positions :]
+    x_arrived = x_arrived.reshape(-1, width)
     clip_slots = round_up(clips, 16)
     mod = small_all[:, :clips, :ada_cols].transpose(1, 0, 2).reshape(clips, -1)
     mod = jnp.pad(mod, ((0, clip_slots - clips), (0, 0)))
@@ -989,21 +1081,21 @@
     spread_attn = Spread(got_attn, True)
     near_attn = spread_attn.near()
     got_fc1 = gather_frame(
-        after(jnp.stack(jnp.split(w_fc1, 4, axis=1)), x_arrived, *near_attn)
+        jnp.stack(jnp.split(w_fc1, 4, axis=1))
     )
     far_attn = spread_attn.far()
     fc2_rows = w_fc2.shape[0] // 4
-    got_fc2 = gather_frame(after(w_fc2.reshape(4, fc2_rows, width), *far_attn))
+    got_fc2 = gather_frame(after(w_fc2.reshape(4, fc2_rows, width), x_arrived, *far_attn))
 
     square = is_square()
     chips = frame_count // 2
     spread_fc1 = Spread(got_fc1, True)
     spread_fc2 = Spread(got_fc2, False)
-    cot_arrived = to_positions(after(cotangent, x_arrived))
     near_fc1 = spread_fc1.near(*far_attn)
     x_rows, first_in, projected, full_attn = qkv_call(
-        where, x_arrived, hot, mod, spread_attn.pieces(), positions, frames
-    )
+        where, x_arrived, hot, mod, spread_attn.pieces(), positions, frames, own_frames
+    )
+    cot_arrived = to_positions(after(cotangent, projected)).reshape(rows, width)
     mixed = attend(after(projected, *near_fc1), positions, frames, attn_scale)
     far_fc1 = spread_fc1.far()
     near_fc2 = spread_fc2.near(*far_fc1)
@@ -1011,13 +1103,13 @@
         after(mixed, *far_fc1), x_rows, hot, mod, full_attn
     )
     far_fc2 = spread_fc2.far()
-    grad_rows, grad_mlp = cot_call(after(cot_arrived, second_in), hot, mod, positions, frames)
     post_act, slope, full_fc1 = fc1_call(
-        where, after(second_in, grad_mlp), bias, spread_fc1.pieces()
-    )
+        where, second_in, bias, spread_fc1.pieces()
+    )
+    grad_rows, grad_mlp = cot_call(after(cot_arrived, post_act), hot, mod, positions, frames, own_frames)
 
     if square:
-        sum_fc2 = Collect(*fc2_terms(where, post_act, after(grad_mlp, *near_fc2), chips))
+        sum_fc2 = Collect(where, *fc2_terms(where, post_act, after(grad_mlp, *near_fc2), chips))
         sum_fc2.pair()
         seen = (sum_fc2.give,)
     else:
@@ -1039,7 +1131,7 @@
     )
     if square:
         seen = sum_fc2.near(grad_pre)
-        sum_fc1 = Collect(*fc1_terms(where, second_in, after(grad_pre, *seen), chips))
+        sum_fc1 = Collect(where, *fc1_terms(where, second_in, after(grad_pre, *seen), chips))
         sum_fc1.pair()
         seen = (sum_fc1.give,)
     else:
@@ -1048,33 +1140,37 @@
     grad_middle, grad_attn, grad_mixed, sums_mlp = fc1_back_call(
         after(grad_pre, *seen), full_fc1, middle, attn_out, grad_rows, hot, mod, full_attn
     )
-    block_out = to_frames(block_rows, grad_mixed)
     seen = ()
     if square:
-        seen = (*sum_fc2.far(grad_mixed), *sum_fc1.near(grad_mixed), block_out)
+        seen = (*sum_fc2.far(grad_mixed), *sum_fc1.near(grad_mixed))
     grad_proj = attend_back(
         projected, after(grad_mixed, *seen), positions, frames, attn_scale
     )
+    block_out = to_frames(block_rows, grad_proj)
     if square:
-        seen = (*sum_fc2.line(grad_proj), *sum_fc1.far(grad_proj))
+        seen = (*sum_fc2.line(grad_proj), *sum_fc1.far(grad_proj), block_out)
         sum_attn = Collect(
-            *attn_terms(where, first_in, after(grad_proj, *seen), mixed, grad_attn, chips)
+            where, *attn_terms(where, first_in, after(grad_proj, *seen), mixed, grad_attn, chips)
         )
-        sum_attn.pair()
-        seen = (*sum_fc1.line(sum_attn.give), *sum_attn.near())
+        seen = sum_fc1.line()
+        sum_attn.pair(*seen)
+        seen = (sum_attn.give, sum_fc2.own)
     else:
-        part_attn = [dot(first_in, grad_proj[part], ROW_DIMS) for part in range(3)]
+        part_attn = [dot(first_in, part, ROW_DIMS) for part in jnp.split(grad_proj, 3, axis=1)]
         part_attn = jnp.stack([*part_attn, dot(mixed, grad_attn, ROW_DIMS)])
         part_attn = part_attn.reshape(4, frame_count, shard_rows, width)
     token_rows, sums_attn = qkv_back_call(
         after(grad_proj, *seen), full_attn, x_rows, grad_middle, hot, mod, positions, frames
     )
     if square:
-        sum_attn.far(token_rows)
-        sum_attn.line()
-        sum_fc2, sum_fc1, sum_attn = sum_fc2.finish(), sum_fc1.finish(), sum_attn.finish()
+        sum_attn.near(token_rows, sum_fc1.own)
+        sum_attn.far()
+        seen = sum_attn.line()
+        sum_fc2, sum_fc1, sum_attn = sum_fc2.finish(*seen), sum_fc1.finish(*seen), sum_attn.finish()
     else:
+        seen = ()
         sum_fc2, sum_fc1, sum_attn = sum_plain(part_fc2), sum_plain(part_fc1), sum_plain(part_attn)
+    grad_tokens = to_frames(token_rows, *seen)
     part_mod = jnp.concatenate([sums_attn, sums_mlp, sum_gate_mlp[None]], axis=0)[:, :clips]
     part_mod = part_mod.transpose(1, 0, 2).reshape(clips, frame_count, ada_cols)
     part_small = jnp.concatenate(
@@ -1087,8 +1183,7 @@
         ],
         axis=0,
     ).astype(BF16)
-    small_terms = lax.all_to_all(part_small.transpose(1, 0, 2), "frame", 0, 0, tiled=False)
-    grad_tokens = to_frames(after(token_rows, small_terms))
+    small_terms = lax.all_to_all(after(part_small, *seen).transpose(1, 0, 2), "frame", 0, 0, tiled=False)
     small_sum = sum_items(jnp.sum(small_terms.astype(F32), axis=0))
     grad_modulation = small_sum[:clips, :ada_cols]
     sum_bias = small_sum[clips, :bias_cols]

time: 712 us -> 642 us (0.902)
  local copies, waits for them, and re-layouts: 72.1 us -> 31.7 us
  waiting for transfers between devices: 191 us -> 175 us
  other arithmetic: 50.6 us -> 36.3 us
    pallas_call x0 -> x3, Pallas kernels: none -> 23.4 us  [plane_terms(): pl.pallas_call(kernel, out_shape=[jax.ShapeDtypeStruct(shape, BF16) for s...]
    slice x6 -> x0, local copies, waits for them, and re-layouts: 22.9 us -> none  [high(): return pick(self.keep[:, cut:], slot) + pick(got[:, cut:], slot)]
    pallas_call x1, Pallas kernels: 46.7 us -> 29.9 us  [attend_back(): pl.pallas_call(lambda *refs: attend_back_kernel(frames, scale, *refs), ou...]
    ppermute x16, waiting for transfers between devices: 47.8 us -> 63.8 us  [swap_x(): return lax.ppermute(value, 'item', X_SWAP)]
    reduce_scatter x3, waiting for transfers between devices: 24.8 us -> 13.2 us  [line(): lax.psum_scatter(plane, 'frame', scatter_dimension=0, tiled=False, axis_i...]
    add x12 -> x3, other arithmetic: 19 us -> 8.24 us  [far(): low_on, high_on = (self.stay[1] + x_in[1], self.stay[3] + y_in[1])]
    all_gather x3, waiting for transfers between devices: 52 us -> 41.3 us  [gather_frame(): return lax.all_gather(pick(parts, lax.axis_index('item')), 'frame', axis=0)]
    all_to_all x2, waiting for transfers between devices: 7.94 us -> 0.01 us  [to_frames(): moved = after(lax.all_to_all(chunks, 'frame', 0, 0, tiled=True), *wait_for)]
  transfers between devices with their start and end apart: 63 -> 62, of which waited for: 27 -> 20; matrix products, arithmetic and copies ran while one was open for 16% -> 10% of each run, Pallas kernels for 38% -> 40%
where the time goes in v2:
time: 642 us; the launch traced here: 634 us
  Pallas kernels  290 us (45%)
  waiting for transfers between devices  175 us (27%)
  starting transfers between devices  77.3 us (12%)
  other arithmetic  36.3 us (6%)
  local copies, waits for them, and re-layouts  31.7 us (5%)
  between operations  15.4 us (2%)
  matrix products  9.37 us (1%)
    pallas_call x10, Pallas kernels, call(): pl.pallas_call(kernel, out_shape=[jax.ShapeDtypeStruct(shape, dtype) for...  217 us
    ppermute x16, waiting for transfers between devices, swap_x(): return lax.ppermute(value, 'item', X_SWAP)  63.8 us
    all_gather x3, waiting for transfers between devices, gather_frame(): return lax.all_gather(pick(parts, lax.axis_index('item')), 'frame', axis=0)  41.3 us
    ppermute x16, waiting for transfers between devices, swap_y(): return lax.ppermute(value, 'item', Y_SWAP)  30.7 us
    pallas_call x1, Pallas kernels, attend_back(): pl.pallas_call(lambda *refs: attend_back_kernel(frames, scale, *refs), ou...  29.9 us
    pallas_call x3, Pallas kernels, plane_terms(): pl.pallas_call(kernel, out_shape=[jax.ShapeDtypeStruct(shape, BF16) for s...  23.4 us
    pallas_call x1, Pallas kernels, attend(): pl.pallas_call(lambda *refs: attend_kernel(frames, scale, *refs), out_sha...  19.7 us
    ppermute x16, starting transfers between devices, swap_y(): return lax.ppermute(value, 'item', Y_SWAP)  18.4 us
  transfers between devices with their start and end apart: 62, of which 20 were waited for; matrix products, arithmetic and copies ran while one was open for 10% of the time, Pallas kernels for 40%

profile of v2, /device:TPU:0, one launch (start us, length us, event | category | flops | bytes accessed | tf_op | source)
XLA Modules:
  0.0 634.5 jit_solution(307349323490378762)
XLA Ops:
  25.2 41.3 %all-gather.4.cloned.1.call-done = bf16[8,144,1152]{2,1,0:T(8,128)(2,1)} async-done(((bf16[1,144,1152]{2,1,0:T(8,128)(2,1)}), bf16[8,144,1152]{2,1,0:T(8,128)(2,1)}) %all-gather.4.cloned.1.call-update) | async-done | bytes 2654224 | tf_op jit(solution)/shard_map/all_gather | solution.py:883
  70.9 28.4 %collective-permute-done = bf16[4,144,1152]{2,1,0:T(8,128)(2,1)S(1)} collective-permute-done((bf16[4,144,1152]{2,1,0:T(8,128)(2,1)S(1)}, bf16[4,144,1152]{2,1,0:T(8,128)(2,1)S(1)}, u32[]{:S(2)}, u32[]{:S(2)}) %collective-permute-start) | collective-permute-done | bytes 1327136 | tf_op jit(solution)/shard_map/ppermute | solution.py:848
  103.5 15.7 %all-to-all-done = bf16[8,128,1152]{2,1,0:T(8,128)(2,1)} async-done(((bf16[8,128,1152]{2,1,0:T(8,128)(2,1)}), bf16[8,128,1152]{2,1,0:T(8,128)(2,1)}, u32[]{:S(2)}, u32[]{:S(2)}) %all-to-all-start) | async-done | bytes 2359328 | tf_op jit(solution)/shard_map/all_to_all | solution.py:1046
  131.0 21.4 %project.1 = (bf16[896,1152]{1,0:T(8,128)(2,1)}, bf16[896,1152]{1,0:T(8,128)(2,1)}, bf16[896,3456]{1,0:T(8,128)(2,1)}, bf16[2,1152,2304]{2,1,0:T(8,128)(2,1)}) custom-call(s32[3]{0:T(128)} %pad_add_fusion.where_ref, bf16[1024,1152]{1,0:T(8,128)(2,1)} %bitcast.6.x_ref, bf16[896,16]{1,0:T(8,128)(2,1)} %bitcast.150, bf16[16,6912]{1,0:T(8,128)(2,1)} %pad.29.mod_ref, ...), custom_call_target="tpu_custom_call" | custom-call | flops 20000000000 | bytes 34164748 | tf_op jit(solution)/shard_map/project/pallas_call | solution.py:225
  153.9 7.3 %all-to-all-start.1 = ((bf16[8,112,1152]{2,1,0:T(8,128)(2,1)}), bf16[8,112,1152]{2,1,0:T(8,128)(2,1)}, u32[]{:S(2)}, u32[]{:S(2)}) async-start(bf16[8,112,1152]{2,1,0:T(8,128)(2,1)} %bitcast.124), calls=%async_computation.1 | async-start | bytes 4128768 | tf_op jit(solution)/shard_map/all_to_all | solution.py:1046
  167.0 19.7 %attend.1.mixed_ref = bf16[896,1152]{1,0:T(8,128)(2,1)} custom-call(bf16[896,3456]{1,0:T(8,128)(2,1)} %get-tuple-element.92.refs_0_), custom_call_target="tpu_custom_call" | custom-call | flops 12999999488 | bytes 8257536 | tf_op jit(solution)/shard_map/attend/pallas_call | solution.py:173
  187.2 9.2 %attn_out.1 = (bf16[896,1152]{1,0:T(8,128)(2,1)}, f32[896,1152]{1,0:T(8,128)}, bf16[896,1152]{1,0:T(8,128)(2,1)}) custom-call(bf16[896,1152]{1,0:T(8,128)(2,1)} %attend.1.mixed_ref, bf16[896,1152]{1,0:T(8,128)(2,1)} %get-tuple-element.96.x_ref, bf16[896,16]{1,0:T(8,128)(2,1)} %bitcast.151, bf16[16,6912]{1,0:T(8,128)(2,1)} %pad.29.mod_ref, ...), custom_call_target="tpu_custom_call" | custom-call | flops 8999999488 | bytes 23252992 | tf_op jit(solution)/shard_map/attn_out/pallas_call | solution.py:225
  199.2 24.1 %fc1.1 = (bf16[896,4608]{1,0:T(8,128)(2,1)}, bf16[896,4608]{1,0:T(8,128)(2,1)}, bf16[2,1152,2304]{2,1,0:T(8,128)(2,1)}) custom-call(s32[3]{0:T(128)} %pad_add_fusion.where_ref, bf16[896,1152]{1,0:T(8,128)(2,1)} %get-tuple-element.98.x_ref.left_ref, bf16[1,4608]{1,0:T(2,128)(2,1)} %reshape_squeeze.10.bias_ref, bf16[1152,1152]{1,0:T(8,128)(2,1)} %bitcast.132, ...), custom_call_target="tpu_custom_call" | custom-call | flops 24999999488 | bytes 39822348 | tf_op jit(solution)/shard_map/fc1/pallas_call | solution.py:225
  223.4 6.6 %cotangent.1 = (bf16[896,1152]{1,0:T(8,128)(2,1)}, bf16[896,1152]{1,0:T(8,128)(2,1)}) custom-call(bf16[896,1152]{1,0:T(8,128)(2,1)} %bitcast.38.cot_ref, bf16[896,16]{1,0:T(8,128)(2,1)} %bitcast.152, bf16[16,6912]{1,0:T(8,128)(2,1)} %pad.29.mod_ref), custom_call_target="tpu_custom_call" | custom-call | flops 6000000000 | bytes 6443008 | tf_op jit(solution)/shard_map/cotangent/pallas_call | solution.py:225
  236.3 18.1 %fc2_terms.1 = (bf16[4,4,144,1152]{3,2,1,0:T(8,128)(2,1)}, bf16[4,4,144,1152]{3,2,1,0:T(8,128)(2,1)}) custom-call(s32[3]{0:T(128)} %pad_add_fusion.where_ref, bf16[896,4608]{1,0:T(8,128)(2,1)} %get-tuple-element.99.left_ref.post_ref, bf16[896,1152]{1,0:T(8,128)(2,1)} %get-tuple-element.108.right_ref.gmlp_ref), custom_call_target="tpu_custom_call" | custom-call | flops 17999998976 | bytes 20938764 | tf_op jit(solution)/shard_map/fc2_terms/pallas_call | solution.py:225
  255.1 7.4 %collective-permute-done.22.rest_7_ = bf16[2,144,1152]{2,1,0:T(8,128)(2,1)S(1)} collective-permute-done((bf16[2,144,1152]{2,1,0:T(8,128)(2,1)}, bf16[2,144,1152]{2,1,0:T(8,128)(2,1)S(1)}, u32[]{:S(2)}, u32[]{:S(2)}) %collective-permute-start.22) | collective-permute-done | bytes 663584 | tf_op jit(solution)/shard_map/ppermute | solution.py:857
  266.1 40.3 %fc2.1 = (bf16[896,1152]{1,0:T(8,128)(2,1)}, bf16[896,4608]{1,0:T(8,128)(2,1)}, f32[1,4608]{1,0:T(1,128)}, f32[16,1152]{1,0:T(8,128)}) custom-call(s32[3]{0:T(128)} %pad_add_fusion.where_ref, bf16[896,4608]{1,0:T(8,128)(2,1)} %get-tuple-element.99.left_ref.post_ref, bf16[896,4608]{1,0:T(8,128)(2,1)} %get-tuple-element.100.slope_ref, ...), custom_call_target="tpu_custom_call" | custom-call | flops 44000002048 | bytes 46053388 | tf_op jit(solution)/shard_map/fc2/pallas_call | solution.py:225
  306.4 7.8 %plane_terms.3 = (bf16[2,2,144,1152]{3,2,1,0:T(8,128)(2,1)}, bf16[2,2,144,1152]{3,2,1,0:T(8,128)(2,1)}, bf16[4,2,144,1152]{3,2,1,0:T(8,128)(2,1)}) custom-call(s32[3]{0:T(128)} %pad_add_fusion.where_ref, bf16[4,4,144,1152]{3,2,1,0:T(8,128)(2,1)} %get-tuple-element.115.keep_ref, bf16[4,4,144,1152]{3,2,1,0:T(8,128)(2,1)} %collective-permute-done.24.got_ref), custom_call_target="tpu_custom_call" | custom-call | flops 7000000000 | bytes 15925248 | tf_op jit(solution)/shard_map/plane_terms/pallas_call | solution.py:824
  314.2 17.9 %fc1_terms.1 = (bf16[4,4,144,1152]{3,2,1,0:T(8,128)(2,1)}, bf16[4,4,144,1152]{3,2,1,0:T(8,128)(2,1)}) custom-call(s32[3]{0:T(128)} %pad_add_fusion.where_ref, bf16[896,1152]{1,0:T(8,128)(2,1)} %get-tuple-element.98.x_ref.left_ref, bf16[896,4608]{1,0:T(8,128)(2,1)} %get-tuple-element.120.right_ref.pre_ref), custom_call_target="tpu_custom_call" | custom-call | flops 17999998976 | bytes 20938764 | tf_op jit(solution)/shard_map/fc1_terms/pallas_call | solution.py:225
  340.0 35.0 %fc1_back.1 = (f32[896,1152]{1,0:T(8,128)}, bf16[896,1152]{1,0:T(8,128)(2,1)}, bf16[896,1152]{1,0:T(8,128)(2,1)}, f32[3,16,1152]{2,1,0:T(8,128)}) custom-call(bf16[896,4608]{1,0:T(8,128)(2,1)} %get-tuple-element.120.right_ref.pre_ref, bf16[2,1152,2304]{2,1,0:T(8,128)(2,1)} %get-tuple-element.121.w_ref, f32[896,1152]{1,0:T(8,128)} %get-tuple-element.110.mid_ref, ...), custom_call_target="tpu_custom_call" | custom-call | flops 32000000000 | bytes 46477312 | tf_op jit(solution)/shard_map/fc1_back/pallas_call | solution.py:225
  380.9 7.8 %plane_terms.4 = (bf16[2,2,144,1152]{3,2,1,0:T(8,128)(2,1)}, bf16[2,2,144,1152]{3,2,1,0:T(8,128)(2,1)}, bf16[4,2,144,1152]{3,2,1,0:T(8,128)(2,1)}) custom-call(s32[3]{0:T(128)} %pad_add_fusion.where_ref, bf16[4,4,144,1152]{3,2,1,0:T(8,128)(2,1)} %get-tuple-element.128.keep_ref, bf16[4,4,144,1152]{3,2,1,0:T(8,128)(2,1)} %collective-permute-done.27.got_ref), custom_call_target="tpu_custom_call" | custom-call | flops 7000000000 | bytes 15925248 | tf_op jit(solution)/shard_map/plane_terms/pallas_call | solution.py:824
  389.7 29.9 %attend_back.1.proj_ref = bf16[896,3456]{1,0:T(8,128)(2,1)} custom-call(bf16[896,3456]{1,0:T(8,128)(2,1)} %get-tuple-element.92.refs_0_, bf16[896,1152]{1,0:T(8,128)(2,1)} %get-tuple-element.131.refs_1_), custom_call_target="tpu_custom_call" | custom-call | flops 27000000512 | bytes 14450688 | tf_op jit(solution)/shard_map/attend_back/pallas_call | solution.py:190
  431.6 19.6 %attn_terms.1 = (bf16[4,4,144,1152]{3,2,1,0:T(8,128)(2,1)}, bf16[4,4,144,1152]{3,2,1,0:T(8,128)(2,1)}) custom-call(s32[3]{0:T(128)} %pad_add_fusion.where_ref, bf16[896,1152]{1,0:T(8,128)(2,1)} %get-tuple-element.133.first_ref, bf16[896,3456]{1,0:T(8,128)(2,1)} %attend_back.1.proj_ref, bf16[896,1152]{1,0:T(8,128)(2,1)} %attend.1.mixed_ref, ...), custom_call_target="tpu_custom_call" | custom-call | flops 19000000512 | bytes 23003148 | tf_op jit(solution)/shard_map/attn_terms/pallas_call | solution.py:225
  458.9 24.7 %project_back.1 = (bf16[896,1152]{1,0:T(8,128)(2,1)}, f32[2,16,1152]{2,1,0:T(8,128)}) custom-call(bf16[896,3456]{1,0:T(8,128)(2,1)} %attend_back.1.proj_ref, bf16[2,1152,2304]{2,1,0:T(8,128)(2,1)} %get-tuple-element.97.w_ref.wo_ref, bf16[896,1152]{1,0:T(8,128)(2,1)} %get-tuple-element.96.x_ref, f32[896,1152]{1,0:T(8,128)} %get-tuple-element.147.gmid_ref, ...), custom_call_target="tpu_custom_call" | custom-call | flops 23000000512 | bytes 25464832 | tf_op jit(solution)/shard_map/project_back/pallas_call | solution.py:225
  483.7 8.5 %reduce-scatter.6.cloned.1.call-done = bf16[1,144,1152]{2,1,0:T(8,128)(2,1)} async-done(((bf16[4,144,1152]{2,1,0:T(8,128)(2,1)}), bf16[1,144,1152]{2,1,0:T(8,128)(2,1)}) %reduce-scatter.6.cloned.1.call-update) | async-done | bytes 331792 | tf_op jit(solution)/shard_map/reduce_scatter | solution.py:978
  492.2 7.8 %plane_terms.5 = (bf16[2,2,144,1152]{3,2,1,0:T(8,128)(2,1)}, bf16[2,2,144,1152]{3,2,1,0:T(8,128)(2,1)}, bf16[4,2,144,1152]{3,2,1,0:T(8,128)(2,1)}) custom-call(s32[3]{0:T(128)} %pad_add_fusion.where_ref, bf16[4,4,144,1152]{3,2,1,0:T(8,128)(2,1)} %get-tuple-element.149.keep_ref, bf16[4,4,144,1152]{3,2,1,0:T(8,128)(2,1)} %collective-permute-done.34.got_ref), custom_call_target="tpu_custom_call" | custom-call | flops 7000000000 | bytes 15925248 | tf_op jit(solution)/shard_map/plane_terms/pallas_call | solution.py:824
  507.3 23.6 %collective-permute-done.35 = bf16[2,2,144,1152]{3,2,1,0:T(8,128)(2,1)S(1)} collective-permute-done((bf16[2,2,144,1152]{3,2,1,0:T(8,128)(2,1)}, bf16[2,2,144,1152]{3,2,1,0:T(8,128)(2,1)S(1)}, u32[]{:S(2)}, u32[]{:S(2)}) %collective-permute-start.35) | collective-permute-done | bytes 1327136 | tf_op jit(solution)/shard_map/ppermute | solution.py:848
  539.0 11.5 %collective-permute-done.37 = bf16[2,144,1152]{2,1,0:T(8,128)(2,1)} collective-permute-done((bf16[2,144,1152]{2,1,0:T(8,128)(2,1)}, bf16[2,144,1152]{2,1,0:T(8,128)(2,1)}, u32[]{:S(2)}, u32[]{:S(2)}) %collective-permute-start.37) | collective-permute-done | bytes 663584 | tf_op jit(solution)/shard_map/ppermute | solution.py:852
  615.8 7.8 %collective-permute-done.40 = bf16[144,1152]{1,0:T(8,128)(2,1)S(1)} collective-permute-done((bf16[144,1152]{1,0:T(8,128)(2,1)}, bf16[144,1152]{1,0:T(8,128)(2,1)S(1)}, u32[]{:S(2)}, u32[]{:S(2)}) %collective-permute-start.40) | collective-permute-done | bytes 331808 | tf_op jit(solution)/shard_map/ppermute | solution.py:852
  (259 shorter events, 177.8 us)
Async XLA Ops:
  7.2 59.3 %all-gather.4.cloned.1.call-start = ((), (), s32[]{:S(2)}) async-start(), calls=%async_computation.9 | async-start | bytes 2985984 | tf_op jit(solution)/shard_map/all_gather | solution.py:883
  11.6 114.2 %all-gather.6.cloned.1.call-start = ((), (), s32[]{:S(2)}) async-start(), calls=%async_computation.10 | async-start | bytes 2985984 | tf_op jit(solution)/shard_map/all_gather | solution.py:883
  18.8 100.4 %all-to-all-start = ((bf16[8,128,1152]{2,1,0:T(8,128)(2,1)}), bf16[8,128,1152]{2,1,0:T(8,128)(2,1)}, u32[]{:S(2)}, u32[]{:S(2)}) async-start(bf16[8,128,1152]{2,1,0:T(8,128)(2,1)} %pad_maximum_fusion), calls=%async_computation | async-start | bytes 4718592 | tf_op jit(solution)/shard_map/all_to_all | solution.py:1046
  25.1 171.2 %all-gather.8.cloned.1.call-start = ((), (), s32[]{:S(2)}) async-start(), calls=%async_computation.11 | async-start | bytes 2985984 | tf_op jit(solution)/shard_map/all_gather | solution.py:883
  127.3 34.0 %collective-permute-start.8 = (bf16[4,144,1152]{2,1,0:T(8,128)(2,1)S(1)}, bf16[4,144,1152]{2,1,0:T(8,128)(2,1)}, u32[]{:S(2)}, u32[]{:S(2)}) collective-permute-start(bf16[4,144,1152]{2,1,0:T(8,128)(2,1)S(1)} %constant_dynamic-slice_fusion.6), channel_id=1, source_target_pairs={{0,8},{8,0},{16,24},{24,16},{1,9},{9,1},{17,25},{25,17},{2,10},{10... | collective-permute-start | bytes 3981320 | tf_op jit(solution)/shard_map/ppermute | solution.py:848
  128.8 32.4 %collective-permute-start.9 = (bf16[4,144,1152]{2,1,0:T(8,128)(2,1)S(1)}, bf16[4,144,1152]{2,1,0:T(8,128)(2,1)}, u32[]{:S(2)}, u32[]{:S(2)}) collective-permute-start(bf16[4,144,1152]{2,1,0:T(8,128)(2,1)S(1)} %constant_dynamic-slice_fusion.6), channel_id=1, source_target_pairs={{0,16},{16,0},{8,24},{24,8},{1,17},{17,1},{9,25},{25,9},{2,18},{18... | collective-permute-start | bytes 3981320 | tf_op jit(solution)/shard_map/ppermute | solution.py:852
  153.9 69.5 %all-to-all-start.1 = ((bf16[8,112,1152]{2,1,0:T(8,128)(2,1)}), bf16[8,112,1152]{2,1,0:T(8,128)(2,1)}, u32[]{:S(2)}, u32[]{:S(2)}) async-start(bf16[8,112,1152]{2,1,0:T(8,128)(2,1)} %bitcast.124), calls=%async_computation.1 | async-start | bytes 4128768 | tf_op jit(solution)/shard_map/all_to_all | solution.py:1046
  162.4 36.8 %collective-permute-start.12 = (bf16[4,144,1152]{2,1,0:T(8,128)(2,1)}, bf16[4,144,1152]{2,1,0:T(8,128)(2,1)}, u32[]{:S(2)}, u32[]{:S(2)}) collective-permute-start(bf16[4,144,1152]{2,1,0:T(8,128)(2,1)} %collective-permute-done.8), channel_id=1, source_target_pairs={{0,1},{1,0},{2,3},{3,2},{4,5},{5,4},{6,7},{7,6},{8,9},{9,8},{10,11... | collective-permute-start | bytes 3981320 | tf_op jit(solution)/shard_map/ppermute | solution.py:857
  164.1 35.1 %collective-permute-start.13 = (bf16[4,144,1152]{2,1,0:T(8,128)(2,1)}, bf16[4,144,1152]{2,1,0:T(8,128)(2,1)}, u32[]{:S(2)}, u32[]{:S(2)}) collective-permute-start(bf16[4,144,1152]{2,1,0:T(8,128)(2,1)} %collective-permute-done.9), channel_id=1, source_target_pairs={{0,1},{1,0},{2,3},{3,2},{4,5},{5,4},{6,7},{7,6},{8,9},{9,8},{10,11... | collective-permute-start | bytes 3981320 | tf_op jit(solution)/shard_map/ppermute | solution.py:857
  231.1 33.3 %collective-permute-start.20 = (bf16[4,144,1152]{2,1,0:T(8,128)(2,1)}, bf16[4,144,1152]{2,1,0:T(8,128)(2,1)S(1)}, u32[]{:S(2)}, u32[]{:S(2)}) collective-permute-start(bf16[4,144,1152]{2,1,0:T(8,128)(2,1)} %collective-permute-done.16.rest_1_), channel_id=1, source_target_pairs={{0,1},{1,0},{2,3},{3,2},{4,5},{5,4},{6,7},{7,6},{8,9},{9,8},{10,11... | collective-permute-start | bytes 3981320 | tf_op jit(solution)/shard_map/ppermute | solution.py:857
  254.5 52.0 %collective-permute-start.24 = (bf16[4,4,144,1152]{3,2,1,0:T(8,128)(2,1)}, bf16[4,4,144,1152]{3,2,1,0:T(8,128)(2,1)}, u32[]{:S(2)}, u32[]{:S(2)}) collective-permute-start(bf16[4,4,144,1152]{3,2,1,0:T(8,128)(2,1)} %get-tuple-element.107), channel_id=1, source_target_pairs={{0,1},{1,0},{2,3},{3,2},{4,5},{5,4},{6,7},{7,6},{8,9},{9,8},{10,11... | collective-permute-start | bytes 15925256 | tf_op jit(solution)/shard_map/ppermute | solution.py:857
  332.1 48.7 %collective-permute-start.27 = (bf16[4,4,144,1152]{3,2,1,0:T(8,128)(2,1)}, bf16[4,4,144,1152]{3,2,1,0:T(8,128)(2,1)}, u32[]{:S(2)}, u32[]{:S(2)}) collective-permute-start(bf16[4,4,144,1152]{3,2,1,0:T(8,128)(2,1)} %get-tuple-element.119), channel_id=1, source_target_pairs={{0,1},{1,0},{2,3},{3,2},{4,5},{5,4},{6,7},{7,6},{8,9},{9,8},{10,11... | collective-permute-start | bytes 15925256 | tf_op jit(solution)/shard_map/ppermute | solution.py:857
  333.6 86.0 %all-to-all-start.2 = ((bf16[8,2,56,1152]{3,2,1,0:T(8,128)(2,1)}), bf16[8,2,56,1152]{3,2,1,0:T(8,128)(2,1)}, u32[]{:S(2)}, u32[]{:S(2)}) async-start(bf16[8,2,56,1152]{3,2,1,0:T(8,128)(2,1)} %bitcast.130), calls=%async_computation.2 | async-start | bytes 4128768 | tf_op jit(solution)/shard_map/all_to_all | solution.py:1050
  338.9 120.1 %reduce-scatter.4.cloned.1.call-start = ((), (), s32[]{:S(2)}) async-start(), calls=%async_computation.12 | async-start | bytes 1658880 | tf_op jit(solution)/shard_map/reduce_scatter | solution.py:978
  338.9 36.1 %collective-permute-start.25 = (bf16[2,2,144,1152]{3,2,1,0:T(8,128)(2,1)}, bf16[2,2,144,1152]{3,2,1,0:T(8,128)(2,1)S(1)}, u32[]{:S(2)}, u32[]{:S(2)}) collective-permute-start(bf16[2,2,144,1152]{3,2,1,0:T(8,128)(2,1)} %get-tuple-element.124), channel_id=1, source_target_pairs={{0,8},{8,0},{16,24},{24,16},{1,9},{9,1},{17,25},{25,17},{2,10},{10... | collective-permute-start | bytes 3981320 | tf_op jit(solution)/shard_map/ppermute | solution.py:848
  340.0 35.0 %collective-permute-start.26 = (bf16[2,2,144,1152]{3,2,1,0:T(8,128)(2,1)}, bf16[2,2,144,1152]{3,2,1,0:T(8,128)(2,1)}, u32[]{:S(2)}, u32[]{:S(2)}) collective-permute-start(bf16[2,2,144,1152]{3,2,1,0:T(8,128)(2,1)} %get-tuple-element.125), channel_id=1, source_target_pairs={{0,16},{16,0},{8,24},{24,8},{1,17},{17,1},{9,25},{25,9},{2,18},{18... | collective-permute-start | bytes 3981320 | tf_op jit(solution)/shard_map/ppermute | solution.py:852
  377.8 41.8 %collective-permute-start.28 = (bf16[2,144,1152]{2,1,0:T(8,128)(2,1)}, bf16[2,144,1152]{2,1,0:T(8,128)(2,1)}, u32[]{:S(2)}, u32[]{:S(2)}) collective-permute-start(bf16[2,144,1152]{2,1,0:T(8,128)(2,1)} %get-tuple-element.177), channel_id=1, source_target_pairs={{0,16},{16,0},{8,24},{24,8},{1,17},{17,1},{9,25},{25,9},{2,18},{18... | collective-permute-start | bytes 1990664 | tf_op jit(solution)/shard_map/ppermute | solution.py:852
  379.9 39.7 %collective-permute-start.29 = (bf16[2,144,1152]{2,1,0:T(8,128)(2,1)}, bf16[2,144,1152]{2,1,0:T(8,128)(2,1)}, u32[]{:S(2)}, u32[]{:S(2)}) collective-permute-start(bf16[2,144,1152]{2,1,0:T(8,128)(2,1)} %get-tuple-element.176), channel_id=1, source_target_pairs={{0,8},{8,0},{16,24},{24,16},{1,9},{9,1},{17,25},{25,17},{2,10},{10... | collective-permute-start | bytes 1990664 | tf_op jit(solution)/shard_map/ppermute | solution.py:848
  388.7 37.2 %collective-permute-start.30 = (bf16[2,2,144,1152]{3,2,1,0:T(8,128)(2,1)}, bf16[2,2,144,1152]{3,2,1,0:T(8,128)(2,1)S(1)}, u32[]{:S(2)}, u32[]{:S(2)}) collective-permute-start(bf16[2,2,144,1152]{3,2,1,0:T(8,128)(2,1)} %get-tuple-element.136), channel_id=1, source_target_pairs={{0,8},{8,0},{16,24},{24,16},{1,9},{9,1},{17,25},{25,17},{2,10},{10... | collective-permute-start | bytes 3981320 | tf_op jit(solution)/shard_map/ppermute | solution.py:848
  389.7 36.1 %collective-permute-start.31 = (bf16[2,2,144,1152]{3,2,1,0:T(8,128)(2,1)}, bf16[2,2,144,1152]{3,2,1,0:T(8,128)(2,1)}, u32[]{:S(2)}, u32[]{:S(2)}) collective-permute-start(bf16[2,2,144,1152]{3,2,1,0:T(8,128)(2,1)} %get-tuple-element.137), channel_id=1, source_target_pairs={{0,16},{16,0},{8,24},{24,8},{1,17},{17,1},{9,25},{25,9},{2,18},{18... | collective-permute-start | bytes 3981320 | tf_op jit(solution)/shard_map/ppermute | solution.py:852
  425.8 66.4 %reduce-scatter.6.cloned.1.call-start = ((), (), s32[]{:S(2)}) async-start(), calls=%async_computation.13 | async-start | bytes 1658880 | tf_op jit(solution)/shard_map/reduce_scatter | solution.py:978
  454.2 38.0 %collective-permute-start.34 = (bf16[4,4,144,1152]{3,2,1,0:T(8,128)(2,1)}, bf16[4,4,144,1152]{3,2,1,0:T(8,128)(2,1)}, u32[]{:S(2)}, u32[]{:S(2)}) collective-permute-start(bf16[4,4,144,1152]{3,2,1,0:T(8,128)(2,1)} %get-tuple-element.145), channel_id=1, source_target_pairs={{0,1},{1,0},{2,3},{3,2},{4,5},{5,4},{6,7},{7,6},{8,9},{9,8},{10,11... | collective-permute-start | bytes 15925256 | tf_op jit(solution)/shard_map/ppermute | solution.py:857
  502.9 58.0 %all-to-all-start.3 = ((bf16[8,2,56,1152]{3,2,1,0:T(8,128)(2,1)}), bf16[8,2,56,1152]{3,2,1,0:T(8,128)(2,1)}, u32[]{:S(2)}, u32[]{:S(2)}) async-start(bf16[8,2,56,1152]{3,2,1,0:T(8,128)(2,1)} %bitcast.129), calls=%async_computation.4 | async-start | bytes 4128768 | tf_op jit(solution)/shard_map/all_to_all | solution.py:1050
  507.3 97.7 %reduce-scatter.8.cloned.1.call-start = ((), (), s32[]{:S(2)}) async-start(), calls=%async_computation.14 | async-start | bytes 1658880 | tf_op jit(solution)/shard_map/reduce_scatter | solution.py:978
  (66 other events, 944.2 us)
Sparse Core Ops, SparseCore 0:
  11.7 54.6 all-gather.3
  68.7 50.7 all-gather.5
  121.7 36.8 all-gather.7
  425.9 33.0 reduce-scatter.3
  461.7 30.4 reduce-scatter.5
  560.3 34.3 reduce-scatter.7

commit v3 on v2

--- a/solution.py
+++ b/solution.py
@@ -248,35 +248,41 @@
 
 
 class Pieces:
-    def __init__(self, arrays, places, shape, by_columns):
-        self.arrays, self.places, self.shape, self.by_columns = arrays, places, shape, by_columns
+    def __init__(self, arrays, places, shape, by_columns, flipped):
+        self.arrays, self.places, self.shape = arrays, places, shape
+        self.by_columns, self.flipped = by_columns, flipped
+
+    def quarter(self, where_ref, turn):
+        return where_ref[0] ^ turn if self.flipped else turn
+
+    def columns(self, slot):
+        width = self.shape[1] // 4
+        return pl.ds(pl.multiple_of(slot * width, width), width)
 
     def start(self, where_ref, refs, full, sems):
         for ref, place in zip(refs, self.places):
             slot, first, count = place(where_ref[0], where_ref[1])
             if self.by_columns:
-                width = self.shape[2] // 2
-                column = pl.multiple_of(slot % 2 * width, width)
-                target = full.at[slot // 2, pl.ds(first, count), pl.ds(column, width)]
-                pltpu.make_async_copy(ref, target, sems.at[slot // 2]).start()
+                target = full.at[pl.ds(first, count), self.columns(slot)]
+                pltpu.make_async_copy(ref, target, sems.at[slot]).start()
                 continue
-            half = self.shape[0] // 2
             for turn in range(count):
                 target = full.at[first + turn, slot]
-                pltpu.make_async_copy(ref.at[turn], target, sems.at[(first + turn) // half]).start()
-
-    def part(self, full, half):
+                sem = sems.at[(first + turn) // (self.shape[0] // 4)]
+                pltpu.make_async_copy(ref.at[turn], target, sem).start()
+
+    def part(self, full, at):
         if self.by_columns:
-            return full.at[half]
-        turns = self.shape[0] // 2
-        return full.at[half * turns : (half + 1) * turns]
-
-    def wait(self, half, full, sems):
-        part = self.part(full, half)
-        pltpu.make_async_copy(part, part, sems.at[half]).wait()
+            return full.at[:, self.columns(at)]
+        turns = self.shape[0] // 4
+        return full.at[at * turns : (at + 1) * turns]
+
+    def wait(self, at, full, sems):
+        part = self.part(full, at)
+        pltpu.make_async_copy(part, part, sems.at[at]).wait()
 
     def scratch(self):
-        return [pltpu.VMEM(self.shape, BF16), pltpu.SemaphoreType.DMA((3,))]
+        return [pltpu.VMEM(self.shape, BF16), pltpu.SemaphoreType.DMA((5,))]
 
 
 def norm_parts(values):
@@ -292,16 +298,16 @@
 
 
 def gather_order(first, count, frames, positions, own_frames, chunk):
-    at = first + lax.broadcasted_iota(jnp.int32, (count, frames // own_frames * chunk), 0)
-    source = lax.broadcasted_iota(jnp.int32, (count, frames // own_frames * chunk), 1)
+    at = first + lax.broadcasted_iota(jnp.int32, (count, 1), 0)
+    source = lax.broadcasted_iota(jnp.int32, (1, frames // own_frames * chunk), 1)
     frame, position = at % frames, at // frames
     wanted = frame // own_frames * chunk + frame % own_frames * positions + position
     return (source == wanted).astype(F32).astype(BF16)
 
 
 def row_order(rows, first, count, inner, outer):
-    at = first + lax.broadcasted_iota(jnp.int32, (count, rows), 0)
-    source = lax.broadcasted_iota(jnp.int32, (count, rows), 1)
+    at = first + lax.broadcasted_iota(jnp.int32, (count, 1), 0)
+    source = lax.broadcasted_iota(jnp.int32, (1, rows), 1)
     return (source == (at % outer) * inner + at // outer).astype(F32).astype(BF16)
 
 
@@ -311,6 +317,26 @@
     return dot(hot, high, ROW_DIMS) + dot(hot, low, ROW_DIMS)
 
 
+def by_tile(my_rows, mod, frames):
+    count = row_tile(my_rows.shape[0] * frames) // frames
+    tiles = my_rows.astype(BF16).reshape(-1, count, my_rows.shape[1])
+    tiles = jnp.pad(tiles, ((0, 0), (0, -count % 8), (0, 0)))
+    return lax.dot_general(tiles, mod, (((2,), (0,)), ((), ())), preferred_element_type=F32)
+
+
+def tile_mod(mod):
+    return pl.BlockSpec((1, *mod.shape[1:]), lambda step: (step, 0, 0))
+
+
+def spread_rows(mod_ref, part, count, frames):
+    width = mod_ref.shape[2] // 6
+    cols = slice(part * width, (part + 1) * width)
+    rows = [
+        jnp.broadcast_to(mod_ref[0, at : at + 1, cols], (frames, width)) for at in range(count)
+    ]
+    return jnp.concatenate(rows, axis=0)
+
+
 def first_step(step, action):
     @pl.when(step == 0)
     def _():
@@ -325,14 +351,14 @@
     ref[index] += value
 
 
-def qkv_call(where, arrived, hot, mod, pieces, positions, frames, own_frames):
+def qkv_call(where, arrived, mod, pieces, positions, frames, own_frames):
     rows, width = positions * frames, arrived.shape[1]
     chunk = arrived.shape[0] * own_frames // frames
     tile = row_tile(rows)
     steps = rows // tile
     count = len(pieces.arrays)
 
-    def kernel(where_ref, x_ref, hot_ref, mod_ref, *rest):
+    def kernel(where_ref, x_ref, mod_ref, *rest):
         piece_refs, rest = rest[:count], rest[count:]
         x_out, first_out, proj_out, full_out, full, sems = rest
         step = pl.program_id(0)
@@ -345,16 +371,28 @@
         inputs = dot(order, x_ref[...])
         x_out[...] = inputs.astype(BF16)
         normed, _ = norm_parts(inputs)
-        shift = dot(hot_ref[...], mod_ref[:, :width])
-        scale = dot(hot_ref[...], mod_ref[:, width : 2 * width])
+        shift = spread_rows(mod_ref, 0, tile // frames, frames)
+        scale = spread_rows(mod_ref, 1, tile // frames, frames)
         first = (normed * (1.0 + scale) + shift).astype(BF16)
         first_out[...] = first
-        back = pltpu.make_async_copy(full, full_out, sems.at[2])
-        first_step(step, lambda: pieces.wait(0, full, sems))
-        proj_out[:, : 2 * width] = dot(first, full[0]).astype(BF16)
-        first_step(step, lambda: pieces.wait(1, full, sems))
-        first_step(step, back.start)
-        proj_out[:, 2 * width :] = dot(first, full[1, :, :width]).astype(BF16)
+        back = pltpu.make_async_copy(full, full_out, sems.at[4])
+
+        @pl.when(step == 0)
+        def _():
+            for turn in range(4):
+                slot = pieces.quarter(where_ref, turn)
+                pieces.wait(slot, full, sems)
+
+                @pl.when(slot < 3)
+                def _():
+                    weight = pieces.part(full, slot)[...]
+                    proj_out[:, pieces.columns(slot)] = dot(first, weight).astype(BF16)
+
+            back.start()
+
+        @pl.when(step > 0)
+        def _():
+            proj_out[...] = dot(first, full[:, : 3 * width]).astype(BF16)
 
         @pl.when(step == steps - 1)
         def _():
@@ -367,8 +405,7 @@
         [
             (where, SCALARS),
             (arrived, whole(arrived)),
-            (hot, tiled(tile, hot.shape[1])),
-            (mod, whole(mod)),
+            (mod, tile_mod(mod)),
             *[(array, HBM) for array in pieces.arrays],
         ],
         [
@@ -382,17 +419,18 @@
     )
 
 
-def out_call(mixed, x_rows, hot, mod, full_attn):
+def out_call(mixed, x_rows, mod, full_attn, frames):
     rows, width = mixed.shape
     tile = row_tile(rows)
 
-    def kernel(mixed_ref, x_ref, hot_ref, mod_ref, w_ref, attn_out, middle_out, second_out):
-        attn = dot(mixed_ref[...], w_ref[0])
-        hot = hot_ref[...]
-        middle = x_ref[...].astype(F32) + dot(hot, mod_ref[:, 2 * width : 3 * width]) * attn
+    def kernel(mixed_ref, x_ref, mod_ref, w_ref, attn_out, middle_out, second_out):
+        attn = dot(mixed_ref[...], w_ref[...])
+        shift, scale, gate = [
+            spread_rows(mod_ref, part, tile // frames, frames)
+            for part in (3, 4, 2)
+        ]
+        middle = x_ref[...].astype(F32) + gate * attn
         normed, _ = norm_parts(middle)
-        shift = dot(hot, mod_ref[:, 3 * width : 4 * width])
-        scale = dot(hot, mod_ref[:, 4 * width : 5 * width])
         attn_out[...] = attn.astype(BF16)
         middle_out[...] = middle
         second_out[...] = (normed * (1.0 + scale) + shift).astype(BF16)
@@ -404,9 +442,8 @@
         [
             (mixed, tiled(tile, width)),
             (x_rows, tiled(tile, width)),
-            (hot, tiled(tile, hot.shape[1])),
-            (mod, whole(mod)),
-            (full_attn, pl.BlockSpec((1, width, width), lambda step: (1, 0, 1))),
+            (mod, tile_mod(mod)),
+            (full_attn, pl.BlockSpec((width, width), lambda step: (0, 3))),
         ],
         [
             ((rows, width), BF16, tiled(tile, width)),
@@ -426,20 +463,16 @@
     tile = row_tile(rows)
     steps = rows // tile
     count = len(pieces.arrays)
-    part = pieces.shape[2]
+    part = pieces.shape[1] // 4
 
     def kernel(where_ref, x_ref, bias_ref, *rest):
         piece_refs, rest = rest[:count], rest[count:]
         post_out, slope_out, full_out, full, sems = rest
         step = pl.program_id(0)
-        back = pltpu.make_async_copy(full, full_out, sems.at[2])
-        first_step(step, lambda: pieces.start(where_ref, piece_refs, full, sems))
-        for half in range(2):
-            first_step(step, lambda half=half: pieces.wait(half, full, sems))
-            if half:
-                first_step(step, back.start)
-            cols = slice(half * part, (half + 1) * part)
-            pre = dot(x_ref[...], full[half]) + bias_ref[:, cols].astype(F32)
+        back = pltpu.make_async_copy(full, full_out, sems.at[4])
+
+        def run(cols):
+            pre = dot(x_ref[...], full[:, cols]) + bias_ref[:, cols].astype(F32)
             square = pre * pre
             curve = jnp.tanh(pre * (GELU_A + GELU_B * square))
             half = 0.5 + 0.5 * curve
@@ -447,6 +480,20 @@
             rise = (0.5 * pre) * (1.0 - curve * curve)
             slope_out[:, cols] = (half + rise * (GELU_A + 3.0 * GELU_B * square)).astype(BF16)
 
+        @pl.when(step == 0)
+        def _():
+            pieces.start(where_ref, piece_refs, full, sems)
+            for turn in range(4):
+                slot = pieces.quarter(where_ref, turn)
+                pieces.wait(slot, full, sems)
+                run(pieces.columns(slot))
+            back.start()
+
+        @pl.when(step > 0)
+        def _():
+            for half in range(2):
+                run(slice(half * 2 * part, (half + 1) * 2 * part))
+
         @pl.when(step == steps - 1)
         def _():
             back.wait()
@@ -462,8 +509,8 @@
             *[(array, HBM) for array in pieces.arrays],
         ],
         [
-            ((rows, 2 * part), BF16, tiled(tile, 2 * part)),
-            ((rows, 2 * part), BF16, tiled(tile, 2 * part)),
+            ((rows, 4 * part), BF16, tiled(tile, 4 * part)),
+            ((rows, 4 * part), BF16, tiled(tile, 4 * part)),
             (pieces.shape, BF16, HBM),
         ],
         pieces.scratch(),
@@ -482,7 +529,7 @@
         valid = jnp.sum(hot.astype(F32), axis=1, keepdims=True)
         grad = dot(order, cot_ref[...]) * valid
         rows_out[...] = grad.astype(BF16)
-        mlp_out[...] = (grad * dot(hot, mod_ref[:, 5 * width :])).astype(BF16)
+        mlp_out[...] = (grad * spread_rows(mod_ref, 5, tile // frames, frames)).astype(BF16)
 
     return call(
         kernel,
@@ -491,7 +538,7 @@
         [
             (arrived, whole(arrived)),
             (hot, tiled(tile, hot.shape[1])),
-            (mod, whole(mod)),
+            (mod, tile_mod(mod)),
         ],
         [
             ((rows, width), BF16, tiled(tile, width)),
@@ -508,31 +555,41 @@
     steps = rows // tile
     count = len(pieces.arrays)
     clips = hot.shape[1]
-    part = hidden // 2
 
     def kernel(where_ref, post_ref, slope_ref, gmlp_ref, grows_ref, mid_ref, hot_ref, mod_ref, *rest):
         piece_refs, rest = rest[:count], rest[count:]
-        block_out, pre_out, bias_out, gate_out, full, sems, held = rest
+        block_out, pre_out, bias_out, gate_out, full, sems, held, sums = rest
         step = pl.program_id(0)
 
-        first_step(step, lambda: pieces.start(where_ref, piece_refs, full, sems))
-        total = None
-        for half in range(2):
-            first_step(step, lambda half=half: pieces.wait(half, full, sems))
-            cols = slice(half * part, (half + 1) * part)
-            weight = pieces.part(full, half)[...].reshape(part, width)
+        def run(first, last):
+            part = hidden // 4
+            cols = slice(first * part, last * part)
+            turns = pieces.shape[0] // 4
+            weight = full[first * turns : last * turns].reshape((last - first) * part, width)
             term = dot(post_ref[:, cols], weight)
-            total = term if total is None else total + term
-            grad_pre = (dot(gmlp_ref[...], weight, COL_DIMS) * slope_ref[:, cols].astype(F32)).astype(BF16)
+            sums[...] = term if not first else sums[...] + term
+            grad_pre = dot(gmlp_ref[...], weight, COL_DIMS) * slope_ref[:, cols].astype(F32)
+            grad_pre = grad_pre.astype(BF16)
             pre_out[:, cols] = grad_pre
-            add_into(
-                bias_out,
-                (slice(None), cols),
-                jnp.sum(grad_pre.astype(F32), axis=0, keepdims=True),
-            )
+            total = jnp.sum(grad_pre.astype(F32), axis=0, keepdims=True)
+            add_into(bias_out, (slice(None), cols), total)
+
+        @pl.when(step == 0)
+        def _():
+            pieces.start(where_ref, piece_refs, full, sems)
+            for at in range(4):
+                pieces.wait(at, full, sems)
+                run(at, at + 1)
+
+        @pl.when(step > 0)
+        def _():
+            run(0, 2)
+            run(2, 4)
+
+        total = sums[...]
         hot = hot_ref[...]
         valid = jnp.sum(hot.astype(F32), axis=1, keepdims=True)
-        gate = dot(hot, mod_ref[:, 5 * width :])
+        gate = spread_rows(mod_ref, 5, tile // frames, frames)
         result = valid * (mid_ref[...] + gate * total)
         held[pl.ds(pl.multiple_of(step * tile, 16), tile), :] = result.astype(BF16)
         add_into(gate_out, slice(None), clip_sums(hot, grows_ref[...].astype(F32) * total))
@@ -555,7 +612,7 @@
             (grad_rows, tiled(tile, width)),
             (middle, tiled(tile, width)),
             (hot, tiled(tile, clips)),
-            (mod, whole(mod)),
+            (mod, tile_mod(mod)),
             *[(array, HBM) for array in pieces.arrays],
         ],
         [
@@ -564,39 +621,54 @@
             ((1, hidden), F32, pl.BlockSpec((1, hidden), lambda step: (0, 0))),
             ((clips, width), F32, pl.BlockSpec((clips, width), lambda step: (0, 0))),
         ],
-        [*pieces.scratch(), pltpu.VMEM((rows, width), BF16)],
+        [*pieces.scratch(), pltpu.VMEM((rows, width), BF16), pltpu.VMEM((tile, width), F32)],
         flops=44 * 10**9,
     )
 
 
-def fc1_back_call(grad_pre, full_fc1, middle, attn_out, grad_rows, hot, mod, full_attn):
+def load_and_dot(step, left_ref, w_ref, held, sems, total, parts):
+    width = left_ref.shape[1] // parts
+    runs = [slice(at * width, (at + 1) * width) for at in range(parts)]
+    loads = [
+        pltpu.make_async_copy(w_ref.at[:, run], held.at[:, run], sems.at[at])
+        for at, run in enumerate(runs)
+    ]
+
+    @pl.when(step == 0)
+    def _():
+        for load in loads:
+            load.start()
+        for at, load in enumerate(loads):
+            load.wait()
+            term = dot(left_ref[:, runs[at]], held[:, runs[at]], COL_DIMS)
+            total[...] = term if not at else total[...] + term
+
+    @pl.when(step > 0)
+    def _():
+        total[...] = dot(left_ref[...], held[...], COL_DIMS)
+
+    return total[...]
+
+
+def fc1_back_call(grad_pre, full_fc1, middle, attn_out, grad_rows, hot, mod, full_attn, frames):
     rows, hidden = grad_pre.shape
     width = middle.shape[1]
     tile = row_tile(rows)
     clips = hot.shape[1]
-    part = hidden // 2
 
     def kernel(pre_ref, w_ref, mid_ref, attn_ref, grows_ref, hot_ref, mod_ref, wo_ref, *outs):
-        gmid_out, gattn_out, gmix_out, sums_out, held, sems = outs
+        gmid_out, gattn_out, gmix_out, sums_out, held, sems, total = outs
         step = pl.program_id(0)
-        loads = [pltpu.make_async_copy(w_ref.at[at], held.at[at], sems.at[at]) for at in range(2)]
-        grad = None
-        for at in range(2):
-            if not at:
-                first_step(step, loads[0].start)
-                first_step(step, loads[1].start)
-            first_step(step, loads[at].wait)
-            term = dot(pre_ref[:, at * part : (at + 1) * part], held[at], COL_DIMS)
-            grad = term if grad is None else grad + term
+        grad = load_and_dot(step, pre_ref, w_ref, held, sems, total, 4)
         hot = hot_ref[...]
-        scale = dot(hot, mod_ref[:, 4 * width : 5 * width])
-        gate = dot(hot, mod_ref[:, 2 * width : 3 * width])
+        scale = spread_rows(mod_ref, 4, tile // frames, frames)
+        gate = spread_rows(mod_ref, 2, tile // frames, frames)
         normed, inverse = norm_parts(mid_ref[...])
         grad_middle = grows_ref[...].astype(F32) + norm_back(normed, inverse, grad * (1.0 + scale))
         gmid_out[...] = grad_middle
         grad_attn = (grad_middle * gate).astype(BF16)
         gattn_out[...] = grad_attn
-        gmix_out[...] = dot(grad_attn, wo_ref[0], COL_DIMS).astype(BF16)
+        gmix_out[...] = dot(grad_attn, wo_ref[...], COL_DIMS).astype(BF16)
         add_into(sums_out, 0, clip_sums(hot, grad_middle * attn_ref[...].astype(F32)))
         add_into(sums_out, 1, clip_sums(hot, grad))
         add_into(sums_out, 2, clip_sums(hot, grad * normed))
@@ -612,8 +684,8 @@
             (attn_out, tiled(tile, width)),
             (grad_rows, tiled(tile, width)),
             (hot, tiled(tile, clips)),
-            (mod, whole(mod)),
-            (full_attn, pl.BlockSpec((1, width, width), lambda step: (1, 0, 1))),
+            (mod, tile_mod(mod)),
+            (full_attn, pl.BlockSpec((width, width), lambda step: (0, 3))),
         ],
         [
             ((rows, width), F32, tiled(tile, width)),
@@ -621,7 +693,11 @@
             ((rows, width), BF16, tiled(tile, width)),
             ((3, clips, width), F32, pl.BlockSpec((3, clips, width), lambda step: (0, 0, 0))),
         ],
-        [pltpu.VMEM(full_fc1.shape, BF16), pltpu.SemaphoreType.DMA((2,))],
+        [
+            pltpu.VMEM(full_fc1.shape, BF16),
+            pltpu.SemaphoreType.DMA((4,)),
+            pltpu.VMEM((tile, width), F32),
+        ],
         flops=32 * 10**9,
     )
 
@@ -632,22 +708,11 @@
     steps = rows // tile
     clips = hot.shape[1]
 
-    def kernel(proj_ref, w_ref, x_ref, gmid_ref, hot_ref, mod_ref, tok_out, sums_out, held, w_held, sems):
+    def kernel(proj_ref, w_ref, x_ref, gmid_ref, hot_ref, mod_ref, tok_out, sums_out, held, w_held, sems, total):
         step = pl.program_id(0)
-        loads = [
-            pltpu.make_async_copy(w_ref.at[0], w_held.at[0], sems.at[0]),
-            pltpu.make_async_copy(
-                w_ref.at[1, :, :width], w_held.at[1, :, :width], sems.at[1]
-            ),
-        ]
-        first_step(step, loads[0].start)
-        first_step(step, loads[1].start)
-        first_step(step, loads[0].wait)
-        grad = dot(proj_ref[:, : 2 * width], w_held[0], COL_DIMS)
-        first_step(step, loads[1].wait)
-        grad += dot(proj_ref[:, 2 * width :], w_held[1, :, :width], COL_DIMS)
+        grad = load_and_dot(step, proj_ref, w_ref, w_held, sems, total, 3)
         hot = hot_ref[...]
-        scale = dot(hot, mod_ref[:, width : 2 * width])
+        scale = spread_rows(mod_ref, 1, tile // frames, frames)
         normed, inverse = norm_parts(x_ref[...].astype(F32))
         result = gmid_ref[...] + norm_back(normed, inverse, grad * (1.0 + scale))
         held[pl.ds(pl.multiple_of(step * tile, 16), tile), :] = result.astype(BF16)
@@ -670,7 +735,7 @@
             (x_rows, tiled(tile, width)),
             (grad_middle, tiled(tile, width)),
             (hot, tiled(tile, clips)),
-            (mod, whole(mod)),
+            (mod, tile_mod(mod)),
         ],
         [
             ((rows, width), BF16, pl.BlockSpec((rows, width), lambda step: (0, 0))),
@@ -678,8 +743,9 @@
         ],
         [
             pltpu.VMEM((rows, width), BF16),
-            pltpu.VMEM(full_attn.shape, BF16),
-            pltpu.SemaphoreType.DMA((2,)),
+            pltpu.VMEM((width, 3 * width), BF16),
+            pltpu.SemaphoreType.DMA((3,)),
+            pltpu.VMEM((tile, width), F32),
         ],
         flops=23 * 10**9,
     )
@@ -915,13 +981,15 @@
                 return Pieces(
                     [gathered[part].reshape(count * rows, width) for part in range(4)],
                     [lambda item, core, part=part: (part, 0, count * rows) for part in range(4)],
-                    (2, count * rows, 2 * width),
+                    (count * rows, 4 * width),
                     True,
+                    False,
                 )
             return Pieces(
                 [gathered[part] for part in range(4)],
                 [lambda item, core, part=part: (part, 0, count) for part in range(4)],
                 (count, 4, rows, width),
+                False,
                 False,
             )
         count, rows, width = gathered.shape
@@ -932,7 +1000,7 @@
         unit = rows if slot_first else 1
         if slot_first:
             arrays = [array.reshape(-1, width) for array in arrays]
-            shape = (2, count * rows, 2 * width)
+            shape = (count * rows, 4 * width)
         else:
             shape = (count, 4, rows, width)
         places = [lambda item, core: (item, 0, count * unit)]
@@ -945,7 +1013,9 @@
                         length * unit,
                     )
                 )
-        return Pieces(arrays, places, shape, slot_first)
+        order = (0, 1, 5, 2, 6, 3, 4, 7, 8)
+        arrays, places = [arrays[at] for at in order], [places[at] for at in order]
+        return Pieces(arrays, places, shape, slot_first, True)
 
 
 class Collect:
@@ -1002,8 +1072,9 @@
 def sum_items(value):
     if not is_square():
         return lax.psum(value.astype(BF16), "item").astype(F32)
-    value = value + swap_x(value.astype(BF16)).astype(F32)
-    return value + swap_y(value.astype(BF16)).astype(F32)
+    low = value.astype(BF16)
+    far = lax.ppermute(low, "item", [(at, at ^ 3) for at in range(4)])
+    return value + swap_x(low).astype(F32) + swap_y(low).astype(F32) + far.astype(F32)
 
 
 def round_up(number, unit):
@@ -1071,7 +1142,7 @@
     x_arrived = x_arrived.reshape(-1, width)
     clip_slots = round_up(clips, 16)
     mod = small_all[:, :clips, :ada_cols].transpose(1, 0, 2).reshape(clips, -1)
-    mod = jnp.pad(mod, ((0, clip_slots - clips), (0, 0)))
+    mod = by_tile(my_rows, mod, frames)
     bias = small_all[:, clips, :bias_cols].reshape(1, -1)
     hot = jnp.pad(my_rows.astype(BF16), ((0, 0), (0, clip_slots - clips)))
     hot = jnp.repeat(hot, frames, axis=0)
@@ -1093,14 +1164,14 @@
     spread_fc2 = Spread(got_fc2, False)
     near_fc1 = spread_fc1.near(*far_attn)
     x_rows, first_in, projected, full_attn = qkv_call(
-        where, x_arrived, hot, mod, spread_attn.pieces(), positions, frames, own_frames
+        where, x_arrived, mod, spread_attn.pieces(), positions, frames, own_frames
     )
     cot_arrived = to_positions(after(cotangent, projected)).reshape(rows, width)
     mixed = attend(after(projected, *near_fc1), positions, frames, attn_scale)
     far_fc1 = spread_fc1.far()
     near_fc2 = spread_fc2.near(*far_fc1)
     attn_out, middle, second_in = out_call(
-        after(mixed, *far_fc1), x_rows, hot, mod, full_attn
+        after(mixed, *far_fc1), x_rows, mod, full_attn, frames
     )
     far_fc2 = spread_fc2.far()
     post_act, slope, full_fc1 = fc1_call(
@@ -1138,7 +1209,7 @@
         part_fc1 = [dot(second_in, part, ROW_DIMS) for part in jnp.split(grad_pre, 4, axis=1)]
         part_fc1 = jnp.stack(part_fc1).reshape(4, frame_count, shard_rows, -1)
     grad_middle, grad_attn, grad_mixed, sums_mlp = fc1_back_call(
-        after(grad_pre, *seen), full_fc1, middle, attn_out, grad_rows, hot, mod, full_attn
+        after(grad_pre, *seen), full_fc1, middle, attn_out, grad_rows, hot, mod, full_attn, frames
     )
     seen = ()
     if square:
@@ -1147,30 +1218,31 @@
         projected, after(grad_mixed, *seen), positions, frames, attn_scale
     )
     block_out = to_frames(block_rows, grad_proj)
+    seen = ()
     if square:
         seen = (*sum_fc2.line(grad_proj), *sum_fc1.far(grad_proj), block_out)
+    token_rows, sums_attn = qkv_back_call(
+        after(grad_proj, *seen), full_attn, x_rows, grad_middle, hot, mod, positions, frames
+    )
+    if square:
+        seen = (token_rows, sum_fc2.own, *sum_fc1.line(token_rows))
         sum_attn = Collect(
             where, *attn_terms(where, first_in, after(grad_proj, *seen), mixed, grad_attn, chips)
         )
-        seen = sum_fc1.line()
-        sum_attn.pair(*seen)
-        seen = (sum_attn.give, sum_fc2.own)
+        sum_attn.pair()
+        sum_attn.near()
+        sum_attn.far()
+        seen = sum_attn.line(sum_fc1.own)
+        last = (sum_attn.own,)
+        grad_tokens = to_frames(token_rows, *seen)
+        sum_fc2, sum_fc1, sum_attn = sum_fc2.finish(*seen), sum_fc1.finish(*seen), sum_attn.finish()
     else:
+        grad_tokens = to_frames(token_rows)
         part_attn = [dot(first_in, part, ROW_DIMS) for part in jnp.split(grad_proj, 3, axis=1)]
         part_attn = jnp.stack([*part_attn, dot(mixed, grad_attn, ROW_DIMS)])
         part_attn = part_attn.reshape(4, frame_count, shard_rows, width)
-    token_rows, sums_attn = qkv_back_call(
-        after(grad_proj, *seen), full_attn, x_rows, grad_middle, hot, mod, positions, frames
-    )
-    if square:
-        sum_attn.near(token_rows, sum_fc1.own)
-        sum_attn.far()
-        seen = sum_attn.line()
-        sum_fc2, sum_fc1, sum_attn = sum_fc2.finish(*seen), sum_fc1.finish(*seen), sum_attn.finish()
-    else:
-        seen = ()
+        seen, last = (), ()
         sum_fc2, sum_fc1, sum_attn = sum_plain(part_fc2), sum_plain(part_fc1), sum_plain(part_attn)
-    grad_tokens = to_frames(token_rows, *seen)
     part_mod = jnp.concatenate([sums_attn, sums_mlp, sum_gate_mlp[None]], axis=0)[:, :clips]
     part_mod = part_mod.transpose(1, 0, 2).reshape(clips, frame_count, ada_cols)
     part_small = jnp.concatenate(
@@ -1184,13 +1256,18 @@
         axis=0,
     ).astype(BF16)
     small_terms = lax.all_to_all(after(part_small, *seen).transpose(1, 0, 2), "frame", 0, 0, tiled=False)
+    small_terms = after(small_terms, *last)
     small_sum = sum_items(jnp.sum(small_terms.astype(F32), axis=0))
     grad_modulation = small_sum[:clips, :ada_cols]
     sum_bias = small_sum[clips, :bias_cols]
-    grad_w_ada = lax.dot_general(activated, grad_modulation, ROW_DIMS, precision=HIGHEST)
     grad_b_ada = jnp.sum(grad_modulation, axis=0)
-    act_part = lax.dot_general(grad_modulation, w_ada.astype(F32), COL_DIMS, precision=HIGHEST)
-    grad_activated = jnp.sum(share_small(act_part.astype(BF16)).astype(F32), axis=0)
+    high = grad_modulation.astype(BF16)
+    low = (grad_modulation - high.astype(F32)).astype(BF16)
+    act_part = (dot(high, w_ada, COL_DIMS) + dot(low, w_ada, COL_DIMS)).astype(BF16)
+    grad_w_ada = lax.dot_general(
+        activated, after(grad_modulation, act_part), ROW_DIMS, precision=HIGHEST
+    )
+    grad_activated = jnp.sum(share_small(act_part).astype(F32), axis=0)
     _, silu_back = jax.vjp(jax.nn.silu, condition)
     grad_condition = silu_back(grad_activated)[0]
     grad_table = lax.dot_general(class_hot, grad_condition, ROW_DIMS, precision=HIGHEST)

time: 642 us -> 628 us (0.978)
  waiting for transfers between devices: 175 us -> 159 us
    reduce_scatter x3, waiting for transfers between devices: 13.2 us -> 0.89 us  [line(): lax.psum_scatter(plane, 'frame', scatter_dimension=0, tiled=False, axis_i...]
    ppermute x15, waiting for transfers between devices: 9.3 us -> 18.4 us  [swap_core(): return lax.ppermute(value, 'frame', [(at, at ^ 1) for at in range(count)])]
    ppermute x16, waiting for transfers between devices: 30.7 us -> 22.3 us  [swap_y(): return lax.ppermute(value, 'item', Y_SWAP)]
  transfers between devices with their start and end apart: 62 -> 63, of which waited for: 20 -> 19; matrix products, arithmetic and copies ran while one was open for 10% -> 11% of each run, Pallas kernels for 40% -> 39%
where the time goes in v3:
time: 628 us; the launch traced here: 618 us
  Pallas kernels  284 us (45%)
  waiting for transfers between devices  159 us (25%)
  starting transfers between devices  80.5 us (13%)
  other arithmetic  34.5 us (5%)
  local copies, waits for them, and re-layouts  34.2 us (5%)
  between operations  15.1 us (2%)
  matrix products  10.8 us (2%)
    pallas_call x10, Pallas kernels, call(): pl.pallas_call(kernel, out_shape=[jax.ShapeDtypeStruct(shape, dtype) for...  211 us
    ppermute x16, waiting for transfers between devices, swap_x(): return lax.ppermute(value, 'item', X_SWAP)  63.2 us
    all_gather x3, waiting for transfers between devices, gather_frame(): return lax.all_gather(pick(parts, lax.axis_index('item')), 'frame', axis=0)  41.3 us
    pallas_call x1, Pallas kernels, attend_back(): pl.pallas_call(lambda *refs: attend_back_kernel(frames, scale, *refs), ou...  29.9 us
    pallas_call x3, Pallas kernels, plane_terms(): pl.pallas_call(kernel, out_shape=[jax.ShapeDtypeStruct(shape, BF16) for s...  23.4 us
    ppermute x16, waiting for transfers between devices, swap_y(): return lax.ppermute(value, 'item', Y_SWAP)  22.3 us
    pallas_call x1, Pallas kernels, attend(): pl.pallas_call(lambda *refs: attend_kernel(frames, scale, *refs), out_sha...  19.7 us
    ppermute x16, starting transfers between devices, swap_y(): return lax.ppermute(value, 'item', Y_SWAP)  19.5 us
  transfers between devices with their start and end apart: 63, of which 19 were waited for; matrix products, arithmetic and copies ran while one was open for 11% of the time, Pallas kernels for 39%

profile of v3, /device:TPU:0, one launch (start us, length us, event | category | flops | bytes accessed | tf_op | source)
XLA Modules:
  0.0 617.6 jit_solution(12923956605747596051)
XLA Ops:
  25.2 41.3 %all-gather.4.cloned.1.call-done = bf16[8,144,1152]{2,1,0:T(8,128)(2,1)} async-done(((bf16[1,144,1152]{2,1,0:T(8,128)(2,1)}), bf16[8,144,1152]{2,1,0:T(8,128)(2,1)}) %all-gather.4.cloned.1.call-update) | async-done | bytes 2654224 | tf_op jit(solution)/shard_map/all_gather | solution.py:949
  70.9 28.5 %collective-permute-done = bf16[4,144,1152]{2,1,0:T(8,128)(2,1)} collective-permute-done((bf16[4,144,1152]{2,1,0:T(8,128)(2,1)S(1)}, bf16[4,144,1152]{2,1,0:T(8,128)(2,1)}, u32[]{:S(2)}, u32[]{:S(2)}) %collective-permute-start) | collective-permute-done | bytes 1327136 | tf_op jit(solution)/shard_map/ppermute | solution.py:914
  106.8 12.3 %all-to-all-done = bf16[8,128,1152]{2,1,0:T(8,128)(2,1)} async-done(((bf16[8,128,1152]{2,1,0:T(8,128)(2,1)}), bf16[8,128,1152]{2,1,0:T(8,128)(2,1)}, u32[]{:S(2)}, u32[]{:S(2)}) %all-to-all-start) | async-done | bytes 2359328 | tf_op jit(solution)/shard_map/all_to_all | solution.py:1117
  130.4 20.3 %project.1 = (bf16[896,1152]{1,0:T(8,128)(2,1)}, bf16[896,1152]{1,0:T(8,128)(2,1)}, bf16[896,3456]{1,0:T(8,128)(2,1)}, bf16[1152,4608]{1,0:T(8,128)(2,1)}) custom-call(s32[3]{0:T(128)} %pad_add_fusion.where_ref, bf16[1024,1152]{1,0:T(8,128)(2,1)} %bitcast.6.x_ref, f32[4,16,6912]{2,1,0:T(8,128)} %fusion.24.mod_ref, bf16[1152,1152]{1,0:T(8,128)(2,1)} %bitcast.138, ...), custom_call_target="tpu_custom_call" | custom-call | flops 20000000000 | bytes 35684364 | tf_op jit(solution)/shard_map/project/pallas_call | solution.py:225
  152.1 9.1 %all-to-all-start.1 = ((bf16[8,112,1152]{2,1,0:T(8,128)(2,1)}), bf16[8,112,1152]{2,1,0:T(8,128)(2,1)}, u32[]{:S(2)}, u32[]{:S(2)}) async-start(bf16[8,112,1152]{2,1,0:T(8,128)(2,1)} %bitcast.129), calls=%async_computation.1 | async-start | bytes 4128768 | tf_op jit(solution)/shard_map/all_to_all | solution.py:1117
  167.5 19.7 %attend.1.mixed_ref = bf16[896,1152]{1,0:T(8,128)(2,1)} custom-call(bf16[896,3456]{1,0:T(8,128)(2,1)} %get-tuple-element.92.refs_0_), custom_call_target="tpu_custom_call" | custom-call | flops 12999999488 | bytes 8257536 | tf_op jit(solution)/shard_map/attend/pallas_call | solution.py:173
  187.8 8.9 %attn_out.1 = (bf16[896,1152]{1,0:T(8,128)(2,1)}, f32[896,1152]{1,0:T(8,128)}, bf16[896,1152]{1,0:T(8,128)(2,1)}) custom-call(bf16[896,1152]{1,0:T(8,128)(2,1)} %attend.1.mixed_ref, bf16[896,1152]{1,0:T(8,128)(2,1)} %get-tuple-element.96.x_ref, f32[4,16,6912]{2,1,0:T(8,128)} %fusion.24.mod_ref, bf16[1152,4608]{1,0:T(8,128)(2,1)} %get-tuple-element.97.w_ref.wo_ref), custom_call_target="tpu_custom_call" | custom-call | flops 8999999488 | bytes 24772608 | tf_op jit(solution)/shard_map/attn_out/pallas_call | solution.py:225
  199.0 23.4 %fc1.1 = (bf16[896,4608]{1,0:T(8,128)(2,1)}, bf16[896,4608]{1,0:T(8,128)(2,1)}, bf16[1152,4608]{1,0:T(8,128)(2,1)}) custom-call(s32[3]{0:T(128)} %pad_add_fusion.where_ref, bf16[896,1152]{1,0:T(8,128)(2,1)} %get-tuple-element.98.x_ref.left_ref, bf16[1,4608]{1,0:T(2,128)(2,1)} %reshape_squeeze.10.bias_ref, bf16[1152,1152]{1,0:T(8,128)(2,1)} %bitcast.137, ...), custom_call_target="tpu_custom_call" | custom-call | flops 24999999488 | bytes 39822348 | tf_op jit(solution)/shard_map/fc1/pallas_call | solution.py:225
  223.1 6.9 %cotangent.1 = (bf16[896,1152]{1,0:T(8,128)(2,1)}, bf16[896,1152]{1,0:T(8,128)(2,1)}) custom-call(bf16[896,1152]{1,0:T(8,128)(2,1)} %bitcast.37.cot_ref, bf16[896,16]{1,0:T(8,128)(2,1)} %bitcast.150, f32[4,16,6912]{2,1,0:T(8,128)} %fusion.24.mod_ref), custom_call_target="tpu_custom_call" | custom-call | flops 6000000000 | bytes 7991296 | tf_op jit(solution)/shard_map/cotangent/pallas_call | solution.py:225
  236.3 17.8 %fc2_terms.1 = (bf16[4,4,144,1152]{3,2,1,0:T(8,128)(2,1)}, bf16[4,4,144,1152]{3,2,1,0:T(8,128)(2,1)}) custom-call(s32[3]{0:T(128)} %pad_add_fusion.where_ref, bf16[896,4608]{1,0:T(8,128)(2,1)} %get-tuple-element.99.left_ref.post_ref, bf16[896,1152]{1,0:T(8,128)(2,1)} %get-tuple-element.108.right_ref.gmlp_ref), custom_call_target="tpu_custom_call" | custom-call | flops 17999998976 | bytes 20938764 | tf_op jit(solution)/shard_map/fc2_terms/pallas_call | solution.py:225
  254.6 7.4 %collective-permute-done.22.rest_7_ = bf16[2,144,1152]{2,1,0:T(8,128)(2,1)S(1)} collective-permute-done((bf16[2,144,1152]{2,1,0:T(8,128)(2,1)}, bf16[2,144,1152]{2,1,0:T(8,128)(2,1)S(1)}, u32[]{:S(2)}, u32[]{:S(2)}) %collective-permute-start.22) | collective-permute-done | bytes 663584 | tf_op jit(solution)/shard_map/ppermute | solution.py:923
  265.6 40.5 %fc2.1 = (bf16[896,1152]{1,0:T(8,128)(2,1)}, bf16[896,4608]{1,0:T(8,128)(2,1)}, f32[1,4608]{1,0:T(1,128)}, f32[16,1152]{1,0:T(8,128)}) custom-call(s32[3]{0:T(128)} %pad_add_fusion.where_ref, bf16[896,4608]{1,0:T(8,128)(2,1)} %get-tuple-element.99.left_ref.post_ref, bf16[896,4608]{1,0:T(8,128)(2,1)} %get-tuple-element.100.slope_ref, ...), custom_call_target="tpu_custom_call" | custom-call | flops 44000002048 | bytes 47601676 | tf_op jit(solution)/shard_map/fc2/pallas_call | solution.py:225
  306.1 7.8 %plane_terms.3 = (bf16[2,2,144,1152]{3,2,1,0:T(8,128)(2,1)}, bf16[2,2,144,1152]{3,2,1,0:T(8,128)(2,1)}, bf16[4,2,144,1152]{3,2,1,0:T(8,128)(2,1)}) custom-call(s32[3]{0:T(128)} %pad_add_fusion.where_ref, bf16[4,4,144,1152]{3,2,1,0:T(8,128)(2,1)} %get-tuple-element.115.keep_ref, bf16[4,4,144,1152]{3,2,1,0:T(8,128)(2,1)} %collective-permute-done.24.got_ref), custom_call_target="tpu_custom_call" | custom-call | flops 7000000000 | bytes 15925248 | tf_op jit(solution)/shard_map/plane_terms/pallas_call | solution.py:890
  313.9 17.9 %fc1_terms.1 = (bf16[4,4,144,1152]{3,2,1,0:T(8,128)(2,1)}, bf16[4,4,144,1152]{3,2,1,0:T(8,128)(2,1)}) custom-call(s32[3]{0:T(128)} %pad_add_fusion.where_ref, bf16[896,1152]{1,0:T(8,128)(2,1)} %get-tuple-element.98.x_ref.left_ref, bf16[896,4608]{1,0:T(8,128)(2,1)} %get-tuple-element.120.right_ref.pre_ref), custom_call_target="tpu_custom_call" | custom-call | flops 17999998976 | bytes 20938764 | tf_op jit(solution)/shard_map/fc1_terms/pallas_call | solution.py:225
  332.5 6.4 %all-to-all-start.2 = ((bf16[8,2,56,1152]{3,2,1,0:T(8,128)(2,1)}), bf16[8,2,56,1152]{3,2,1,0:T(8,128)(2,1)}, u32[]{:S(2)}, u32[]{:S(2)}) async-start(bf16[8,2,56,1152]{3,2,1,0:T(8,128)(2,1)} %bitcast.135), calls=%async_computation.2 | async-start | bytes 4128768 | tf_op jit(solution)/shard_map/all_to_all | solution.py:1121
  341.1 31.4 %fc1_back.1 = (f32[896,1152]{1,0:T(8,128)}, bf16[896,1152]{1,0:T(8,128)(2,1)}, bf16[896,1152]{1,0:T(8,128)(2,1)}, f32[3,16,1152]{2,1,0:T(8,128)}) custom-call(bf16[896,4608]{1,0:T(8,128)(2,1)} %get-tuple-element.120.right_ref.pre_ref, bf16[1152,4608]{1,0:T(8,128)(2,1)} %get-tuple-element.121.w_ref, f32[896,1152]{1,0:T(8,128)} %get-tuple-element.110.mid_ref, ...), custom_call_target="tpu_custom_call" | custom-call | flops 32000000000 | bytes 48025600 | tf_op jit(solution)/shard_map/fc1_back/pallas_call | solution.py:225
  377.3 7.8 %plane_terms.4 = (bf16[2,2,144,1152]{3,2,1,0:T(8,128)(2,1)}, bf16[2,2,144,1152]{3,2,1,0:T(8,128)(2,1)}, bf16[4,2,144,1152]{3,2,1,0:T(8,128)(2,1)}) custom-call(s32[3]{0:T(128)} %pad_add_fusion.where_ref, bf16[4,4,144,1152]{3,2,1,0:T(8,128)(2,1)} %get-tuple-element.128.keep_ref, bf16[4,4,144,1152]{3,2,1,0:T(8,128)(2,1)} %collective-permute-done.27.got_ref), custom_call_target="tpu_custom_call" | custom-call | flops 7000000000 | bytes 15925248 | tf_op jit(solution)/shard_map/plane_terms/pallas_call | solution.py:890
  387.2 29.9 %attend_back.1.proj_ref = bf16[896,3456]{1,0:T(8,128)(2,1)} custom-call(bf16[896,3456]{1,0:T(8,128)(2,1)} %get-tuple-element.92.refs_0_, bf16[896,1152]{1,0:T(8,128)(2,1)} %get-tuple-element.131.refs_1_), custom_call_target="tpu_custom_call" | custom-call | flops 27000000512 | bytes 14450688 | tf_op jit(solution)/shard_map/attend_back/pallas_call | solution.py:190
  428.1 24.4 %project_back.1 = (bf16[896,1152]{1,0:T(8,128)(2,1)}, f32[2,16,1152]{2,1,0:T(8,128)}) custom-call(bf16[896,3456]{1,0:T(8,128)(2,1)} %attend_back.1.proj_ref, bf16[1152,4608]{1,0:T(8,128)(2,1)} %get-tuple-element.97.w_ref.wo_ref, bf16[896,1152]{1,0:T(8,128)(2,1)} %get-tuple-element.96.x_ref, f32[896,1152]{1,0:T(8,128)} %get-tuple-element.140.gmid_ref, ...), custom_call_target="tpu_custom_call" | custom-call | flops 23000000512 | bytes 27013120 | tf_op jit(solution)/shard_map/project_back/pallas_call | solution.py:225
  455.7 19.2 %attn_terms.1 = (bf16[4,4,144,1152]{3,2,1,0:T(8,128)(2,1)}, bf16[4,4,144,1152]{3,2,1,0:T(8,128)(2,1)}) custom-call(s32[3]{0:T(128)} %pad_add_fusion.where_ref, bf16[896,1152]{1,0:T(8,128)(2,1)} %get-tuple-element.142.first_ref, bf16[896,3456]{1,0:T(8,128)(2,1)} %attend_back.1.proj_ref, bf16[896,1152]{1,0:T(8,128)(2,1)} %attend.1.mixed_ref, ...), custom_call_target="tpu_custom_call" | custom-call | flops 19000000512 | bytes 23003148 | tf_op jit(solution)/shard_map/attn_terms/pallas_call | solution.py:225
  474.9 9.1 %collective-permute-done.34.got_ref = bf16[4,4,144,1152]{3,2,1,0:T(8,128)(2,1)} collective-permute-done((bf16[4,4,144,1152]{3,2,1,0:T(8,128)(2,1)}, bf16[4,4,144,1152]{3,2,1,0:T(8,128)(2,1)}, u32[]{:S(2)}, u32[]{:S(2)}) %collective-permute-start.34) | collective-permute-done | bytes 5308448 | tf_op jit(solution)/shard_map/ppermute | solution.py:923
  483.9 7.8 %plane_terms.5 = (bf16[2,2,144,1152]{3,2,1,0:T(8,128)(2,1)}, bf16[2,2,144,1152]{3,2,1,0:T(8,128)(2,1)}, bf16[4,2,144,1152]{3,2,1,0:T(8,128)(2,1)}) custom-call(s32[3]{0:T(128)} %pad_add_fusion.where_ref, bf16[4,4,144,1152]{3,2,1,0:T(8,128)(2,1)} %get-tuple-element.147.keep_ref, bf16[4,4,144,1152]{3,2,1,0:T(8,128)(2,1)} %collective-permute-done.34.got_ref), custom_call_target="tpu_custom_call" | custom-call | flops 7000000000 | bytes 15925248 | tf_op jit(solution)/shard_map/plane_terms/pallas_call | solution.py:890
  498.9 24.2 %collective-permute-done.35 = bf16[2,2,144,1152]{3,2,1,0:T(8,128)(2,1)S(1)} collective-permute-done((bf16[2,2,144,1152]{3,2,1,0:T(8,128)(2,1)}, bf16[2,2,144,1152]{3,2,1,0:T(8,128)(2,1)S(1)}, u32[]{:S(2)}, u32[]{:S(2)}) %collective-permute-start.35) | collective-permute-done | bytes 1327136 | tf_op jit(solution)/shard_map/ppermute | solution.py:914
  529.1 14.0 %collective-permute-done.37 = bf16[2,144,1152]{2,1,0:T(8,128)(2,1)} collective-permute-done((bf16[2,144,1152]{2,1,0:T(8,128)(2,1)}, bf16[2,144,1152]{2,1,0:T(8,128)(2,1)}, u32[]{:S(2)}, u32[]{:S(2)}) %collective-permute-start.37) | collective-permute-done | bytes 663584 | tf_op jit(solution)/shard_map/ppermute | solution.py:918
  (267 shorter events, 166.6 us)
Async XLA Ops:
  7.2 59.3 %all-gather.4.cloned.1.call-start = ((), (), s32[]{:S(2)}) async-start(), calls=%async_computation.9 | async-start | bytes 2985984 | tf_op jit(solution)/shard_map/all_gather | solution.py:949
  11.6 115.2 %all-gather.6.cloned.1.call-start = ((), (), s32[]{:S(2)}) async-start(), calls=%async_computation.10 | async-start | bytes 2985984 | tf_op jit(solution)/shard_map/all_gather | solution.py:949
  18.8 100.4 %all-to-all-start = ((bf16[8,128,1152]{2,1,0:T(8,128)(2,1)}), bf16[8,128,1152]{2,1,0:T(8,128)(2,1)}, u32[]{:S(2)}, u32[]{:S(2)}) async-start(bf16[8,128,1152]{2,1,0:T(8,128)(2,1)} %pad_maximum_fusion), calls=%async_computation | async-start | bytes 4718592 | tf_op jit(solution)/shard_map/all_to_all | solution.py:1117
  25.1 171.6 %all-gather.8.cloned.1.call-start = ((), (), s32[]{:S(2)}) async-start(), calls=%async_computation.11 | async-start | bytes 2985984 | tf_op jit(solution)/shard_map/all_gather | solution.py:949
  128.3 32.9 %collective-permute-start.8 = (bf16[4,144,1152]{2,1,0:T(8,128)(2,1)S(1)}, bf16[4,144,1152]{2,1,0:T(8,128)(2,1)}, u32[]{:S(2)}, u32[]{:S(2)}) collective-permute-start(bf16[4,144,1152]{2,1,0:T(8,128)(2,1)S(1)} %constant_dynamic-slice_fusion.6), channel_id=1, source_target_pairs={{0,8},{8,0},{16,24},{24,16},{1,9},{9,1},{17,25},{25,17},{2,10},{10... | collective-permute-start | bytes 3981320 | tf_op jit(solution)/shard_map/ppermute | solution.py:914
  129.0 32.2 %collective-permute-start.9 = (bf16[4,144,1152]{2,1,0:T(8,128)(2,1)S(1)}, bf16[4,144,1152]{2,1,0:T(8,128)(2,1)}, u32[]{:S(2)}, u32[]{:S(2)}) collective-permute-start(bf16[4,144,1152]{2,1,0:T(8,128)(2,1)S(1)} %constant_dynamic-slice_fusion.6), channel_id=1, source_target_pairs={{0,16},{16,0},{8,24},{24,8},{1,17},{17,1},{9,25},{25,9},{2,18},{18... | collective-permute-start | bytes 3981320 | tf_op jit(solution)/shard_map/ppermute | solution.py:918
  152.1 70.3 %all-to-all-start.1 = ((bf16[8,112,1152]{2,1,0:T(8,128)(2,1)}), bf16[8,112,1152]{2,1,0:T(8,128)(2,1)}, u32[]{:S(2)}, u32[]{:S(2)}) async-start(bf16[8,112,1152]{2,1,0:T(8,128)(2,1)} %bitcast.129), calls=%async_computation.1 | async-start | bytes 4128768 | tf_op jit(solution)/shard_map/all_to_all | solution.py:1117
  162.4 36.6 %collective-permute-start.12 = (bf16[4,144,1152]{2,1,0:T(8,128)(2,1)}, bf16[4,144,1152]{2,1,0:T(8,128)(2,1)}, u32[]{:S(2)}, u32[]{:S(2)}) collective-permute-start(bf16[4,144,1152]{2,1,0:T(8,128)(2,1)} %collective-permute-done.8), channel_id=1, source_target_pairs={{0,1},{1,0},{2,3},{3,2},{4,5},{5,4},{6,7},{7,6},{8,9},{9,8},{10,11... | collective-permute-start | bytes 3981320 | tf_op jit(solution)/shard_map/ppermute | solution.py:923
  164.1 34.9 %collective-permute-start.13 = (bf16[4,144,1152]{2,1,0:T(8,128)(2,1)}, bf16[4,144,1152]{2,1,0:T(8,128)(2,1)}, u32[]{:S(2)}, u32[]{:S(2)}) collective-permute-start(bf16[4,144,1152]{2,1,0:T(8,128)(2,1)} %collective-permute-done.9), channel_id=1, source_target_pairs={{0,1},{1,0},{2,3},{3,2},{4,5},{5,4},{6,7},{7,6},{8,9},{9,8},{10,11... | collective-permute-start | bytes 3981320 | tf_op jit(solution)/shard_map/ppermute | solution.py:923
  198.1 31.9 %collective-permute-start.16 = (bf16[4,144,1152]{2,1,0:T(8,128)(2,1)S(1)}, bf16[4,144,1152]{2,1,0:T(8,128)(2,1)}, u32[]{:S(2)}, u32[]{:S(2)}) collective-permute-start(bf16[4,144,1152]{2,1,0:T(8,128)(2,1)S(1)} %constant_dynamic-slice_fusion.4), channel_id=1, source_target_pairs={{0,8},{8,0},{16,24},{24,16},{1,9},{9,1},{17,25},{25,17},{2,10},{10... | collective-permute-start | bytes 3981320 | tf_op jit(solution)/shard_map/ppermute | solution.py:914
  231.2 32.8 %collective-permute-start.18 = (bf16[4,144,1152]{2,1,0:T(8,128)(2,1)}, bf16[4,144,1152]{2,1,0:T(8,128)(2,1)S(1)}, u32[]{:S(2)}, u32[]{:S(2)}) collective-permute-start(bf16[4,144,1152]{2,1,0:T(8,128)(2,1)} %collective-permute-done.16.rest_1_), channel_id=1, source_target_pairs={{0,1},{1,0},{2,3},{3,2},{4,5},{5,4},{6,7},{7,6},{8,9},{9,8},{10,11... | collective-permute-start | bytes 3981320 | tf_op jit(solution)/shard_map/ppermute | solution.py:923
  254.0 52.1 %collective-permute-start.24 = (bf16[4,4,144,1152]{3,2,1,0:T(8,128)(2,1)}, bf16[4,4,144,1152]{3,2,1,0:T(8,128)(2,1)}, u32[]{:S(2)}, u32[]{:S(2)}) collective-permute-start(bf16[4,4,144,1152]{3,2,1,0:T(8,128)(2,1)} %get-tuple-element.107), channel_id=1, source_target_pairs={{0,1},{1,0},{2,3},{3,2},{4,5},{5,4},{6,7},{7,6},{8,9},{9,8},{10,11... | collective-permute-start | bytes 15925256 | tf_op jit(solution)/shard_map/ppermute | solution.py:923
  331.8 45.6 %collective-permute-start.27 = (bf16[4,4,144,1152]{3,2,1,0:T(8,128)(2,1)}, bf16[4,4,144,1152]{3,2,1,0:T(8,128)(2,1)}, u32[]{:S(2)}, u32[]{:S(2)}) collective-permute-start(bf16[4,4,144,1152]{3,2,1,0:T(8,128)(2,1)} %get-tuple-element.119), channel_id=1, source_target_pairs={{0,1},{1,0},{2,3},{3,2},{4,5},{5,4},{6,7},{7,6},{8,9},{9,8},{10,11... | collective-permute-start | bytes 15925256 | tf_op jit(solution)/shard_map/ppermute | solution.py:923
  332.5 84.6 %all-to-all-start.2 = ((bf16[8,2,56,1152]{3,2,1,0:T(8,128)(2,1)}), bf16[8,2,56,1152]{3,2,1,0:T(8,128)(2,1)}, u32[]{:S(2)}, u32[]{:S(2)}) async-start(bf16[8,2,56,1152]{3,2,1,0:T(8,128)(2,1)} %bitcast.135), calls=%async_computation.2 | async-start | bytes 4128768 | tf_op jit(solution)/shard_map/all_to_all | solution.py:1121
  339.0 116.7 %reduce-scatter.4.cloned.1.call-start = ((), (), s32[]{:S(2)}) async-start(), calls=%async_computation.12 | async-start | bytes 1658880 | tf_op jit(solution)/shard_map/reduce_scatter | solution.py:1048
  339.0 33.5 %collective-permute-start.25 = (bf16[2,2,144,1152]{3,2,1,0:T(8,128)(2,1)}, bf16[2,2,144,1152]{3,2,1,0:T(8,128)(2,1)S(1)}, u32[]{:S(2)}, u32[]{:S(2)}) collective-permute-start(bf16[2,2,144,1152]{3,2,1,0:T(8,128)(2,1)} %get-tuple-element.124), channel_id=1, source_target_pairs={{0,8},{8,0},{16,24},{24,16},{1,9},{9,1},{17,25},{25,17},{2,10},{10... | collective-permute-start | bytes 3981320 | tf_op jit(solution)/shard_map/ppermute | solution.py:914
  340.2 32.4 %collective-permute-start.26 = (bf16[2,2,144,1152]{3,2,1,0:T(8,128)(2,1)}, bf16[2,2,144,1152]{3,2,1,0:T(8,128)(2,1)}, u32[]{:S(2)}, u32[]{:S(2)}) collective-permute-start(bf16[2,2,144,1152]{3,2,1,0:T(8,128)(2,1)} %get-tuple-element.125), channel_id=1, source_target_pairs={{0,16},{16,0},{8,24},{24,8},{1,17},{17,1},{9,25},{25,9},{2,18},{18... | collective-permute-start | bytes 3981320 | tf_op jit(solution)/shard_map/ppermute | solution.py:918
  375.3 41.8 %collective-permute-start.28 = (bf16[2,144,1152]{2,1,0:T(8,128)(2,1)}, bf16[2,144,1152]{2,1,0:T(8,128)(2,1)}, u32[]{:S(2)}, u32[]{:S(2)}) collective-permute-start(bf16[2,144,1152]{2,1,0:T(8,128)(2,1)} %get-tuple-element.177), channel_id=1, source_target_pairs={{0,16},{16,0},{8,24},{24,8},{1,17},{17,1},{9,25},{25,9},{2,18},{18... | collective-permute-start | bytes 1990664 | tf_op jit(solution)/shard_map/ppermute | solution.py:918
  376.4 40.7 %collective-permute-start.29 = (bf16[2,144,1152]{2,1,0:T(8,128)(2,1)}, bf16[2,144,1152]{2,1,0:T(8,128)(2,1)}, u32[]{:S(2)}, u32[]{:S(2)}) collective-permute-start(bf16[2,144,1152]{2,1,0:T(8,128)(2,1)} %get-tuple-element.176), channel_id=1, source_target_pairs={{0,8},{8,0},{16,24},{24,16},{1,9},{9,1},{17,25},{25,17},{2,10},{10... | collective-permute-start | bytes 1990664 | tf_op jit(solution)/shard_map/ppermute | solution.py:914
  385.1 38.3 %collective-permute-start.30 = (bf16[2,2,144,1152]{3,2,1,0:T(8,128)(2,1)}, bf16[2,2,144,1152]{3,2,1,0:T(8,128)(2,1)S(1)}, u32[]{:S(2)}, u32[]{:S(2)}) collective-permute-start(bf16[2,2,144,1152]{3,2,1,0:T(8,128)(2,1)} %get-tuple-element.135), channel_id=1, source_target_pairs={{0,8},{8,0},{16,24},{24,16},{1,9},{9,1},{17,25},{25,17},{2,10},{10... | collective-permute-start | bytes 3981320 | tf_op jit(solution)/shard_map/ppermute | solution.py:914
  386.2 37.2 %collective-permute-start.31 = (bf16[2,2,144,1152]{3,2,1,0:T(8,128)(2,1)}, bf16[2,2,144,1152]{3,2,1,0:T(8,128)(2,1)}, u32[]{:S(2)}, u32[]{:S(2)}) collective-permute-start(bf16[2,2,144,1152]{3,2,1,0:T(8,128)(2,1)} %get-tuple-element.136), channel_id=1, source_target_pairs={{0,16},{16,0},{8,24},{24,8},{1,17},{17,1},{9,25},{25,9},{2,18},{18... | collective-permute-start | bytes 3981320 | tf_op jit(solution)/shard_map/ppermute | solution.py:918
  423.4 105.7 %reduce-scatter.6.cloned.1.call-start = ((), (), s32[]{:S(2)}) async-start(), calls=%async_computation.13 | async-start | bytes 1658880 | tf_op jit(solution)/shard_map/reduce_scatter | solution.py:1048
  494.5 66.3 %all-to-all-start.3 = ((bf16[8,2,56,1152]{3,2,1,0:T(8,128)(2,1)}), bf16[8,2,56,1152]{3,2,1,0:T(8,128)(2,1)}, u32[]{:S(2)}, u32[]{:S(2)}) async-start(bf16[8,2,56,1152]{3,2,1,0:T(8,128)(2,1)} %bitcast.133), calls=%async_computation.3 | async-start | bytes 4128768 | tf_op jit(solution)/shard_map/all_to_all | solution.py:1121
  498.9 84.0 %reduce-scatter.8.cloned.1.call-start = ((), (), s32[]{:S(2)}) async-start(), calls=%async_computation.14 | async-start | bytes 1658880 | tf_op jit(solution)/shard_map/reduce_scatter | solution.py:1048
  (69 other events, 922.8 us)
Sparse Core Ops, SparseCore 0:
  11.7 54.6 all-gather.3
  68.7 50.7 all-gather.5
  122.0 38.2 all-gather.7
  423.5 31.9 reduce-scatter.3
  475.0 34.1 reduce-scatter.5
  547.8 35.0 reduce-scatter.7

commit v4 on v3

--- a/solution.py
+++ b/solution.py
@@ -49,22 +49,32 @@
 LANES = 128
 
 
-def head_windows(heads, head_dim):
+def pair_windows(heads, head_dim):
     windows = []
-    for head in range(heads):
-        low, high = head * head_dim, (head + 1) * head_dim
-        windows.append((low // LANES * LANES, -(-high // LANES) * LANES, low, high))
+    for head in range(0, heads, 2):
+        low, high = head * head_dim, (head + 2) * head_dim
+        start, end = low // LANES * LANES, -(-high // LANES) * LANES
+        windows.append((start, end, low, low + head_dim, high))
     return windows
 
 
-def lane_mask(window):
-    start, end, low, high = window
+def stacked(value, window):
+    start, end, first, second, last = window
     lanes = start + lax.broadcasted_iota(jnp.int32, (1, end - start), 1)
-    return ((lanes >= low) & (lanes < high)).astype(jnp.float32).astype(jnp.bfloat16)
+    masks = [
+        ((lanes >= low) & (lanes < high)).astype(jnp.float32).astype(jnp.bfloat16)
+        for low, high in ((first, second), (second, last))
+    ]
+    return jnp.concatenate([value * mask for mask in masks], axis=0)
+
+
+def tall(wide):
+    half = wide.shape[1] // 2
+    return jnp.concatenate([wide[:, :half], wide[:, half:]], axis=0)
 
 
 def add_window(totals, window, value):
-    start, end, _, _ = window
+    start, end = window[:2]
     for lane in range(start, end, LANES):
         piece = value[:, lane - start : lane - start + LANES]
         totals[lane] = piece if lane not in totals else totals[lane] + piece
@@ -76,9 +86,9 @@
 
 class Spots:
     def __init__(self, rows, frames):
-        self.frames = frames
-        spot = lax.broadcasted_iota(jnp.int32, (frames, rows), 1) // frames
-        self.own = [spot == at for at in range(rows // frames)]
+        self.frames, count = frames, rows // frames
+        spot = lax.broadcasted_iota(jnp.int32, (frames, 2 * rows), 1) // frames % count
+        self.own = [spot == at for at in range(count)]
         self.masks = [own.astype(jnp.float32).astype(jnp.bfloat16) for own in self.own]
 
     def compact(self, full):
@@ -90,9 +100,19 @@
     def expand(self, compact):
         return jnp.concatenate([compact * mask for mask in self.masks], axis=0)
 
-    def probs(self, queries, keys, scale):
-        scores = lax.dot_general(keys, queries, COL_DIMS, preferred_element_type=jnp.float32)
-        scores = self.compact(scores) * scale
+    def blocks(self, pairs):
+        return jnp.concatenate(
+            [
+                self.compact(
+                    lax.dot_general(left, right, COL_DIMS, preferred_element_type=jnp.float32)
+                )
+                for left, right in pairs
+            ],
+            axis=1,
+        )
+
+    def probs(self, pairs, scale):
+        scores = self.blocks(pairs) * scale
         weights = jnp.exp(scores - jnp.max(scores, axis=0, keepdims=True))
         return weights / jnp.sum(weights, axis=0, keepdims=True)
 
@@ -100,19 +120,23 @@
 def attend_kernel(frames, scale, proj_ref, mixed_ref):
     rows, width = mixed_ref.shape
     spots = Spots(rows, frames)
+    windows = pair_windows(HEADS, width // HEADS)
+
+    def part(index, window):
+        return proj_ref[:, index * width + window[0] : index * width + window[1]]
+
+    prob = spots.probs(
+        [(part(1, window), stacked(part(0, window), window)) for window in windows], scale
+    ).astype(jnp.bfloat16)
     totals = {}
-    for window in head_windows(HEADS, width // HEADS):
-        query, key, value = [
-            slice(part * width + window[0], part * width + window[1]) for part in range(3)
-        ]
-        mask = lane_mask(window)
-        prob = spots.probs(proj_ref[:, query] * mask, proj_ref[:, key], scale)
+    for at, window in enumerate(windows):
+        wide = spots.expand(prob[:, at * 2 * rows : (at + 1) * 2 * rows])
         add_window(
             totals,
             window,
             lax.dot_general(
-                spots.expand(prob.astype(jnp.bfloat16)),
-                proj_ref[:, value] * mask,
+                tall(wide),
+                stacked(part(2, window), window),
                 ROW_DIMS,
                 preferred_element_type=jnp.float32,
             ),
@@ -123,36 +147,47 @@
 def attend_back_kernel(frames, scale, proj_ref, grad_ref, out_ref):
     rows, width = grad_ref.shape
     spots = Spots(rows, frames)
+    windows = pair_windows(HEADS, width // HEADS)
+
+    def part(index, window):
+        return proj_ref[:, index * width + window[0] : index * width + window[1]]
+
+    def grads(window):
+        return stacked(grad_ref[:, window[0] : window[1]], window)
+
+    prob = spots.probs(
+        [(part(1, window), stacked(part(0, window), window)) for window in windows], scale
+    )
+    grad_prob = spots.blocks([(part(2, window), grads(window)) for window in windows])
+    weighted = prob * grad_prob
+    grad_scores = weighted - prob * jnp.sum(weighted, axis=0, keepdims=True)
+    grad_scores, prob = grad_scores.astype(jnp.bfloat16), prob.astype(jnp.bfloat16)
     to_query, to_key, to_value = {}, {}, {}
-    for window in head_windows(HEADS, width // HEADS):
-        query, key, value = [
-            slice(part * width + window[0], part * width + window[1]) for part in range(3)
-        ]
-        mask = lane_mask(window)
-        queries = proj_ref[:, query] * mask
-        keys = proj_ref[:, key]
-        grads = grad_ref[:, window[0] : window[1]] * mask
-        prob = spots.probs(queries, keys, scale)
-        grad_prob = spots.compact(
-            lax.dot_general(
-                proj_ref[:, value], grads, COL_DIMS, preferred_element_type=jnp.float32
-            )
-        )
-        weighted = prob * grad_prob
-        grad_scores = weighted - prob * jnp.sum(weighted, axis=0, keepdims=True)
-        grad_scores = spots.expand(grad_scores.astype(jnp.bfloat16))
-        prob_low = spots.expand(prob.astype(jnp.bfloat16))
+    for at, window in enumerate(windows):
+        span = slice(at * 2 * rows, (at + 1) * 2 * rows)
+        wide = spots.expand(grad_scores[:, span])
         add_window(
-            to_value, window, jnp.dot(prob_low, grads, preferred_element_type=jnp.float32)
+            to_value,
+            window,
+            jnp.dot(
+                spots.expand(prob[:, span]), grads(window), preferred_element_type=jnp.float32
+            ),
         )
         add_window(
-            to_key, window, jnp.dot(grad_scores, queries, preferred_element_type=jnp.float32)
+            to_key,
+            window,
+            jnp.dot(
+                wide, stacked(part(0, window), window), preferred_element_type=jnp.float32
+            ),
         )
         add_window(
             to_query,
             window,
             lax.dot_general(
-                grad_scores, keys * mask, ROW_DIMS, preferred_element_type=jnp.float32
+                tall(wide),
+                stacked(part(1, window), window),
+                ROW_DIMS,
+                preferred_element_type=jnp.float32,
             ),
         )
     out_ref[:, :width] = (joined(to_query) * scale).astype(jnp.bfloat16)
@@ -177,7 +212,7 @@
         in_specs=[pl.BlockSpec((tile, 3 * width), lambda step: (step, 0))],
         out_specs=pl.BlockSpec((tile, width), lambda step: (step, 0)),
         cost_estimate=pl.CostEstimate(
-            flops=13 * 10**9, bytes_accessed=8 * rows * width, transcendentals=0
+            flops=9 * 10**9, bytes_accessed=8 * rows * width, transcendentals=0
         ),
         compiler_params=pltpu.CompilerParams(vmem_limit_bytes=VMEM_LIMIT),
         name="attend",
@@ -197,7 +232,7 @@
         ],
         out_specs=pl.BlockSpec((tile, 3 * width), lambda step: (step, 0)),
         cost_estimate=pl.CostEstimate(
-            flops=27 * 10**9, bytes_accessed=14 * rows * width, transcendentals=0
+            flops=12 * 10**9, bytes_accessed=14 * rows * width, transcendentals=0
         ),
         compiler_params=pltpu.CompilerParams(vmem_limit_bytes=VMEM_LIMIT),
         name="attend_back",
@@ -1220,16 +1255,17 @@
     block_out = to_frames(block_rows, grad_proj)
     seen = ()
     if square:
-        seen = (*sum_fc2.line(grad_proj), *sum_fc1.far(grad_proj), block_out)
+        seen = (*sum_fc2.line(grad_proj), block_out)
     token_rows, sums_attn = qkv_back_call(
         after(grad_proj, *seen), full_attn, x_rows, grad_middle, hot, mod, positions, frames
     )
     if square:
-        seen = (token_rows, sum_fc2.own, *sum_fc1.line(token_rows))
+        seen = (token_rows, sum_fc2.own, *sum_fc1.far(token_rows))
         sum_attn = Collect(
             where, *attn_terms(where, first_in, after(grad_proj, *seen), mixed, grad_attn, chips)
         )
         sum_attn.pair()
+        sum_fc1.line(sum_attn.give)
         sum_attn.near()
         sum_attn.far()
         seen = sum_attn.line(sum_fc1.own)

time: 628 us -> 619 us (0.986)
  Pallas kernels: 284 us -> 255 us
  waiting for transfers between devices: 159 us -> 184 us
    pallas_call x1, Pallas kernels: 29.9 us -> 12 us  [attend_back(): pl.pallas_call(lambda *refs: attend_back_kernel(frames, scale, *refs), ou...]
    ppermute x16, waiting for transfers between devices: 22.3 us -> 39.9 us  [swap_y(): return lax.ppermute(value, 'item', Y_SWAP)]
    pallas_call x1, Pallas kernels: 19.7 us -> 8.89 us  [attend(): pl.pallas_call(lambda *refs: attend_kernel(frames, scale, *refs), out_sha...]
    all_to_all x2, waiting for transfers between devices: 0.01 us -> 10.2 us  [to_frames(): moved = after(lax.all_to_all(chunks, 'frame', 0, 0, tiled=True), *wait_for)]
    ppermute x15, waiting for transfers between devices: 18.4 us -> 9.36 us  [swap_core(): return lax.ppermute(value, 'frame', [(at, at ^ 1) for at in range(count)])]
  transfers between devices with their start and end apart: 63 -> 63, of which waited for: 19 -> 21; matrix products, arithmetic and copies ran while one was open for 11% -> 10% of each run, Pallas kernels for 39% -> 35%
where the time goes in v4:
time: 619 us; the launch traced here: 608 us
  Pallas kernels  255 us (41%)
  waiting for transfers between devices  184 us (30%)
  starting transfers between devices  78.2 us (13%)
  other arithmetic  33.1 us (5%)
  local copies, waits for them, and re-layouts  32 us (5%)
  between operations  15.1 us (2%)
  matrix products  10.8 us (2%)
    pallas_call x10, Pallas kernels, call(): pl.pallas_call(kernel, out_shape=[jax.ShapeDtypeStruct(shape, dtype) for...  211 us
    ppermute x16, waiting for transfers between devices, swap_x(): return lax.ppermute(value, 'item', X_SWAP)  63.6 us
    all_gather x3, waiting for transfers between devices, gather_frame(): return lax.all_gather(pick(parts, lax.axis_index('item')), 'frame', axis=0)  41.3 us
    ppermute x16, waiting for transfers between devices, swap_y(): return lax.ppermute(value, 'item', Y_SWAP)  39.9 us
    pallas_call x3, Pallas kernels, plane_terms(): pl.pallas_call(kernel, out_shape=[jax.ShapeDtypeStruct(shape, BF16) for s...  23.4 us
    ppermute x16, starting transfers between devices, swap_y(): return lax.ppermute(value, 'item', Y_SWAP)  19.4 us
    ppermute x16, starting transfers between devices, swap_x(): return lax.ppermute(value, 'item', X_SWAP)  17.7 us
    all_to_all x2, waiting for transfers between devices, to_positions(): return lax.all_to_all(chunks, 'frame', 0, 0, tiled=True)  15.7 us
  transfers between devices with their start and end apart: 63, of which 21 were waited for; matrix products, arithmetic and copies ran while one was open for 10% of the time, Pallas kernels for 35%

profile of v4, /device:TPU:0, one launch (start us, length us, event | category | flops | bytes accessed | tf_op | source)
XLA Modules:
  0.0 608.3 jit_solution(14232350301052947891)
XLA Ops:
  25.2 41.3 %all-gather.4.cloned.1.call-done = bf16[8,144,1152]{2,1,0:T(8,128)(2,1)} async-done(((bf16[1,144,1152]{2,1,0:T(8,128)(2,1)}), bf16[8,144,1152]{2,1,0:T(8,128)(2,1)}) %all-gather.4.cloned.1.call-update) | async-done | bytes 2654224 | tf_op jit(solution)/shard_map/all_gather | solution.py:984
  70.9 28.4 %collective-permute-done = bf16[4,144,1152]{2,1,0:T(8,128)(2,1)S(1)} collective-permute-done((bf16[4,144,1152]{2,1,0:T(8,128)(2,1)S(1)}, bf16[4,144,1152]{2,1,0:T(8,128)(2,1)S(1)}, u32[]{:S(2)}, u32[]{:S(2)}) %collective-permute-start) | collective-permute-done | bytes 1327136 | tf_op jit(solution)/shard_map/ppermute | solution.py:949
  103.5 15.7 %all-to-all-done = bf16[8,128,1152]{2,1,0:T(8,128)(2,1)} async-done(((bf16[8,128,1152]{2,1,0:T(8,128)(2,1)}), bf16[8,128,1152]{2,1,0:T(8,128)(2,1)}, u32[]{:S(2)}, u32[]{:S(2)}) %all-to-all-start) | async-done | bytes 2359328 | tf_op jit(solution)/shard_map/all_to_all | solution.py:1152
  131.4 20.3 %project.1 = (bf16[896,1152]{1,0:T(8,128)(2,1)}, bf16[896,1152]{1,0:T(8,128)(2,1)}, bf16[896,3456]{1,0:T(8,128)(2,1)}, bf16[1152,4608]{1,0:T(8,128)(2,1)}) custom-call(s32[3]{0:T(128)} %pad_add_fusion.where_ref, bf16[1024,1152]{1,0:T(8,128)(2,1)} %bitcast.6.x_ref, f32[4,16,6912]{2,1,0:T(8,128)} %fusion.24.mod_ref, bf16[1152,1152]{1,0:T(8,128)(2,1)} %bitcast.138, ...), custom_call_target="tpu_custom_call" | custom-call | flops 20000000000 | bytes 35684364 | tf_op jit(solution)/shard_map/project/pallas_call | solution.py:260
  153.2 7.4 %all-to-all-start.1 = ((bf16[8,112,1152]{2,1,0:T(8,128)(2,1)}), bf16[8,112,1152]{2,1,0:T(8,128)(2,1)}, u32[]{:S(2)}, u32[]{:S(2)}) async-start(bf16[8,112,1152]{2,1,0:T(8,128)(2,1)} %bitcast.129), calls=%async_computation.1 | async-start | bytes 4128768 | tf_op jit(solution)/shard_map/all_to_all | solution.py:1152
  166.4 8.9 %attend.1.mixed_ref = bf16[896,1152]{1,0:T(8,128)(2,1)} custom-call(bf16[896,3456]{1,0:T(8,128)(2,1)} %get-tuple-element.92.refs_0_), custom_call_target="tpu_custom_call" | custom-call | flops 8999999488 | bytes 8257536 | tf_op jit(solution)/shard_map/attend/pallas_call | solution.py:208
  182.5 8.9 %attn_out.1 = (bf16[896,1152]{1,0:T(8,128)(2,1)}, f32[896,1152]{1,0:T(8,128)}, bf16[896,1152]{1,0:T(8,128)(2,1)}) custom-call(bf16[896,1152]{1,0:T(8,128)(2,1)} %attend.1.mixed_ref, bf16[896,1152]{1,0:T(8,128)(2,1)} %get-tuple-element.96.x_ref, f32[4,16,6912]{2,1,0:T(8,128)} %fusion.24.mod_ref, bf16[1152,4608]{1,0:T(8,128)(2,1)} %get-tuple-element.97.w_ref.wo_ref), custom_call_target="tpu_custom_call" | custom-call | flops 8999999488 | bytes 24772608 | tf_op jit(solution)/shard_map/attn_out/pallas_call | solution.py:260
  195.1 23.4 %fc1.1 = (bf16[896,4608]{1,0:T(8,128)(2,1)}, bf16[896,4608]{1,0:T(8,128)(2,1)}, bf16[1152,4608]{1,0:T(8,128)(2,1)}) custom-call(s32[3]{0:T(128)} %pad_add_fusion.where_ref, bf16[896,1152]{1,0:T(8,128)(2,1)} %get-tuple-element.98.x_ref.left_ref, bf16[1,4608]{1,0:T(2,128)(2,1)} %reshape_squeeze.10.bias_ref, bf16[1152,1152]{1,0:T(8,128)(2,1)} %bitcast.137, ...), custom_call_target="tpu_custom_call" | custom-call | flops 24999999488 | bytes 39822348 | tf_op jit(solution)/shard_map/fc1/pallas_call | solution.py:260
  230.9 17.8 %fc2_terms.1 = (bf16[4,4,144,1152]{3,2,1,0:T(8,128)(2,1)}, bf16[4,4,144,1152]{3,2,1,0:T(8,128)(2,1)}) custom-call(s32[3]{0:T(128)} %pad_add_fusion.where_ref, bf16[896,4608]{1,0:T(8,128)(2,1)} %get-tuple-element.99.left_ref.post_ref, bf16[896,1152]{1,0:T(8,128)(2,1)} %get-tuple-element.108.right_ref.gmlp_ref), custom_call_target="tpu_custom_call" | custom-call | flops 17999998976 | bytes 20938764 | tf_op jit(solution)/shard_map/fc2_terms/pallas_call | solution.py:260
  249.3 7.4 %collective-permute-done.22.rest_7_ = bf16[2,144,1152]{2,1,0:T(8,128)(2,1)S(1)} collective-permute-done((bf16[2,144,1152]{2,1,0:T(8,128)(2,1)}, bf16[2,144,1152]{2,1,0:T(8,128)(2,1)S(1)}, u32[]{:S(2)}, u32[]{:S(2)}) %collective-permute-start.22) | collective-permute-done | bytes 663584 | tf_op jit(solution)/shard_map/ppermute | solution.py:958
  260.4 40.2 %fc2.1 = (bf16[896,1152]{1,0:T(8,128)(2,1)}, bf16[896,4608]{1,0:T(8,128)(2,1)}, f32[1,4608]{1,0:T(1,128)}, f32[16,1152]{1,0:T(8,128)}) custom-call(s32[3]{0:T(128)} %pad_add_fusion.where_ref, bf16[896,4608]{1,0:T(8,128)(2,1)} %get-tuple-element.99.left_ref.post_ref, bf16[896,4608]{1,0:T(8,128)(2,1)} %get-tuple-element.100.slope_ref, ...), custom_call_target="tpu_custom_call" | custom-call | flops 44000002048 | bytes 47601676 | tf_op jit(solution)/shard_map/fc2/pallas_call | solution.py:260
  300.6 7.8 %plane_terms.3 = (bf16[2,2,144,1152]{3,2,1,0:T(8,128)(2,1)}, bf16[2,2,144,1152]{3,2,1,0:T(8,128)(2,1)}, bf16[4,2,144,1152]{3,2,1,0:T(8,128)(2,1)}) custom-call(s32[3]{0:T(128)} %pad_add_fusion.where_ref, bf16[4,4,144,1152]{3,2,1,0:T(8,128)(2,1)} %get-tuple-element.115.keep_ref, bf16[4,4,144,1152]{3,2,1,0:T(8,128)(2,1)} %collective-permute-done.24.got_ref), custom_call_target="tpu_custom_call" | custom-call | flops 7000000000 | bytes 15925248 | tf_op jit(solution)/shard_map/plane_terms/pallas_call | solution.py:925
  308.4 17.8 %fc1_terms.1 = (bf16[4,4,144,1152]{3,2,1,0:T(8,128)(2,1)}, bf16[4,4,144,1152]{3,2,1,0:T(8,128)(2,1)}) custom-call(s32[3]{0:T(128)} %pad_add_fusion.where_ref, bf16[896,1152]{1,0:T(8,128)(2,1)} %get-tuple-element.98.x_ref.left_ref, bf16[896,4608]{1,0:T(8,128)(2,1)} %get-tuple-element.120.right_ref.pre_ref), custom_call_target="tpu_custom_call" | custom-call | flops 17999998976 | bytes 20938764 | tf_op jit(solution)/shard_map/fc1_terms/pallas_call | solution.py:260
  327.0 7.1 %all-to-all-start.2 = ((bf16[8,2,56,1152]{3,2,1,0:T(8,128)(2,1)}), bf16[8,2,56,1152]{3,2,1,0:T(8,128)(2,1)}, u32[]{:S(2)}, u32[]{:S(2)}) async-start(bf16[8,2,56,1152]{3,2,1,0:T(8,128)(2,1)} %bitcast.135), calls=%async_computation.2 | async-start | bytes 4128768 | tf_op jit(solution)/shard_map/all_to_all | solution.py:1156
  336.1 31.4 %fc1_back.1 = (f32[896,1152]{1,0:T(8,128)}, bf16[896,1152]{1,0:T(8,128)(2,1)}, bf16[896,1152]{1,0:T(8,128)(2,1)}, f32[3,16,1152]{2,1,0:T(8,128)}) custom-call(bf16[896,4608]{1,0:T(8,128)(2,1)} %get-tuple-element.120.right_ref.pre_ref, bf16[1152,4608]{1,0:T(8,128)(2,1)} %get-tuple-element.121.w_ref, f32[896,1152]{1,0:T(8,128)} %get-tuple-element.110.mid_ref, ...), custom_call_target="tpu_custom_call" | custom-call | flops 32000000000 | bytes 48025600 | tf_op jit(solution)/shard_map/fc1_back/pallas_call | solution.py:260
  372.0 7.8 %plane_terms.4 = (bf16[2,2,144,1152]{3,2,1,0:T(8,128)(2,1)}, bf16[2,2,144,1152]{3,2,1,0:T(8,128)(2,1)}, bf16[4,2,144,1152]{3,2,1,0:T(8,128)(2,1)}) custom-call(s32[3]{0:T(128)} %pad_add_fusion.where_ref, bf16[4,4,144,1152]{3,2,1,0:T(8,128)(2,1)} %get-tuple-element.128.keep_ref, bf16[4,4,144,1152]{3,2,1,0:T(8,128)(2,1)} %collective-permute-done.27.got_ref), custom_call_target="tpu_custom_call" | custom-call | flops 7000000000 | bytes 15925248 | tf_op jit(solution)/shard_map/plane_terms/pallas_call | solution.py:925
  379.8 12.0 %attend_back.1.proj_ref = bf16[896,3456]{1,0:T(8,128)(2,1)} custom-call(bf16[896,3456]{1,0:T(8,128)(2,1)} %get-tuple-element.92.refs_0_, bf16[896,1152]{1,0:T(8,128)(2,1)} %get-tuple-element.131.refs_1_), custom_call_target="tpu_custom_call" | custom-call | flops 12000000000 | bytes 14450688 | tf_op jit(solution)/shard_map/attend_back/pallas_call | solution.py:225
  400.1 24.4 %project_back.1 = (bf16[896,1152]{1,0:T(8,128)(2,1)}, f32[2,16,1152]{2,1,0:T(8,128)}) custom-call(bf16[896,3456]{1,0:T(8,128)(2,1)} %attend_back.1.proj_ref, bf16[1152,4608]{1,0:T(8,128)(2,1)} %get-tuple-element.97.w_ref.wo_ref, bf16[896,1152]{1,0:T(8,128)(2,1)} %get-tuple-element.96.x_ref, f32[896,1152]{1,0:T(8,128)} %get-tuple-element.136.gmid_ref, ...), custom_call_target="tpu_custom_call" | custom-call | flops 23000000512 | bytes 27013120 | tf_op jit(solution)/shard_map/project_back/pallas_call | solution.py:260
  431.9 19.3 %attn_terms.1 = (bf16[4,4,144,1152]{3,2,1,0:T(8,128)(2,1)}, bf16[4,4,144,1152]{3,2,1,0:T(8,128)(2,1)}) custom-call(s32[3]{0:T(128)} %pad_add_fusion.where_ref, bf16[896,1152]{1,0:T(8,128)(2,1)} %get-tuple-element.138.first_ref, bf16[896,3456]{1,0:T(8,128)(2,1)} %attend_back.1.proj_ref, bf16[896,1152]{1,0:T(8,128)(2,1)} %attend.1.mixed_ref, ...), custom_call_target="tpu_custom_call" | custom-call | flops 19000000512 | bytes 23003148 | tf_op jit(solution)/shard_map/attn_terms/pallas_call | solution.py:260
  452.8 15.9 %collective-permute-done.37 = bf16[2,144,1152]{2,1,0:T(8,128)(2,1)S(1)} collective-permute-done((bf16[2,144,1152]{2,1,0:T(8,128)(2,1)}, bf16[2,144,1152]{2,1,0:T(8,128)(2,1)S(1)}, u32[]{:S(2)}, u32[]{:S(2)}) %collective-permute-start.37) | collective-permute-done | bytes 663584 | tf_op jit(solution)/shard_map/ppermute | solution.py:953
  471.9 7.8 %plane_terms.5 = (bf16[2,2,144,1152]{3,2,1,0:T(8,128)(2,1)}, bf16[2,2,144,1152]{3,2,1,0:T(8,128)(2,1)}, bf16[4,2,144,1152]{3,2,1,0:T(8,128)(2,1)}) custom-call(s32[3]{0:T(128)} %pad_add_fusion.where_ref, bf16[4,4,144,1152]{3,2,1,0:T(8,128)(2,1)} %get-tuple-element.145.keep_ref, bf16[4,4,144,1152]{3,2,1,0:T(8,128)(2,1)} %collective-permute-done.32.got_ref), custom_call_target="tpu_custom_call" | custom-call | flops 7000000000 | bytes 15925248 | tf_op jit(solution)/shard_map/plane_terms/pallas_call | solution.py:925
  486.6 23.8 %collective-permute-done.33 = bf16[2,2,144,1152]{3,2,1,0:T(8,128)(2,1)S(1)} collective-permute-done((bf16[2,2,144,1152]{3,2,1,0:T(8,128)(2,1)}, bf16[2,2,144,1152]{3,2,1,0:T(8,128)(2,1)S(1)}, u32[]{:S(2)}, u32[]{:S(2)}) %collective-permute-start.33) | collective-permute-done | bytes 1327136 | tf_op jit(solution)/shard_map/ppermute | solution.py:949
  516.1 12.9 %collective-permute-done.35 = bf16[2,144,1152]{2,1,0:T(8,128)(2,1)} collective-permute-done((bf16[2,144,1152]{2,1,0:T(8,128)(2,1)}, bf16[2,144,1152]{2,1,0:T(8,128)(2,1)}, u32[]{:S(2)}, u32[]{:S(2)}) %collective-permute-start.35) | collective-permute-done | bytes 663584 | tf_op jit(solution)/shard_map/ppermute | solution.py:953
  547.3 10.2 %all-to-all-done.3 = bf16[8,2,56,1152]{3,2,1,0:T(8,128)(2,1)} async-done(((bf16[8,2,56,1152]{3,2,1,0:T(8,128)(2,1)}), bf16[8,2,56,1152]{3,2,1,0:T(8,128)(2,1)}, u32[]{:S(2)}, u32[]{:S(2)}) %all-to-all-start.3) | async-done | bytes 2064416 | tf_op jit(solution)/shard_map/all_to_all | solution.py:1156
  (269 shorter events, 175.2 us)
Async XLA Ops:
  7.2 59.3 %all-gather.4.cloned.1.call-start = ((), (), s32[]{:S(2)}) async-start(), calls=%async_computation.9 | async-start | bytes 2985984 | tf_op jit(solution)/shard_map/all_gather | solution.py:984
  11.6 115.3 %all-gather.6.cloned.1.call-start = ((), (), s32[]{:S(2)}) async-start(), calls=%async_computation.10 | async-start | bytes 2985984 | tf_op jit(solution)/shard_map/all_gather | solution.py:984
  18.8 100.4 %all-to-all-start = ((bf16[8,128,1152]{2,1,0:T(8,128)(2,1)}), bf16[8,128,1152]{2,1,0:T(8,128)(2,1)}, u32[]{:S(2)}, u32[]{:S(2)}) async-start(bf16[8,128,1152]{2,1,0:T(8,128)(2,1)} %pad_maximum_fusion), calls=%async_computation | async-start | bytes 4718592 | tf_op jit(solution)/shard_map/all_to_all | solution.py:1152
  25.1 166.3 %all-gather.8.cloned.1.call-start = ((), (), s32[]{:S(2)}) async-start(), calls=%async_computation.11 | async-start | bytes 2985984 | tf_op jit(solution)/shard_map/all_gather | solution.py:984
  67.9 31.3 %collective-permute-start = (bf16[4,144,1152]{2,1,0:T(8,128)(2,1)S(1)}, bf16[4,144,1152]{2,1,0:T(8,128)(2,1)S(1)}, u32[]{:S(2)}, u32[]{:S(2)}) collective-permute-start(bf16[4,144,1152]{2,1,0:T(8,128)(2,1)S(1)} %constant_dynamic-slice_fusion.7), channel_id=1, source_target_pairs={{0,8},{8,0},{16,24},{24,16},{1,9},{9,1},{17,25},{25,17},{2,10},{10... | collective-permute-start | bytes 3981320 | tf_op jit(solution)/shard_map/ppermute | solution.py:949
  69.5 31.0 %collective-permute-start.1 = (bf16[4,144,1152]{2,1,0:T(8,128)(2,1)S(1)}, bf16[4,144,1152]{2,1,0:T(8,128)(2,1)S(1)}, u32[]{:S(2)}, u32[]{:S(2)}) collective-permute-start(bf16[4,144,1152]{2,1,0:T(8,128)(2,1)S(1)} %constant_dynamic-slice_fusion.7), channel_id=1, source_target_pairs={{0,16},{16,0},{8,24},{24,8},{1,17},{17,1},{9,25},{25,9},{2,18},{18... | collective-permute-start | bytes 3981320 | tf_op jit(solution)/shard_map/ppermute | solution.py:953
  128.4 32.2 %collective-permute-start.8 = (bf16[4,144,1152]{2,1,0:T(8,128)(2,1)S(1)}, bf16[4,144,1152]{2,1,0:T(8,128)(2,1)}, u32[]{:S(2)}, u32[]{:S(2)}) collective-permute-start(bf16[4,144,1152]{2,1,0:T(8,128)(2,1)S(1)} %constant_dynamic-slice_fusion.6), channel_id=1, source_target_pairs={{0,8},{8,0},{16,24},{24,16},{1,9},{9,1},{17,25},{25,17},{2,10},{10... | collective-permute-start | bytes 3981320 | tf_op jit(solution)/shard_map/ppermute | solution.py:949
  129.9 30.9 %collective-permute-start.9 = (bf16[4,144,1152]{2,1,0:T(8,128)(2,1)S(1)}, bf16[4,144,1152]{2,1,0:T(8,128)(2,1)}, u32[]{:S(2)}, u32[]{:S(2)}) collective-permute-start(bf16[4,144,1152]{2,1,0:T(8,128)(2,1)S(1)} %constant_dynamic-slice_fusion.6), channel_id=1, source_target_pairs={{0,16},{16,0},{8,24},{24,8},{1,17},{17,1},{9,25},{25,9},{2,18},{18... | collective-permute-start | bytes 3981320 | tf_op jit(solution)/shard_map/ppermute | solution.py:953
  153.2 65.4 %all-to-all-start.1 = ((bf16[8,112,1152]{2,1,0:T(8,128)(2,1)}), bf16[8,112,1152]{2,1,0:T(8,128)(2,1)}, u32[]{:S(2)}, u32[]{:S(2)}) async-start(bf16[8,112,1152]{2,1,0:T(8,128)(2,1)} %bitcast.129), calls=%async_computation.1 | async-start | bytes 4128768 | tf_op jit(solution)/shard_map/all_to_all | solution.py:1152
  162.0 33.1 %collective-permute-start.12 = (bf16[4,144,1152]{2,1,0:T(8,128)(2,1)}, bf16[4,144,1152]{2,1,0:T(8,128)(2,1)}, u32[]{:S(2)}, u32[]{:S(2)}) collective-permute-start(bf16[4,144,1152]{2,1,0:T(8,128)(2,1)} %collective-permute-done.8), channel_id=1, source_target_pairs={{0,1},{1,0},{2,3},{3,2},{4,5},{5,4},{6,7},{7,6},{8,9},{9,8},{10,11... | collective-permute-start | bytes 3981320 | tf_op jit(solution)/shard_map/ppermute | solution.py:958
  163.5 31.6 %collective-permute-start.13 = (bf16[4,144,1152]{2,1,0:T(8,128)(2,1)}, bf16[4,144,1152]{2,1,0:T(8,128)(2,1)}, u32[]{:S(2)}, u32[]{:S(2)}) collective-permute-start(bf16[4,144,1152]{2,1,0:T(8,128)(2,1)} %collective-permute-done.9), channel_id=1, source_target_pairs={{0,1},{1,0},{2,3},{3,2},{4,5},{5,4},{6,7},{7,6},{8,9},{9,8},{10,11... | collective-permute-start | bytes 3981320 | tf_op jit(solution)/shard_map/ppermute | solution.py:958
  192.8 33.4 %collective-permute-start.16 = (bf16[4,144,1152]{2,1,0:T(8,128)(2,1)S(1)}, bf16[4,144,1152]{2,1,0:T(8,128)(2,1)}, u32[]{:S(2)}, u32[]{:S(2)}) collective-permute-start(bf16[4,144,1152]{2,1,0:T(8,128)(2,1)S(1)} %constant_dynamic-slice_fusion.4), channel_id=1, source_target_pairs={{0,8},{8,0},{16,24},{24,16},{1,9},{9,1},{17,25},{25,17},{2,10},{10... | collective-permute-start | bytes 3981320 | tf_op jit(solution)/shard_map/ppermute | solution.py:949
  194.4 31.9 %collective-permute-start.17 = (bf16[4,144,1152]{2,1,0:T(8,128)(2,1)S(1)}, bf16[4,144,1152]{2,1,0:T(8,128)(2,1)}, u32[]{:S(2)}, u32[]{:S(2)}) collective-permute-start(bf16[4,144,1152]{2,1,0:T(8,128)(2,1)S(1)} %constant_dynamic-slice_fusion.4), channel_id=1, source_target_pairs={{0,16},{16,0},{8,24},{24,8},{1,17},{17,1},{9,25},{25,9},{2,18},{18... | collective-permute-start | bytes 3981320 | tf_op jit(solution)/shard_map/ppermute | solution.py:953
  227.4 31.3 %collective-permute-start.18 = (bf16[4,144,1152]{2,1,0:T(8,128)(2,1)}, bf16[4,144,1152]{2,1,0:T(8,128)(2,1)S(1)}, u32[]{:S(2)}, u32[]{:S(2)}) collective-permute-start(bf16[4,144,1152]{2,1,0:T(8,128)(2,1)} %collective-permute-done.16.rest_1_), channel_id=1, source_target_pairs={{0,1},{1,0},{2,3},{3,2},{4,5},{5,4},{6,7},{7,6},{8,9},{9,8},{10,11... | collective-permute-start | bytes 3981320 | tf_op jit(solution)/shard_map/ppermute | solution.py:958
  248.7 51.9 %collective-permute-start.24 = (bf16[4,4,144,1152]{3,2,1,0:T(8,128)(2,1)}, bf16[4,4,144,1152]{3,2,1,0:T(8,128)(2,1)}, u32[]{:S(2)}, u32[]{:S(2)}) collective-permute-start(bf16[4,4,144,1152]{3,2,1,0:T(8,128)(2,1)} %get-tuple-element.107), channel_id=1, source_target_pairs={{0,1},{1,0},{2,3},{3,2},{4,5},{5,4},{6,7},{7,6},{8,9},{9,8},{10,11... | collective-permute-start | bytes 15925256 | tf_op jit(solution)/shard_map/ppermute | solution.py:958
  326.2 45.8 %collective-permute-start.27 = (bf16[4,4,144,1152]{3,2,1,0:T(8,128)(2,1)}, bf16[4,4,144,1152]{3,2,1,0:T(8,128)(2,1)}, u32[]{:S(2)}, u32[]{:S(2)}) collective-permute-start(bf16[4,4,144,1152]{3,2,1,0:T(8,128)(2,1)} %get-tuple-element.119), channel_id=1, source_target_pairs={{0,1},{1,0},{2,3},{3,2},{4,5},{5,4},{6,7},{7,6},{8,9},{9,8},{10,11... | collective-permute-start | bytes 15925256 | tf_op jit(solution)/shard_map/ppermute | solution.py:958
  327.0 64.8 %all-to-all-start.2 = ((bf16[8,2,56,1152]{3,2,1,0:T(8,128)(2,1)}), bf16[8,2,56,1152]{3,2,1,0:T(8,128)(2,1)}, u32[]{:S(2)}, u32[]{:S(2)}) async-start(bf16[8,2,56,1152]{3,2,1,0:T(8,128)(2,1)} %bitcast.135), calls=%async_computation.2 | async-start | bytes 4128768 | tf_op jit(solution)/shard_map/all_to_all | solution.py:1156
  334.1 97.8 %reduce-scatter.4.cloned.1.call-start = ((), (), s32[]{:S(2)}) async-start(), calls=%async_computation.12 | async-start | bytes 1658880 | tf_op jit(solution)/shard_map/reduce_scatter | solution.py:1083
  334.1 33.5 %collective-permute-start.25 = (bf16[2,2,144,1152]{3,2,1,0:T(8,128)(2,1)}, bf16[2,2,144,1152]{3,2,1,0:T(8,128)(2,1)S(1)}, u32[]{:S(2)}, u32[]{:S(2)}) collective-permute-start(bf16[2,2,144,1152]{3,2,1,0:T(8,128)(2,1)} %get-tuple-element.124), channel_id=1, source_target_pairs={{0,8},{8,0},{16,24},{24,16},{1,9},{9,1},{17,25},{25,17},{2,10},{10... | collective-permute-start | bytes 3981320 | tf_op jit(solution)/shard_map/ppermute | solution.py:949
  335.2 32.4 %collective-permute-start.26 = (bf16[2,2,144,1152]{3,2,1,0:T(8,128)(2,1)}, bf16[2,2,144,1152]{3,2,1,0:T(8,128)(2,1)}, u32[]{:S(2)}, u32[]{:S(2)}) collective-permute-start(bf16[2,2,144,1152]{3,2,1,0:T(8,128)(2,1)} %get-tuple-element.125), channel_id=1, source_target_pairs={{0,16},{16,0},{8,24},{24,8},{1,17},{17,1},{9,25},{25,9},{2,18},{18... | collective-permute-start | bytes 3981320 | tf_op jit(solution)/shard_map/ppermute | solution.py:953
  398.0 118.0 %reduce-scatter.6.cloned.1.call-start = ((), (), s32[]{:S(2)}) async-start(), calls=%async_computation.13 | async-start | bytes 1658880 | tf_op jit(solution)/shard_map/reduce_scatter | solution.py:1083
  479.7 30.7 %collective-permute-start.33 = (bf16[2,2,144,1152]{3,2,1,0:T(8,128)(2,1)}, bf16[2,2,144,1152]{3,2,1,0:T(8,128)(2,1)S(1)}, u32[]{:S(2)}, u32[]{:S(2)}) collective-permute-start(bf16[2,2,144,1152]{3,2,1,0:T(8,128)(2,1)} %get-tuple-element.148), channel_id=1, source_target_pairs={{0,8},{8,0},{16,24},{24,16},{1,9},{9,1},{17,25},{25,17},{2,10},{10... | collective-permute-start | bytes 3981320 | tf_op jit(solution)/shard_map/ppermute | solution.py:949
  481.8 75.7 %all-to-all-start.3 = ((bf16[8,2,56,1152]{3,2,1,0:T(8,128)(2,1)}), bf16[8,2,56,1152]{3,2,1,0:T(8,128)(2,1)}, u32[]{:S(2)}, u32[]{:S(2)}) async-start(bf16[8,2,56,1152]{3,2,1,0:T(8,128)(2,1)} %bitcast.133), calls=%async_computation.3 | async-start | bytes 4128768 | tf_op jit(solution)/shard_map/all_to_all | solution.py:1156
  486.5 86.8 %reduce-scatter.8.cloned.1.call-start = ((), (), s32[]{:S(2)}) async-start(), calls=%async_computation.14 | async-start | bytes 1658880 | tf_op jit(solution)/shard_map/reduce_scatter | solution.py:1083
  (70 other events, 967.4 us)
Sparse Core Ops, SparseCore 0:
  11.7 54.6 all-gather.3
  68.7 50.7 all-gather.5
  121.7 36.8 all-gather.7
  398.2 31.9 reduce-scatter.3
  472.1 42.8 reduce-scatter.5
  533.6 38.6 reduce-scatter.7

commit v5 on v4

--- a/solution.py
+++ b/solution.py
@@ -1151,10 +1151,13 @@
             chunks = jnp.concatenate([chunks, more], axis=1)
         return lax.all_to_all(chunks, "frame", 0, 0, tiled=True)
 
-    def to_frames(value, *wait_for):
+    def send_frames(value):
         chunks = value.reshape(frame_count, own_frames, positions, width)
-        moved = after(lax.all_to_all(chunks, "frame", 0, 0, tiled=True), *wait_for)
-        return moved.transpose(1, 0, 2, 3).reshape(1, own_frames, capacity, width)
+        return lax.all_to_all(chunks, "frame", 0, 0, tiled=True)
+
+    def to_frames(arrived, *wait_for):
+        moved = after(arrived, *wait_for).transpose(1, 0, 2, 3)
+        return moved.reshape(1, own_frames, capacity, width)
 
     layout = row_items(patch_counts, assignment, group_idx, capacity)
     my_rows = lax.dynamic_slice_in_dim(layout, frame_pos * positions, positions, 0)
@@ -1252,10 +1255,10 @@
     grad_proj = attend_back(
         projected, after(grad_mixed, *seen), positions, frames, attn_scale
     )
-    block_out = to_frames(block_rows, grad_proj)
+    out_arrived = send_frames(block_rows)
     seen = ()
     if square:
-        seen = (*sum_fc2.line(grad_proj), block_out)
+        seen = (*sum_fc2.line(grad_proj), out_arrived)
     token_rows, sums_attn = qkv_back_call(
         after(grad_proj, *seen), full_attn, x_rows, grad_middle, hot, mod, positions, frames
     )
@@ -1265,15 +1268,16 @@
             where, *attn_terms(where, first_in, after(grad_proj, *seen), mixed, grad_attn, chips)
         )
         sum_attn.pair()
+        block_out = to_frames(out_arrived, sum_attn.give)
         sum_fc1.line(sum_attn.give)
         sum_attn.near()
         sum_attn.far()
         seen = sum_attn.line(sum_fc1.own)
         last = (sum_attn.own,)
-        grad_tokens = to_frames(token_rows, *seen)
+        grad_tokens = to_frames(send_frames(token_rows), *seen)
         sum_fc2, sum_fc1, sum_attn = sum_fc2.finish(*seen), sum_fc1.finish(*seen), sum_attn.finish()
     else:
-        grad_tokens = to_frames(token_rows)
+        grad_tokens, block_out = to_frames(send_frames(token_rows)), to_frames(out_arrived)
         part_attn = [dot(first_in, part, ROW_DIMS) for part in jnp.split(grad_proj, 3, axis=1)]
         part_attn = jnp.stack([*part_attn, dot(mixed, grad_attn, ROW_DIMS)])
         part_attn = part_attn.reshape(4, frame_count, shard_rows, width)

time: 619 us -> 616 us (level)
  transfers between devices with their start and end apart: 63 -> 63, of which waited for: 21 -> 21; matrix products, arithmetic and copies ran while one was open for 10% -> 11% of each run, Pallas kernels for 35% -> 35%
where the time goes in v5:
time: 616 us; the launch traced here: 605 us
  Pallas kernels  255 us (41%)
  waiting for transfers between devices  181 us (29%)
  starting transfers between devices  78.2 us (13%)
  other arithmetic  33.2 us (5%)
  local copies, waits for them, and re-layouts  31.9 us (5%)
  between operations  15.1 us (2%)
  matrix products  10.8 us (2%)
    pallas_call x10, Pallas kernels, call(): pl.pallas_call(kernel, out_shape=[jax.ShapeDtypeStruct(shape, dtype) for...  211 us
    ppermute x16, waiting for transfers between devices, swap_x(): return lax.ppermute(value, 'item', X_SWAP)  63.5 us
    all_gather x3, waiting for transfers between devices, gather_frame(): return lax.all_gather(pick(parts, lax.axis_index('item')), 'frame', axis=0)  41.3 us
    ppermute x16, waiting for transfers between devices, swap_y(): return lax.ppermute(value, 'item', Y_SWAP)  40 us
    pallas_call x3, Pallas kernels, plane_terms(): pl.pallas_call(kernel, out_shape=[jax.ShapeDtypeStruct(shape, BF16) for s...  23.4 us
    ppermute x16, starting transfers between devices, swap_y(): return lax.ppermute(value, 'item', Y_SWAP)  19.4 us
    ppermute x16, starting transfers between devices, swap_x(): return lax.ppermute(value, 'item', X_SWAP)  17.8 us
    all_to_all x2, waiting for transfers between devices, to_positions(): return lax.all_to_all(chunks, 'frame', 0, 0, tiled=True)  15.7 us
  transfers between devices with their start and end apart: 63, of which 21 were waited for; matrix products, arithmetic and copies ran while one was open for 11% of the time, Pallas kernels for 35%

profile of v5, /device:TPU:0, one launch (start us, length us, event | category | flops | bytes accessed | tf_op | source)
XLA Modules:
  0.0 605.3 jit_solution(7740001417092384610)
XLA Ops:
  25.2 41.3 %all-gather.4.cloned.1.call-done = bf16[8,144,1152]{2,1,0:T(8,128)(2,1)} async-done(((bf16[1,144,1152]{2,1,0:T(8,128)(2,1)}), bf16[8,144,1152]{2,1,0:T(8,128)(2,1)}) %all-gather.4.cloned.1.call-update) | async-done | bytes 2654224 | tf_op jit(solution)/shard_map/all_gather | solution.py:984
  70.9 28.4 %collective-permute-done = bf16[4,144,1152]{2,1,0:T(8,128)(2,1)S(1)} collective-permute-done((bf16[4,144,1152]{2,1,0:T(8,128)(2,1)S(1)}, bf16[4,144,1152]{2,1,0:T(8,128)(2,1)S(1)}, u32[]{:S(2)}, u32[]{:S(2)}) %collective-permute-start) | collective-permute-done | bytes 1327136 | tf_op jit(solution)/shard_map/ppermute | solution.py:949
  103.5 15.7 %all-to-all-done = bf16[8,128,1152]{2,1,0:T(8,128)(2,1)} async-done(((bf16[8,128,1152]{2,1,0:T(8,128)(2,1)}), bf16[8,128,1152]{2,1,0:T(8,128)(2,1)}, u32[]{:S(2)}, u32[]{:S(2)}) %all-to-all-start) | async-done | bytes 2359328 | tf_op jit(solution)/shard_map/all_to_all | solution.py:1152
  131.4 20.3 %project.1 = (bf16[896,1152]{1,0:T(8,128)(2,1)}, bf16[896,1152]{1,0:T(8,128)(2,1)}, bf16[896,3456]{1,0:T(8,128)(2,1)}, bf16[1152,4608]{1,0:T(8,128)(2,1)}) custom-call(s32[3]{0:T(128)} %pad_add_fusion.where_ref, bf16[1024,1152]{1,0:T(8,128)(2,1)} %bitcast.6.x_ref, f32[4,16,6912]{2,1,0:T(8,128)} %fusion.24.mod_ref, bf16[1152,1152]{1,0:T(8,128)(2,1)} %bitcast.138, ...), custom_call_target="tpu_custom_call" | custom-call | flops 20000000000 | bytes 35684364 | tf_op jit(solution)/shard_map/project/pallas_call | solution.py:260
  153.2 7.4 %all-to-all-start.1 = ((bf16[8,112,1152]{2,1,0:T(8,128)(2,1)}), bf16[8,112,1152]{2,1,0:T(8,128)(2,1)}, u32[]{:S(2)}, u32[]{:S(2)}) async-start(bf16[8,112,1152]{2,1,0:T(8,128)(2,1)} %bitcast.129), calls=%async_computation.1 | async-start | bytes 4128768 | tf_op jit(solution)/shard_map/all_to_all | solution.py:1152
  166.3 8.9 %attend.1.mixed_ref = bf16[896,1152]{1,0:T(8,128)(2,1)} custom-call(bf16[896,3456]{1,0:T(8,128)(2,1)} %get-tuple-element.92.refs_0_), custom_call_target="tpu_custom_call" | custom-call | flops 8999999488 | bytes 8257536 | tf_op jit(solution)/shard_map/attend/pallas_call | solution.py:208
  182.5 8.9 %attn_out.1 = (bf16[896,1152]{1,0:T(8,128)(2,1)}, f32[896,1152]{1,0:T(8,128)}, bf16[896,1152]{1,0:T(8,128)(2,1)}) custom-call(bf16[896,1152]{1,0:T(8,128)(2,1)} %attend.1.mixed_ref, bf16[896,1152]{1,0:T(8,128)(2,1)} %get-tuple-element.96.x_ref, f32[4,16,6912]{2,1,0:T(8,128)} %fusion.24.mod_ref, bf16[1152,4608]{1,0:T(8,128)(2,1)} %get-tuple-element.97.w_ref.wo_ref), custom_call_target="tpu_custom_call" | custom-call | flops 8999999488 | bytes 24772608 | tf_op jit(solution)/shard_map/attn_out/pallas_call | solution.py:260
  195.2 23.4 %fc1.1 = (bf16[896,4608]{1,0:T(8,128)(2,1)}, bf16[896,4608]{1,0:T(8,128)(2,1)}, bf16[1152,4608]{1,0:T(8,128)(2,1)}) custom-call(s32[3]{0:T(128)} %pad_add_fusion.where_ref, bf16[896,1152]{1,0:T(8,128)(2,1)} %get-tuple-element.98.x_ref.left_ref, bf16[1,4608]{1,0:T(2,128)(2,1)} %reshape_squeeze.10.bias_ref, bf16[1152,1152]{1,0:T(8,128)(2,1)} %bitcast.137, ...), custom_call_target="tpu_custom_call" | custom-call | flops 24999999488 | bytes 39822348 | tf_op jit(solution)/shard_map/fc1/pallas_call | solution.py:260
  231.0 17.8 %fc2_terms.1 = (bf16[4,4,144,1152]{3,2,1,0:T(8,128)(2,1)}, bf16[4,4,144,1152]{3,2,1,0:T(8,128)(2,1)}) custom-call(s32[3]{0:T(128)} %pad_add_fusion.where_ref, bf16[896,4608]{1,0:T(8,128)(2,1)} %get-tuple-element.99.left_ref.post_ref, bf16[896,1152]{1,0:T(8,128)(2,1)} %get-tuple-element.108.right_ref.gmlp_ref), custom_call_target="tpu_custom_call" | custom-call | flops 17999998976 | bytes 20938764 | tf_op jit(solution)/shard_map/fc2_terms/pallas_call | solution.py:260
  249.4 7.4 %collective-permute-done.22.rest_7_ = bf16[2,144,1152]{2,1,0:T(8,128)(2,1)S(1)} collective-permute-done((bf16[2,144,1152]{2,1,0:T(8,128)(2,1)}, bf16[2,144,1152]{2,1,0:T(8,128)(2,1)S(1)}, u32[]{:S(2)}, u32[]{:S(2)}) %collective-permute-start.22) | collective-permute-done | bytes 663584 | tf_op jit(solution)/shard_map/ppermute | solution.py:958
  260.4 40.3 %fc2.1 = (bf16[896,1152]{1,0:T(8,128)(2,1)}, bf16[896,4608]{1,0:T(8,128)(2,1)}, f32[1,4608]{1,0:T(1,128)}, f32[16,1152]{1,0:T(8,128)}) custom-call(s32[3]{0:T(128)} %pad_add_fusion.where_ref, bf16[896,4608]{1,0:T(8,128)(2,1)} %get-tuple-element.99.left_ref.post_ref, bf16[896,4608]{1,0:T(8,128)(2,1)} %get-tuple-element.100.slope_ref, ...), custom_call_target="tpu_custom_call" | custom-call | flops 44000002048 | bytes 47601676 | tf_op jit(solution)/shard_map/fc2/pallas_call | solution.py:260
  300.7 7.8 %plane_terms.3 = (bf16[2,2,144,1152]{3,2,1,0:T(8,128)(2,1)}, bf16[2,2,144,1152]{3,2,1,0:T(8,128)(2,1)}, bf16[4,2,144,1152]{3,2,1,0:T(8,128)(2,1)}) custom-call(s32[3]{0:T(128)} %pad_add_fusion.where_ref, bf16[4,4,144,1152]{3,2,1,0:T(8,128)(2,1)} %get-tuple-element.116.keep_ref, bf16[4,4,144,1152]{3,2,1,0:T(8,128)(2,1)} %collective-permute-done.24.got_ref), custom_call_target="tpu_custom_call" | custom-call | flops 7000000000 | bytes 15925248 | tf_op jit(solution)/shard_map/plane_terms/pallas_call | solution.py:925
  308.5 17.9 %fc1_terms.1 = (bf16[4,4,144,1152]{3,2,1,0:T(8,128)(2,1)}, bf16[4,4,144,1152]{3,2,1,0:T(8,128)(2,1)}) custom-call(s32[3]{0:T(128)} %pad_add_fusion.where_ref, bf16[896,1152]{1,0:T(8,128)(2,1)} %get-tuple-element.98.x_ref.left_ref, bf16[896,4608]{1,0:T(8,128)(2,1)} %get-tuple-element.121.right_ref.pre_ref), custom_call_target="tpu_custom_call" | custom-call | flops 17999998976 | bytes 20938764 | tf_op jit(solution)/shard_map/fc1_terms/pallas_call | solution.py:260
  327.1 7.0 %all-to-all-start.2 = ((bf16[8,2,56,1152]{3,2,1,0:T(8,128)(2,1)}), bf16[8,2,56,1152]{3,2,1,0:T(8,128)(2,1)}, u32[]{:S(2)}, u32[]{:S(2)}) async-start(bf16[8,2,56,1152]{3,2,1,0:T(8,128)(2,1)} %bitcast.135), calls=%async_computation.2 | async-start | bytes 4128768 | tf_op jit(solution)/shard_map/all_to_all | solution.py:1156
  336.2 31.5 %fc1_back.1 = (f32[896,1152]{1,0:T(8,128)}, bf16[896,1152]{1,0:T(8,128)(2,1)}, bf16[896,1152]{1,0:T(8,128)(2,1)}, f32[3,16,1152]{2,1,0:T(8,128)}) custom-call(bf16[896,4608]{1,0:T(8,128)(2,1)} %get-tuple-element.121.right_ref.pre_ref, bf16[1152,4608]{1,0:T(8,128)(2,1)} %get-tuple-element.122.w_ref, f32[896,1152]{1,0:T(8,128)} %get-tuple-element.110.mid_ref, ...), custom_call_target="tpu_custom_call" | custom-call | flops 32000000000 | bytes 48025600 | tf_op jit(solution)/shard_map/fc1_back/pallas_call | solution.py:260
  372.1 7.8 %plane_terms.4 = (bf16[2,2,144,1152]{3,2,1,0:T(8,128)(2,1)}, bf16[2,2,144,1152]{3,2,1,0:T(8,128)(2,1)}, bf16[4,2,144,1152]{3,2,1,0:T(8,128)(2,1)}) custom-call(s32[3]{0:T(128)} %pad_add_fusion.where_ref, bf16[4,4,144,1152]{3,2,1,0:T(8,128)(2,1)} %get-tuple-element.129.keep_ref, bf16[4,4,144,1152]{3,2,1,0:T(8,128)(2,1)} %collective-permute-done.27.got_ref), custom_call_target="tpu_custom_call" | custom-call | flops 7000000000 | bytes 15925248 | tf_op jit(solution)/shard_map/plane_terms/pallas_call | solution.py:925
  379.9 12.0 %attend_back.1.proj_ref = bf16[896,3456]{1,0:T(8,128)(2,1)} custom-call(bf16[896,3456]{1,0:T(8,128)(2,1)} %get-tuple-element.92.refs_0_, bf16[896,1152]{1,0:T(8,128)(2,1)} %get-tuple-element.132.refs_1_), custom_call_target="tpu_custom_call" | custom-call | flops 12000000000 | bytes 14450688 | tf_op jit(solution)/shard_map/attend_back/pallas_call | solution.py:225
  397.2 24.5 %project_back.1 = (bf16[896,1152]{1,0:T(8,128)(2,1)}, f32[2,16,1152]{2,1,0:T(8,128)}) custom-call(bf16[896,3456]{1,0:T(8,128)(2,1)} %attend_back.1.proj_ref, bf16[1152,4608]{1,0:T(8,128)(2,1)} %get-tuple-element.97.w_ref.wo_ref, bf16[896,1152]{1,0:T(8,128)(2,1)} %get-tuple-element.96.x_ref, f32[896,1152]{1,0:T(8,128)} %get-tuple-element.136.gmid_ref, ...), custom_call_target="tpu_custom_call" | custom-call | flops 23000000512 | bytes 27013120 | tf_op jit(solution)/shard_map/project_back/pallas_call | solution.py:260
  428.9 19.3 %attn_terms.1 = (bf16[4,4,144,1152]{3,2,1,0:T(8,128)(2,1)}, bf16[4,4,144,1152]{3,2,1,0:T(8,128)(2,1)}) custom-call(s32[3]{0:T(128)} %pad_add_fusion.where_ref, bf16[896,1152]{1,0:T(8,128)(2,1)} %get-tuple-element.114.first_ref, bf16[896,3456]{1,0:T(8,128)(2,1)} %attend_back.1.proj_ref, bf16[896,1152]{1,0:T(8,128)(2,1)} %attend.1.mixed_ref, ...), custom_call_target="tpu_custom_call" | custom-call | flops 19000000512 | bytes 23003148 | tf_op jit(solution)/shard_map/attn_terms/pallas_call | solution.py:260
  449.8 15.9 %collective-permute-done.37 = bf16[2,144,1152]{2,1,0:T(8,128)(2,1)S(1)} collective-permute-done((bf16[2,144,1152]{2,1,0:T(8,128)(2,1)}, bf16[2,144,1152]{2,1,0:T(8,128)(2,1)S(1)}, u32[]{:S(2)}, u32[]{:S(2)}) %collective-permute-start.37) | collective-permute-done | bytes 663584 | tf_op jit(solution)/shard_map/ppermute | solution.py:953
  469.0 7.8 %plane_terms.5 = (bf16[2,2,144,1152]{3,2,1,0:T(8,128)(2,1)}, bf16[2,2,144,1152]{3,2,1,0:T(8,128)(2,1)}, bf16[4,2,144,1152]{3,2,1,0:T(8,128)(2,1)}) custom-call(s32[3]{0:T(128)} %pad_add_fusion.where_ref, bf16[4,4,144,1152]{3,2,1,0:T(8,128)(2,1)} %get-tuple-element.146.keep_ref, bf16[4,4,144,1152]{3,2,1,0:T(8,128)(2,1)} %collective-permute-done.32.got_ref), custom_call_target="tpu_custom_call" | custom-call | flops 7000000000 | bytes 15925248 | tf_op jit(solution)/shard_map/plane_terms/pallas_call | solution.py:925
  483.6 23.8 %collective-permute-done.33 = bf16[2,2,144,1152]{3,2,1,0:T(8,128)(2,1)S(1)} collective-permute-done((bf16[2,2,144,1152]{3,2,1,0:T(8,128)(2,1)}, bf16[2,2,144,1152]{3,2,1,0:T(8,128)(2,1)S(1)}, u32[]{:S(2)}, u32[]{:S(2)}) %collective-permute-start.33) | collective-permute-done | bytes 1327136 | tf_op jit(solution)/shard_map/ppermute | solution.py:949
  513.1 12.9 %collective-permute-done.35 = bf16[2,144,1152]{2,1,0:T(8,128)(2,1)} collective-permute-done((bf16[2,144,1152]{2,1,0:T(8,128)(2,1)}, bf16[2,144,1152]{2,1,0:T(8,128)(2,1)}, u32[]{:S(2)}, u32[]{:S(2)}) %collective-permute-start.35) | collective-permute-done | bytes 663584 | tf_op jit(solution)/shard_map/ppermute | solution.py:953
  547.4 7.1 %all-to-all-done.3 = bf16[8,2,56,1152]{3,2,1,0:T(8,128)(2,1)} async-done(((bf16[8,2,56,1152]{3,2,1,0:T(8,128)(2,1)}), bf16[8,2,56,1152]{3,2,1,0:T(8,128)(2,1)}, u32[]{:S(2)}, u32[]{:S(2)}) %all-to-all-start.3) | async-done | bytes 2064416 | tf_op jit(solution)/shard_map/all_to_all | solution.py:1156
  (267 shorter events, 175.2 us)
Async XLA Ops:
  7.2 59.3 %all-gather.4.cloned.1.call-start = ((), (), s32[]{:S(2)}) async-start(), calls=%async_computation.9 | async-start | bytes 2985984 | tf_op jit(solution)/shard_map/all_gather | solution.py:984
  11.6 115.3 %all-gather.6.cloned.1.call-start = ((), (), s32[]{:S(2)}) async-start(), calls=%async_computation.10 | async-start | bytes 2985984 | tf_op jit(solution)/shard_map/all_gather | solution.py:984
  18.8 100.4 %all-to-all-start = ((bf16[8,128,1152]{2,1,0:T(8,128)(2,1)}), bf16[8,128,1152]{2,1,0:T(8,128)(2,1)}, u32[]{:S(2)}, u32[]{:S(2)}) async-start(bf16[8,128,1152]{2,1,0:T(8,128)(2,1)} %pad_maximum_fusion), calls=%async_computation | async-start | bytes 4718592 | tf_op jit(solution)/shard_map/all_to_all | solution.py:1152
  25.1 166.3 %all-gather.8.cloned.1.call-start = ((), (), s32[]{:S(2)}) async-start(), calls=%async_computation.11 | async-start | bytes 2985984 | tf_op jit(solution)/shard_map/all_gather | solution.py:984
  67.9 31.3 %collective-permute-start = (bf16[4,144,1152]{2,1,0:T(8,128)(2,1)S(1)}, bf16[4,144,1152]{2,1,0:T(8,128)(2,1)S(1)}, u32[]{:S(2)}, u32[]{:S(2)}) collective-permute-start(bf16[4,144,1152]{2,1,0:T(8,128)(2,1)S(1)} %constant_dynamic-slice_fusion.7), channel_id=1, source_target_pairs={{0,8},{8,0},{16,24},{24,16},{1,9},{9,1},{17,25},{25,17},{2,10},{10... | collective-permute-start | bytes 3981320 | tf_op jit(solution)/shard_map/ppermute | solution.py:949
  69.5 31.0 %collective-permute-start.1 = (bf16[4,144,1152]{2,1,0:T(8,128)(2,1)S(1)}, bf16[4,144,1152]{2,1,0:T(8,128)(2,1)S(1)}, u32[]{:S(2)}, u32[]{:S(2)}) collective-permute-start(bf16[4,144,1152]{2,1,0:T(8,128)(2,1)S(1)} %constant_dynamic-slice_fusion.7), channel_id=1, source_target_pairs={{0,16},{16,0},{8,24},{24,8},{1,17},{17,1},{9,25},{25,9},{2,18},{18... | collective-permute-start | bytes 3981320 | tf_op jit(solution)/shard_map/ppermute | solution.py:953
  128.4 32.2 %collective-permute-start.8 = (bf16[4,144,1152]{2,1,0:T(8,128)(2,1)S(1)}, bf16[4,144,1152]{2,1,0:T(8,128)(2,1)}, u32[]{:S(2)}, u32[]{:S(2)}) collective-permute-start(bf16[4,144,1152]{2,1,0:T(8,128)(2,1)S(1)} %constant_dynamic-slice_fusion.6), channel_id=1, source_target_pairs={{0,8},{8,0},{16,24},{24,16},{1,9},{9,1},{17,25},{25,17},{2,10},{10... | collective-permute-start | bytes 3981320 | tf_op jit(solution)/shard_map/ppermute | solution.py:949
  129.9 30.9 %collective-permute-start.9 = (bf16[4,144,1152]{2,1,0:T(8,128)(2,1)S(1)}, bf16[4,144,1152]{2,1,0:T(8,128)(2,1)}, u32[]{:S(2)}, u32[]{:S(2)}) collective-permute-start(bf16[4,144,1152]{2,1,0:T(8,128)(2,1)S(1)} %constant_dynamic-slice_fusion.6), channel_id=1, source_target_pairs={{0,16},{16,0},{8,24},{24,8},{1,17},{17,1},{9,25},{25,9},{2,18},{18... | collective-permute-start | bytes 3981320 | tf_op jit(solution)/shard_map/ppermute | solution.py:953
  153.2 65.5 %all-to-all-start.1 = ((bf16[8,112,1152]{2,1,0:T(8,128)(2,1)}), bf16[8,112,1152]{2,1,0:T(8,128)(2,1)}, u32[]{:S(2)}, u32[]{:S(2)}) async-start(bf16[8,112,1152]{2,1,0:T(8,128)(2,1)} %bitcast.129), calls=%async_computation.1 | async-start | bytes 4128768 | tf_op jit(solution)/shard_map/all_to_all | solution.py:1152
  162.0 33.2 %collective-permute-start.12 = (bf16[4,144,1152]{2,1,0:T(8,128)(2,1)}, bf16[4,144,1152]{2,1,0:T(8,128)(2,1)}, u32[]{:S(2)}, u32[]{:S(2)}) collective-permute-start(bf16[4,144,1152]{2,1,0:T(8,128)(2,1)} %collective-permute-done.8), channel_id=1, source_target_pairs={{0,1},{1,0},{2,3},{3,2},{4,5},{5,4},{6,7},{7,6},{8,9},{9,8},{10,11... | collective-permute-start | bytes 3981320 | tf_op jit(solution)/shard_map/ppermute | solution.py:958
  163.5 31.7 %collective-permute-start.13 = (bf16[4,144,1152]{2,1,0:T(8,128)(2,1)}, bf16[4,144,1152]{2,1,0:T(8,128)(2,1)}, u32[]{:S(2)}, u32[]{:S(2)}) collective-permute-start(bf16[4,144,1152]{2,1,0:T(8,128)(2,1)} %collective-permute-done.9), channel_id=1, source_target_pairs={{0,1},{1,0},{2,3},{3,2},{4,5},{5,4},{6,7},{7,6},{8,9},{9,8},{10,11... | collective-permute-start | bytes 3981320 | tf_op jit(solution)/shard_map/ppermute | solution.py:958
  192.8 33.4 %collective-permute-start.16 = (bf16[4,144,1152]{2,1,0:T(8,128)(2,1)S(1)}, bf16[4,144,1152]{2,1,0:T(8,128)(2,1)}, u32[]{:S(2)}, u32[]{:S(2)}) collective-permute-start(bf16[4,144,1152]{2,1,0:T(8,128)(2,1)S(1)} %constant_dynamic-slice_fusion.4), channel_id=1, source_target_pairs={{0,8},{8,0},{16,24},{24,16},{1,9},{9,1},{17,25},{25,17},{2,10},{10... | collective-permute-start | bytes 3981320 | tf_op jit(solution)/shard_map/ppermute | solution.py:949
  194.4 31.9 %collective-permute-start.17 = (bf16[4,144,1152]{2,1,0:T(8,128)(2,1)S(1)}, bf16[4,144,1152]{2,1,0:T(8,128)(2,1)}, u32[]{:S(2)}, u32[]{:S(2)}) collective-permute-start(bf16[4,144,1152]{2,1,0:T(8,128)(2,1)S(1)} %constant_dynamic-slice_fusion.4), channel_id=1, source_target_pairs={{0,16},{16,0},{8,24},{24,8},{1,17},{17,1},{9,25},{25,9},{2,18},{18... | collective-permute-start | bytes 3981320 | tf_op jit(solution)/shard_map/ppermute | solution.py:953
  227.4 31.3 %collective-permute-start.18 = (bf16[4,144,1152]{2,1,0:T(8,128)(2,1)}, bf16[4,144,1152]{2,1,0:T(8,128)(2,1)S(1)}, u32[]{:S(2)}, u32[]{:S(2)}) collective-permute-start(bf16[4,144,1152]{2,1,0:T(8,128)(2,1)} %collective-permute-done.16.rest_1_), channel_id=1, source_target_pairs={{0,1},{1,0},{2,3},{3,2},{4,5},{5,4},{6,7},{7,6},{8,9},{9,8},{10,11... | collective-permute-start | bytes 3981320 | tf_op jit(solution)/shard_map/ppermute | solution.py:958
  248.8 51.9 %collective-permute-start.24 = (bf16[4,4,144,1152]{3,2,1,0:T(8,128)(2,1)}, bf16[4,4,144,1152]{3,2,1,0:T(8,128)(2,1)}, u32[]{:S(2)}, u32[]{:S(2)}) collective-permute-start(bf16[4,4,144,1152]{3,2,1,0:T(8,128)(2,1)} %get-tuple-element.107), channel_id=1, source_target_pairs={{0,1},{1,0},{2,3},{3,2},{4,5},{5,4},{6,7},{7,6},{8,9},{9,8},{10,11... | collective-permute-start | bytes 15925256 | tf_op jit(solution)/shard_map/ppermute | solution.py:958
  326.3 45.8 %collective-permute-start.27 = (bf16[4,4,144,1152]{3,2,1,0:T(8,128)(2,1)}, bf16[4,4,144,1152]{3,2,1,0:T(8,128)(2,1)}, u32[]{:S(2)}, u32[]{:S(2)}) collective-permute-start(bf16[4,4,144,1152]{3,2,1,0:T(8,128)(2,1)} %get-tuple-element.120), channel_id=1, source_target_pairs={{0,1},{1,0},{2,3},{3,2},{4,5},{5,4},{6,7},{7,6},{8,9},{9,8},{10,11... | collective-permute-start | bytes 15925256 | tf_op jit(solution)/shard_map/ppermute | solution.py:958
  327.1 68.0 %all-to-all-start.2 = ((bf16[8,2,56,1152]{3,2,1,0:T(8,128)(2,1)}), bf16[8,2,56,1152]{3,2,1,0:T(8,128)(2,1)}, u32[]{:S(2)}, u32[]{:S(2)}) async-start(bf16[8,2,56,1152]{3,2,1,0:T(8,128)(2,1)} %bitcast.135), calls=%async_computation.2 | async-start | bytes 4128768 | tf_op jit(solution)/shard_map/all_to_all | solution.py:1156
  334.1 94.8 %reduce-scatter.4.cloned.1.call-start = ((), (), s32[]{:S(2)}) async-start(), calls=%async_computation.12 | async-start | bytes 1658880 | tf_op jit(solution)/shard_map/reduce_scatter | solution.py:1083
  334.2 33.6 %collective-permute-start.25 = (bf16[2,2,144,1152]{3,2,1,0:T(8,128)(2,1)}, bf16[2,2,144,1152]{3,2,1,0:T(8,128)(2,1)S(1)}, u32[]{:S(2)}, u32[]{:S(2)}) collective-permute-start(bf16[2,2,144,1152]{3,2,1,0:T(8,128)(2,1)} %get-tuple-element.125), channel_id=1, source_target_pairs={{0,8},{8,0},{16,24},{24,16},{1,9},{9,1},{17,25},{25,17},{2,10},{10... | collective-permute-start | bytes 3981320 | tf_op jit(solution)/shard_map/ppermute | solution.py:949
  335.3 32.5 %collective-permute-start.26 = (bf16[2,2,144,1152]{3,2,1,0:T(8,128)(2,1)}, bf16[2,2,144,1152]{3,2,1,0:T(8,128)(2,1)}, u32[]{:S(2)}, u32[]{:S(2)}) collective-permute-start(bf16[2,2,144,1152]{3,2,1,0:T(8,128)(2,1)} %get-tuple-element.126), channel_id=1, source_target_pairs={{0,16},{16,0},{8,24},{24,8},{1,17},{17,1},{9,25},{25,9},{2,18},{18... | collective-permute-start | bytes 3981320 | tf_op jit(solution)/shard_map/ppermute | solution.py:953
  395.0 118.0 %reduce-scatter.6.cloned.1.call-start = ((), (), s32[]{:S(2)}) async-start(), calls=%async_computation.13 | async-start | bytes 1658880 | tf_op jit(solution)/shard_map/reduce_scatter | solution.py:1083
  476.8 30.7 %collective-permute-start.33 = (bf16[2,2,144,1152]{3,2,1,0:T(8,128)(2,1)}, bf16[2,2,144,1152]{3,2,1,0:T(8,128)(2,1)S(1)}, u32[]{:S(2)}, u32[]{:S(2)}) collective-permute-start(bf16[2,2,144,1152]{3,2,1,0:T(8,128)(2,1)} %get-tuple-element.148), channel_id=1, source_target_pairs={{0,8},{8,0},{16,24},{24,16},{1,9},{9,1},{17,25},{25,17},{2,10},{10... | collective-permute-start | bytes 3981320 | tf_op jit(solution)/shard_map/ppermute | solution.py:949
  478.8 75.6 %all-to-all-start.3 = ((bf16[8,2,56,1152]{3,2,1,0:T(8,128)(2,1)}), bf16[8,2,56,1152]{3,2,1,0:T(8,128)(2,1)}, u32[]{:S(2)}, u32[]{:S(2)}) async-start(bf16[8,2,56,1152]{3,2,1,0:T(8,128)(2,1)} %bitcast.132), calls=%async_computation.4 | async-start | bytes 4128768 | tf_op jit(solution)/shard_map/all_to_all | solution.py:1156
  483.5 86.8 %reduce-scatter.8.cloned.1.call-start = ((), (), s32[]{:S(2)}) async-start(), calls=%async_computation.14 | async-start | bytes 1658880 | tf_op jit(solution)/shard_map/reduce_scatter | solution.py:1083
  (69 other events, 956.3 us)
Sparse Core Ops, SparseCore 0:
  11.7 54.6 all-gather.3
  68.7 50.7 all-gather.5
  121.7 36.8 all-gather.7
  395.1 32.0 reduce-scatter.3
  469.1 42.7 reduce-scatter.5
  530.6 38.6 reduce-scatter.7
